TPU v7x, 32 devices: a whole 2x2x4 slice. The times are simulated.
32 devices in a mesh: seq: 16 (over z, x, core), fsdp: 2 (over y).
Axes of the slice: x: 2, y: 2, z: 4, core: 2. Of those that a mesh axis runs over, the one named last changes fastest.
Arguments:
- hidden_in: bfloat16 [2, 6144, 1792], P('fsdp', 'seq'), may hold values from -18 to 18
- cotangent: bfloat16 [2, 6144, 1792], P('fsdp', 'seq'), may hold values from -6 to 6
- mixer_weight: float32 [1792, 5888], P(('seq', 'fsdp')), may hold values from -0.88731955 to 0.88731955
- output_weight: float32 [1792, 1792], P(('seq', 'fsdp')), may hold values from -0.125 to 0.125
- updown_weight: float32 [1792, 8192], P(('seq', 'fsdp')), may hold values from -0.125 to 0.125
- down_weight: float32 [4096, 1792], P(('seq', 'fsdp')), may hold values from -0.09375 to 0.09375
- gain_weight: float32 [1792, 5], P(('seq', 'fsdp')), may hold values from -1.5 to 3.4
- mixer_first: float32 [1792, 5888], P(('seq', 'fsdp')), may hold values from -0.00010681152 to 0.00010681152
- output_first: float32 [1792, 1792], P(('seq', 'fsdp')), may hold values from -0.00010681152 to 0.00010681152
- updown_first: float32 [1792, 8192], P(('seq', 'fsdp')), may hold values from -0.00010681152 to 0.00010681152
- down_first: float32 [4096, 1792], P(('seq', 'fsdp')), may hold values from -0.00010681152 to 0.00010681152
- gain_first: float32 [1792, 5], P(('seq', 'fsdp')), may hold values from -0.0004272461 to 0.0004272461
- mixer_second: float32 [1792, 5888], P(('seq', 'fsdp')), may hold values from 1.4807937e-09 to 5.867296e-09
- output_second: float32 [1792, 1792], P(('seq', 'fsdp')), may hold values from 1.4807937e-09 to 5.867296e-09
- updown_second: float32 [1792, 8192], P(('seq', 'fsdp')), may hold values from 1.4807937e-09 to 5.867296e-09
- down_second: float32 [4096, 1792], P(('seq', 'fsdp')), may hold values from 1.4807937e-09 to 5.867296e-09
- gain_second: float32 [1792, 5], P(('seq', 'fsdp')), may hold values from 3.9115307e-09 to 1.5646123e-08
- lengths: int32 [2, 8], P('fsdp'), may hold values from 1 to 3072, 6144 in all within a row
- seq_order: int32 [2, 8], P('fsdp'), may hold values from 0 to 7, each once within a row
- pad_mask: int32 [2, 6144], P('fsdp'), may hold values 0 or 1
Outputs:
- layer_output: bfloat16 [2, 6144, 1792], P('fsdp', 'seq')
- input_grad: float32 [2, 6144, 1792], P('fsdp', 'seq')
- mixer_next: float32 [1792, 5888], P(('seq', 'fsdp'))
- output_next: float32 [1792, 1792], P(('seq', 'fsdp'))
- updown_next: float32 [1792, 8192], P(('seq', 'fsdp'))
- down_next: float32 [4096, 1792], P(('seq', 'fsdp'))
- gain_next: float32 [1792, 5], P(('seq', 'fsdp'))
- mixer_momentum: float32 [1792, 5888], P(('seq', 'fsdp'))
- output_momentum: float32 [1792, 1792], P(('seq', 'fsdp'))
- updown_momentum: float32 [1792, 8192], P(('seq', 'fsdp'))
- down_momentum: float32 [4096, 1792], P(('seq', 'fsdp'))
- gain_momentum: float32 [1792, 5], P(('seq', 'fsdp'))
- mixer_variance: float32 [1792, 5888], P(('seq', 'fsdp'))
- output_variance: float32 [1792, 1792], P(('seq', 'fsdp'))
- updown_variance: float32 [1792, 8192], P(('seq', 'fsdp'))
- down_variance: float32 [4096, 1792], P(('seq', 'fsdp'))
- gain_variance: float32 [1792, 5], P(('seq', 'fsdp'))
- grad_norm: float32 [], replicated
- layer_rms: float32 [3], replicated
Inputs may be any that keep to these rules, and one draw needn't show every extreme that they name: Each pack's 8 lengths sum to 6144, the largest is exactly 3072. Each row is a permutation; sequence seq_order[p] stands p-th in its pack.
All inputs are finite; a program needn't handle non-finite values. No bound on the sum of `pad_mask` on one device may be relied on, other than what follows from the above.
Results may differ from a plain program's by a relative error of at most 0.015.
The roundings to bfloat16 on the way count: a program that leaves them out, or rounds other values in their place, can miss the bound.
Values may be sent and summed in bfloat16 or wider, within the bound.
A program may use at most 384 MiB of HBM per device.

v0:
```python
import jax
import jax.numpy as jnp
from jax import lax
from jax.sharding import PartitionSpec as P

D = 1792
HEADS = 16
FEAT = 16
FF = 4096
BLOCK = 512
STEP = 10


highest = lax.Precision.HIGHEST
norm_eps = 1e-06
beta_one = 0.9
beta_two = 0.95
adam_eps = 1e-08
rate_matrix = 0.05
rate_gain = 1.5
decay_rate = 0.1
clip_level = 1.0


def passed_along(block, axis, distance):
    devices = range(lax.axis_size(axis))
    route = [(i - distance, i) for i in devices if i - distance in devices]
    return lax.ppermute(block, axis, route)


def taylor(vectors):
    feature_count = vectors.shape[-1]
    quad = (vectors[..., :, None] * vectors[..., None, :]).reshape(
        vectors.shape[:-1] + (feature_count * feature_count,)
    )
    ones_col = jnp.ones(vectors.shape[:-1] + (1,), vectors.dtype)
    return jnp.concatenate(
        [ones_col, vectors * feature_count ** (-0.25), quad * (2.0 * feature_count) ** (-0.5)],
        axis=-1,
    )


def block_step(carried, block_in):
    state, totals, last_seg = carried
    query, key_vecs, value, keep, segment = block_in
    feature_count = query.shape[-1]
    length = query.shape[0]
    dots = jnp.einsum("ihf,jhf->hij", query, key_vecs, precision=highest) * feature_count ** (-0.5)
    kernel = 1.0 + dots + 0.5 * dots * dots
    row_ids = lax.broadcasted_iota(jnp.int32, (length, length), 0)
    col_ids = lax.broadcasted_iota(jnp.int32, (length, length), 1)
    allowed = jnp.where(
        (segment[:, None] == segment[None, :]) & (col_ids <= row_ids), keep[None, :], 0.0
    )
    scores = kernel * allowed[None, :, :]
    numer = jnp.einsum("hij,jhv->ihv", scores, value, precision=highest)
    denom = jnp.sum(scores, axis=2).T
    carried_on = (segment == last_seg).astype(query.dtype)
    query_map = taylor(query)
    numer = numer + carried_on[:, None, None] * jnp.einsum(
        "iht,htv->ihv", query_map, state, precision=highest
    )
    denom = denom + carried_on[:, None] * jnp.einsum(
        "iht,ht->ih", query_map, totals, precision=highest
    )
    output = numer / (denom[:, :, None] + 1.0)
    tail_seg = segment[length - 1]
    holding = (tail_seg == last_seg).astype(query.dtype)
    fresh = jnp.where(segment == tail_seg, keep, 0.0)
    key_map = taylor(key_vecs) * fresh[:, None, None]
    state = holding * state + jnp.einsum("jht,jhv->htv", key_map, value, precision=highest)
    totals = holding * totals + jnp.sum(key_map, axis=0)
    return ((state, totals, tail_seg), output)


def attention(query, key_vecs, value, keep, segment, block_rows):
    total = query.shape[0]
    heads = query.shape[1]
    feature_count = query.shape[2]
    width = value.shape[2]
    blocks = total // block_rows
    features = 1 + feature_count + feature_count * feature_count

    def split_rows(array):
        return array.reshape((blocks, block_rows) + array.shape[1:])

    start = (
        jnp.zeros((heads, features, width), query.dtype),
        jnp.zeros((heads, features), query.dtype),
        jnp.array(-1, jnp.int32),
    )
    inputs = (
        split_rows(query),
        split_rows(key_vecs),
        split_rows(value),
        split_rows(keep),
        split_rows(segment),
    )
    ignored, outputs = lax.scan(jax.checkpoint(block_step), start, inputs)
    return outputs.reshape(total, heads, width)


def short_conv(extended, taps, seg_ext, count):
    result = jnp.zeros((count, extended.shape[1]), extended.dtype)
    for shift_by in range(3):
        piece = lax.slice_in_dim(extended, 2 - shift_by, 2 - shift_by + count, axis=0)
        earlier = lax.slice_in_dim(seg_ext, 2 - shift_by, 2 - shift_by + count, axis=0)
        same = (earlier == seg_ext[2:]).astype(extended.dtype)
        result = result + taps[shift_by][None, :] * piece * same[:, None]
    return result


def norm_scale(values, gain):
    return values * lax.rsqrt(jnp.mean(values * values, axis=-1, keepdims=True) + norm_eps) * gain


def segment_of(lengths_row, order_row, positions):
    count = lengths_row.shape[0]
    picks = order_row[:, None] == jnp.arange(count, dtype=jnp.int32)[None, :]
    ordered = jnp.sum(jnp.where(picks, lengths_row[None, :], 0), axis=1)
    ends = jnp.cumsum(ordered)
    return jnp.sum((positions[:, None] >= ends[None, :]).astype(jnp.int32), axis=1)


def adam_step(weight, first, second, grad, rate, decay):
    momentum = beta_one * first + (1.0 - beta_one) * grad
    variance = beta_two * second + (1.0 - beta_two) * grad * grad
    corrected = momentum / (1.0 - beta_one**STEP)
    scaled = variance / (1.0 - beta_two**STEP)
    return (
        weight - rate * (corrected / (jnp.sqrt(scaled) + adam_eps) + decay * weight),
        momentum,
        variance,
    )


def inner_dot(left_mat, right_mat):
    return lax.dot_general(
        left_mat, right_mat, (((0,), (0,)), ((), ())), preferred_element_type=jnp.float32
    )


def right_dot(left_mat, right_mat):
    return lax.dot_general(
        left_mat, right_mat, (((1,), (1,)), ((), ())), preferred_element_type=jnp.float32
    )


def per_device(
    hidden_in,
    cotangent,
    mixer_weight,
    output_weight,
    updown_weight,
    down_weight,
    gain_weight,
    mixer_first,
    output_first,
    updown_first,
    down_first,
    gain_first,
    mixer_second,
    output_second,
    updown_second,
    down_second,
    gain_second,
    lengths,
    seq_order,
    pad_mask,
):
    shards = lax.axis_size("seq")
    place = lax.axis_index("seq")
    groups = lax.axis_size("fsdp")
    local_rows = hidden_in.shape[1]
    total_rows = local_rows * shards
    qk_cols = HEADS * FEAT
    local_heads = max(1, HEADS // shards)
    q_width = FEAT * local_heads
    v_width = D // shards
    head_width = v_width // local_heads
    mixer_w, output_w, updown_w, down_w, gain_w = (
        lax.all_gather(mixer_weight.astype(jnp.bfloat16), ("seq", "fsdp"), axis=0, tiled=True),
        lax.all_gather(output_weight.astype(jnp.bfloat16), ("seq", "fsdp"), axis=0, tiled=True),
        lax.all_gather(updown_weight.astype(jnp.bfloat16), ("seq", "fsdp"), axis=0, tiled=True),
        lax.all_gather(down_weight.astype(jnp.bfloat16), ("seq", "fsdp"), axis=0, tiled=True),
        lax.all_gather(gain_weight.astype(jnp.bfloat16), ("seq", "fsdp"), axis=0, tiled=True),
    )
    gains = gain_w.astype(jnp.float32)
    taps = gains[:, 2:5].T
    keep_all = pad_mask[0].astype(jnp.float32)
    seg_all = segment_of(lengths[0], seq_order[0], jnp.arange(total_rows, dtype=jnp.int32))
    ext_pos = place * local_rows - 2 + jnp.arange(local_rows + 2, dtype=jnp.int32)
    seg_ext = jnp.where(ext_pos < 0, -1, segment_of(lengths[0], seq_order[0], ext_pos))
    tokens_in = hidden_in[0].astype(jnp.float32)
    normed_f, norm1_back = jax.vjp(norm_scale, tokens_in, gains[:, 0])
    normed = normed_f.astype(jnp.bfloat16)
    proj = jnp.dot(normed, mixer_w, preferred_element_type=jnp.float32)
    proj_low = proj.astype(jnp.bfloat16)
    query = proj_low[:, :qk_cols]
    key_vecs = proj_low[:, qk_cols : 2 * qk_cols]
    value = proj_low[:, 2 * qk_cols : 2 * qk_cols + D]
    conv_in = proj_low[:, 2 * qk_cols + D : 2 * qk_cols + 2 * D]
    gate = proj[:, 2 * qk_cols + 2 * D :]

    def to_dest(columns):
        if shards <= HEADS:
            return columns.reshape(local_rows, shards, q_width)
        repeat = shards // HEADS
        spread = jnp.broadcast_to(
            columns.reshape(local_rows, HEADS, 1, FEAT), (local_rows, HEADS, repeat, FEAT)
        )
        return spread.reshape(local_rows, shards, FEAT)

    def from_dest(columns):
        if shards <= HEADS:
            return columns.reshape(local_rows, qk_cols)
        repeat = shards // HEADS
        return jnp.sum(columns.reshape(local_rows, HEADS, repeat, FEAT), axis=2).reshape(
            local_rows, qk_cols
        )

    query_h, key_h, value_h = (
        lax.all_to_all(to_dest(query), "seq", split_axis=1, concat_axis=0, tiled=True),
        lax.all_to_all(to_dest(key_vecs), "seq", split_axis=1, concat_axis=0, tiled=True),
        lax.all_to_all(
            value.reshape(local_rows, shards, v_width),
            "seq",
            split_axis=1,
            concat_axis=0,
            tiled=True,
        ),
    )

    def attend(query_in, key_in, value_in):
        return attention(query_in, key_in, value_in, keep_all, seg_all, BLOCK)

    att, att_back = jax.vjp(
        attend, query_h.astype(jnp.float32), key_h.astype(jnp.float32), value_h.astype(jnp.float32)
    )
    att_seq = lax.all_to_all(
        att.astype(jnp.bfloat16), "seq", split_axis=0, concat_axis=1, tiled=True
    ).reshape(local_rows, D)
    before = passed_along(conv_in[local_rows - 2 :], "seq", 1)
    extended = jnp.concatenate([before, conv_in], axis=0).astype(jnp.float32)

    def gating(ext_in, taps_in, gate_in):
        return short_conv(ext_in, taps_in, seg_ext, local_rows) * jax.nn.sigmoid(gate_in)

    gated, gate_back = jax.vjp(gating, extended, taps, gate)
    mix = (att_seq.astype(jnp.float32) + gated).astype(jnp.bfloat16)
    branch = jnp.dot(mix, output_w, preferred_element_type=jnp.float32)
    middle = tokens_in + branch
    normed2_f, norm2_back = jax.vjp(norm_scale, middle, gains[:, 1])
    normed2 = normed2_f.astype(jnp.bfloat16)
    gateup = jnp.dot(normed2, updown_w, preferred_element_type=jnp.float32)

    def swiglu(both):
        return jax.nn.silu(both[:, :FF]) * both[:, FF:]

    inner_f, inner_back = jax.vjp(swiglu, gateup)
    inner = inner_f.astype(jnp.bfloat16)
    feed = jnp.dot(inner, down_w, preferred_element_type=jnp.float32)
    layer = (middle + feed).astype(jnp.bfloat16)
    stats = jnp.stack([jnp.sum(middle * middle), jnp.sum(branch * branch), jnp.sum(feed * feed)])
    upstream = cotangent[0]
    down_grad = inner_dot(inner, upstream)
    inner_grad = right_dot(upstream, down_w).astype(jnp.bfloat16)
    gateup_grad = inner_back(inner_grad.astype(jnp.float32))[0].astype(jnp.bfloat16)
    updown_grad = inner_dot(normed2, gateup_grad)
    normed2_grad = right_dot(gateup_grad, updown_w)
    middle_part, gain2_grad = norm2_back(normed2_grad)
    middle_grad = upstream.astype(jnp.float32) + middle_part
    branch_grad = middle_grad.astype(jnp.bfloat16)
    output_grad = inner_dot(mix, branch_grad)
    mix_grad = right_dot(branch_grad, output_w).astype(jnp.bfloat16)
    mix_heads = lax.all_to_all(
        mix_grad.reshape(local_rows, shards, v_width),
        "seq",
        split_axis=1,
        concat_axis=0,
        tiled=True,
    )
    query_g, key_g, value_g = att_back(mix_heads.astype(jnp.float32))
    query_s, key_s, value_s = (
        lax.all_to_all(
            query_g.astype(jnp.bfloat16), "seq", split_axis=0, concat_axis=1, tiled=True
        ).astype(query_g.dtype),
        lax.all_to_all(
            key_g.astype(jnp.bfloat16), "seq", split_axis=0, concat_axis=1, tiled=True
        ).astype(key_g.dtype),
        lax.all_to_all(
            value_g.astype(jnp.bfloat16), "seq", split_axis=0, concat_axis=1, tiled=True
        ).astype(value_g.dtype),
    )
    ext_grad, taps_grad, gate_grad = gate_back(mix_grad.astype(jnp.float32))
    after = passed_along(ext_grad[:2], "seq", -1)
    conv_grad = ext_grad[2:] + jnp.concatenate(
        [jnp.zeros((local_rows - 2, D), jnp.float32), after], axis=0
    )
    proj_grad = jnp.concatenate(
        [
            from_dest(query_s),
            from_dest(key_s),
            value_s.reshape(local_rows, D),
            conv_grad,
            gate_grad,
        ],
        axis=1,
    ).astype(jnp.bfloat16)
    mixer_grad = inner_dot(normed, proj_grad)
    normed_grad = right_dot(proj_grad, mixer_w)
    input_part, gain1_grad = norm1_back(normed_grad)
    input_grad = middle_grad + input_part
    gain_grad = jnp.stack(
        [gain1_grad, gain2_grad, taps_grad[0], taps_grad[1], taps_grad[2]], axis=1
    )
    mixer_sum, output_sum, updown_sum, down_sum, gain_sum = (
        lax.psum_scatter(mixer_grad, ("seq", "fsdp"), scatter_dimension=0, tiled=True),
        lax.psum_scatter(output_grad, ("seq", "fsdp"), scatter_dimension=0, tiled=True),
        lax.psum_scatter(updown_grad, ("seq", "fsdp"), scatter_dimension=0, tiled=True),
        lax.psum_scatter(down_grad, ("seq", "fsdp"), scatter_dimension=0, tiled=True),
        lax.psum_scatter(gain_grad, ("seq", "fsdp"), scatter_dimension=0, tiled=True),
    )
    grad_list = (mixer_sum, output_sum, updown_sum, down_sum, gain_sum)
    square = jnp.float32(0.0)
    for grad_one in grad_list:
        square = square + jnp.sum(grad_one * grad_one)
    total_sq, stat_sum = lax.psum((square, stats), ("seq", "fsdp"))
    grad_norm = jnp.sqrt(total_sq)
    factor = jnp.minimum(1.0, clip_level / grad_norm)
    masters = (mixer_weight, output_weight, updown_weight, down_weight, gain_weight)
    firsts = (mixer_first, output_first, updown_first, down_first, gain_first)
    seconds = (mixer_second, output_second, updown_second, down_second, gain_second)
    nexts, moms, varis = ([], [], [])
    for index in range(5):
        rate = rate_gain if index == 4 else rate_matrix
        decay = 0.0 if index == 4 else decay_rate
        new_w, new_m, new_v = adam_step(
            masters[index], firsts[index], seconds[index], grad_list[index] * factor, rate, decay
        )
        nexts.append(new_w)
        moms.append(new_m)
        varis.append(new_v)
    layer_rms = jnp.sqrt(stat_sum / (total_rows * groups * D))
    return (
        layer[None],
        input_grad[None],
        nexts[0],
        nexts[1],
        nexts[2],
        nexts[3],
        nexts[4],
        moms[0],
        moms[1],
        moms[2],
        moms[3],
        moms[4],
        varis[0],
        varis[1],
        varis[2],
        varis[3],
        varis[4],
        grad_norm,
        layer_rms,
    )


def solution(mesh):
    placed = (
        P("fsdp", "seq", None),
        P("fsdp", "seq", None),
        P(("seq", "fsdp"), None),
        P(("seq", "fsdp"), None),
        P(("seq", "fsdp"), None),
        P(("seq", "fsdp"), None),
        P(("seq", "fsdp"), None),
        P(("seq", "fsdp"), None),
        P(("seq", "fsdp"), None),
        P(("seq", "fsdp"), None),
        P(("seq", "fsdp"), None),
        P(("seq", "fsdp"), None),
        P(("seq", "fsdp"), None),
        P(("seq", "fsdp"), None),
        P(("seq", "fsdp"), None),
        P(("seq", "fsdp"), None),
        P(("seq", "fsdp"), None),
        P("fsdp", None),
        P("fsdp", None),
        P("fsdp", None),
    )
    return jax.shard_map(
        per_device,
        mesh=mesh,
        in_specs=placed,
        out_specs=(
            P("fsdp", "seq", None),
            P("fsdp", "seq", None),
            P(("seq", "fsdp"), None),
            P(("seq", "fsdp"), None),
            P(("seq", "fsdp"), None),
            P(("seq", "fsdp"), None),
            P(("seq", "fsdp"), None),
            P(("seq", "fsdp"), None),
            P(("seq", "fsdp"), None),
            P(("seq", "fsdp"), None),
            P(("seq", "fsdp"), None),
            P(("seq", "fsdp"), None),
            P(("seq", "fsdp"), None),
            P(("seq", "fsdp"), None),
            P(("seq", "fsdp"), None),
            P(("seq", "fsdp"), None),
            P(("seq", "fsdp"), None),
            P(),
            P(),
        ),
        check_vma=False,
    )
```

profile of v0, /device:TPU:0, one launch (start us, length us, event | category | flops | bytes accessed | tf_op | source)
XLA Modules:
  0.0 3699.0 jit_solution(492619855228049586)
XLA Ops:
  7.2 2.4 convert_element_type.318
  12.6 71.3 %all-gather = bf16[32,56,5]{1,2,0:T(8,128)(2,1)S(1)} all-gather(bf16[1,56,5]{1,2,0:T(8,128)(2,1)S(1)} %convert_bitcast_fusion.6), channel_id=1, replica_groups=mesh['seq'=16,'fsdp'=2] {'seq','fsdp'}, dimensions={0}, use_global_device_ids=true | all-gather | bytes 18480 | tf_op jit(solution)/shard_map/all_gather | solution.py:186
  84.5 65.2 %all-gather.6.cloned.1.call-done = bf16[1792,5888]{1,0:T(8,128)(2,1)} async-done(((bf16[56,5888]{1,0:T(8,128)(2,1)}), bf16[1792,5888]{1,0:T(8,128)(2,1)}) %all-gather.6.cloned.1.call-update) | async-done | bytes 21102608 | tf_op jit(solution)/shard_map/all_gather | solution.py:182
  149.7 15.2 fusion.143
  168.0 3.6 all-to-all-start
  172.4 8.2 all-to-all-done
  180.6 3.5 all-to-all-start.2
  184.1 3.0 fusion.141
  188.7 6.9 all-to-all-done.2
  195.5 4.4 all-to-all-start.1
  205.4 39.1 %all-to-all-done.1 = bf16[384,16,112]{0,2,1:T(8,128)(2,1)} async-done(((bf16[384,16,112]{0,2,1:T(8,128)(2,1)}), bf16[384,16,112]{0,2,1:T(8,128)(2,1)}, u32[]{:S(2)}, u32[]{:S(2)}) %all-to-all-start.1) | async-done | bytes 1376288 | tf_op jit(solution)/shard_map/all_to_all | solution.py:225
  246.1 2.3 copy.191
  248.5 158.1 %while.49 = (s32[]{:T(128)}, f32[1,273,112]{2,1,0:T(8,128)S(1)}, f32[1,273]{1,0:T(1,128)S(1)}, s32[]{:T(128)}, bf16[12,512,1,112]{1,3,2,0:T(8,128)(2,1)S(1)}, /*...) while((s32[]{:T(128)}, f32[1,273,112]{2,1,0:T(8,128)S(1)}, ...), condition=%wide.region_7.8_spmd.clone, body=%wide.region_4.7_spmd.clone.sunk | while | flops 785347456 | bytes 8084230 | solution.py:99
  410.4 3.9 reshape.1428
  414.3 8.2 all-to-all-start.3
  423.5 2.7 collective-permute-start
  428.2 32.6 all-to-all-done.3
  460.8 11.1 reshape.1429
  471.9 7.3 copy.199
  481.2 2.4 copy.200
  483.6 3.4 copy.201
  487.0 4.9 add_convert_fusion.2
  491.9 10.4 multiply_reduce_fusion.12
  502.3 20.5 fusion.131
  522.8 18.2 all-gather.12.cloned.1.call-done
  541.0 17.3 convert_multiply_fusion.1
  558.3 23.3 multiply_reduce_fusion.9
  581.7 15.0 multiply_reduce_fusion.4
  598.2 6.6 fusion.115
  604.9 10.4 multiply_reduce_fusion.8
  615.3 2.6 copy.202
  617.9 3.7 all-to-all-start.4
  621.7 15.9 fusion.108
  637.6 15.5 all-to-all-done.4
  660.7 273.6 %while.50 = (s32[]{:T(128)}, f32[1,273,112]{2,1,0:T(8,128)S(1)}, f32[1,273]{1,0:T(1,128)S(1)}, bf16[12,512,1,16]{1,3,2,0:T(8,128)(2,1)S(1)}, bf16[12,512,1,16]{1...) while((s32[]{:T(128)}, f32[1,273,112]{2,1,0:T(8,128)S(1)}, ...), condition=%wide.region_18.19_spmd.clone, body=%wide.region_11.18_spmd.clone.sunk | while | flops 2161928704 | bytes 26814948 | solution.py:99
  936.0 2.3 reshape.1430
  938.4 14.9 all-to-all-start.5
  954.8 2.3 reshape.1432
  957.2 5.1 all-to-all-done.5
  962.3 4.7 all-to-all-start.6
  971.2 3.9 reshape.1434
  976.0 5.4 all-to-all-start.7
  986.8 2.6 reshape.1431
  989.5 2.9 copy.210
  993.2 2.4 reshape.1433
  995.7 2.9 copy.214
  1000.3 13.6 all-to-all-done.7
  1013.8 9.5 reshape.1435
  1028.2 2.7 copy.222
  1030.8 2.5 constant_dynamic-update-slice_fusion.1
  1036.0 3.9 fusion.107
  1039.9 21.7 fusion.119
  1061.7 28.8 fusion.113
  1093.2 16.4 fusion.92
  1109.7 51.8 %all-reduce.10 = f32[1792,5]{0,1:T(8,128)S(1)} all-reduce(f32[1792,5]{0,1:T(8,128)S(1)} %stack.23), channel_id=6, replica_groups=mesh['seq'=16,'fsdp'=2] {'seq','fsdp'}, use_global_device_ids=true, to_apply=%region_33.34.clone | all-reduce | flops 8960 | bytes 71680
  1163.9 338.4 %reduce-scatter.13.cloned.1.call-done = f32[128,1792]{1,0:T(8,128)} async-done(((f32[4096,1792]{1,0:T(8,128)}), f32[128,1792]{1,0:T(8,128)}) %reduce-scatter.13.cloned.1.call-update) | async-done | bytes 917520 | tf_op jit(solution)/shard_map/reduce_scatter | solution.py:321
  1504.3 887.4 %reduce-scatter.9.cloned.1.call-done = f32[56,5888]{1,0:T(8,128)} async-done(((f32[1792,5888]{1,0:T(8,128)}), f32[56,5888]{1,0:T(8,128)}) %reduce-scatter.9.cloned.1.call-update) | async-done | bytes 1318928 | tf_op jit(solution)/shard_map/reduce_scatter | solution.py:318
  2395.3 1228.6 %reduce-scatter.15.cloned.1.call-done = f32[56,8192]{1,0:T(8,128)} async-done(((f32[1792,8192]{1,0:T(8,128)}), f32[56,8192]{1,0:T(8,128)}) %reduce-scatter.15.cloned.1.call-update) | async-done | bytes 1835024
  3623.9 2.6 multiply_reduce_fusion.13
  3628.5 5.0 fusion.97
  3633.4 41.4 %all-reduce.11 = (f32[]{:T(128)}, f32[3]{0:T(128)S(1)}) all-reduce(f32[]{:T(128)S(6)} %add.341, f32[3]{0:T(128)S(1)} %pad_maximum_fusion), channel_id=1, replica_groups=mesh['seq'=16,'fsdp'=2] {'seq','fsdp'}, use_global_device_ids=true, to_apply=%region_35.36 | all-reduce | flops 4 | bytes 32 | tf_op jit(solution)/shard_map/psum | solution.py:328
  3676.8 3.6 multiply_subtract_fusion.2
  3680.6 5.1 multiply_subtract_fusion
  3687.9 2.6 multiply_subtract_fusion.1
  (973 shorter events, 468.1 us)
Async XLA Ops:
  7.2 4.4 copy-start.5
  7.2 142.5 %all-gather.6.cloned.1.call-start = ((), (), s32[]{:S(2)}) async-start(), calls=%async_computation.12 | async-start | bytes 21762048 | tf_op jit(solution)/shard_map/all_gather | solution.py:182
  9.6 3.0 copy-start.37
  9.6 74.5 %copy-start = (bf16[1,384,1792]{2,1,0:T(8,128)(2,1)S(1)}, bf16[1,384,1792]{2,1,0:T(8,128)(2,1)}, u32[]{:S(2)}) copy-start(bf16[1,384,1792]{2,1,0:T(8,128)(2,1)} %param.24) | copy-start | bytes 4128772
  9.6 482.3 %all-gather.8.cloned.1.call-start = ((), (), s32[]{:S(2)}) async-start(), calls=%async_computation.13 | async-start | bytes 6623232 | tf_op jit(solution)/shard_map/all_gather | solution.py:183
  11.5 490.8 %all-gather.10.cloned.1.call-start = ((), (), s32[]{:S(2)}) async-start(), calls=%async_computation.14 | async-start | bytes 30277632 | tf_op jit(solution)/shard_map/all_gather | solution.py:184
  84.1 80.9 %copy-start.26 = (f32[1792]{0:T(1024)}, f32[1792]{0:T(1024)S(1)}, u32[]{:S(2)}) copy-start(f32[1792]{0:T(1024)S(1)} %get-tuple-element.816) | copy-start | bytes 21508
  84.4 80.5 %copy-start.34 = (f32[384]{0:T(512)}, f32[384]{0:T(512)S(1)}, u32[]{:S(2)}) copy-start(f32[384]{0:T(512)S(1)} %fusion.98) | copy-start | bytes 4612
  84.4 80.5 %copy-start.28 = (f32[384]{0:T(512)}, f32[384]{0:T(512)S(1)}, u32[]{:S(2)}) copy-start(f32[384]{0:T(512)S(1)} %fusion.127) | copy-start | bytes 4612
  168.0 12.6 all-to-all-start
  180.6 15.0 all-to-all-start.2
  187.1 13.1 copy-start.12
  188.7 12.4 copy-start.45
  188.7 12.4 copy-start.46
  188.7 13.6 copy-start.33
  195.5 49.0 %all-to-all-start.1 = ((bf16[384,16,112]{0,2,1:T(8,128)(2,1)}), bf16[384,16,112]{0,2,1:T(8,128)(2,1)}, u32[]{:S(2)}, u32[]{:S(2)}) async-start(bf16[384,16,112]{0,2,1:T(8,128)(2,1)} %bitcast.10), calls=%async_computation.1 | async-start | bytes 2752512 | tf_op jit(solution)/shard_map/all_to_all | solution.py:225
  199.9 341.1 %all-gather.12.cloned.1.call-start = ((), (), s32[]{:S(2)}) async-start(), calls=%async_computation.15 | async-start | bytes 15138816 | tf_op jit(solution)/shard_map/all_gather | solution.py:185
  406.7 3.7 copy-start.47
  414.3 46.5 %all-to-all-start.3 = ((bf16[16,2,21504]{2,1,0:T(2,128)(2,1)}), bf16[16,2,21504]{2,1,0:T(2,128)(2,1)}, u32[]{:S(2)}, u32[]{:S(2)}) async-start(bf16[16,2,21504]{2,1,0:T(2,128)(2,1)} %reshape.1428), calls=%async_computation.3 | async-start | bytes 2752512 | tf_op jit(solution)/shard_map/all_to_all | solution.py:240
  422.5 739.7 %reduce-scatter.11.cloned.1.call-start = ((), (), s32[]{:S(2)}) async-start(), calls=%async_computation.17 | async-start | bytes 13246464 | tf_op jit(solution)/shard_map/reduce_scatter | solution.py:319
  422.7 182.2 %copy-start.36 = (f32[384]{0:T(512)}, f32[384]{0:T(512)S(1)}, u32[]{:S(2)}) copy-start(f32[384]{0:T(512)S(1)} %get-tuple-element.935) | copy-start | bytes 4612
  423.5 3.1 collective-permute-start
  426.2 60.7 %copy-start.30 = (f32[1792]{0:T(1024)}, f32[1792]{0:T(1024)S(1)}, u32[]{:S(2)}) copy-start(f32[1792]{0:T(1024)S(1)} %get-tuple-element.817) | copy-start | bytes 21508
  426.2 60.7 %copy-start.31 = (f32[1792]{0:T(1024)}, f32[1792]{0:T(1024)S(1)}, u32[]{:S(2)}) copy-start(f32[1792]{0:T(1024)S(1)} %get-tuple-element.818) | copy-start | bytes 21508
  426.2 60.7 %copy-start.32 = (f32[1792]{0:T(1024)}, f32[1792]{0:T(1024)S(1)}, u32[]{:S(2)}) copy-start(f32[1792]{0:T(1024)S(1)} %get-tuple-element.819) | copy-start | bytes 21508
  581.7 16.5 copy-start.9
  615.3 6.4 copy-start.20
  617.9 35.3 all-to-all-start.4
  621.6 880.7 %reduce-scatter.13.cloned.1.call-start = ((), (), s32[]{:S(2)}) async-start(), calls=%async_computation.18 | async-start | bytes 30277632 | tf_op jit(solution)/shard_map/reduce_scatter | solution.py:321
  657.2 3.5 copy-start.48
  674.9 2.4 copy-start.49
  697.6 2.4 copy-start.49
  720.4 2.4 copy-start.49
  743.2 2.4 copy-start.49
  811.5 2.4 copy-start.49
  879.8 2.4 copy-start.49
  938.4 23.9 all-to-all-start.5
  962.3 13.7 all-to-all-start.6
  975.1 6.4 copy-start.15
  976.0 37.9 %all-to-all-start.7 = ((bf16[16,2,21504]{2,1,0:T(2,128)(2,1)}), bf16[16,2,21504]{2,1,0:T(2,128)(2,1)}, u32[]{:S(2)}, u32[]{:S(2)}) async-start(bf16[16,2,21504]{2,1,0:T(2,128)(2,1)} %reshape.1434), calls=%async_computation.7 | async-start | bytes 2752512 | tf_op jit(solution)/shard_map/all_to_all | solution.py:291
  981.4 1410.3 %reduce-scatter.9.cloned.1.call-start = ((), (), s32[]{:S(2)}) async-start(), calls=%async_computation.16 | async-start | bytes 43524096 | tf_op jit(solution)/shard_map/reduce_scatter | solution.py:318
  983.5 49.9 %collective-permute-start.1 = (f32[2,1792]{1,0:T(2,128)}, f32[2,1792]{1,0:T(2,128)}, u32[]{:S(2)}, u32[]{:S(2)}) collective-permute-start(f32[2,1792]{1,0:T(2,128)} %pad_add_fusion.1), channel_id=1, source_target_pairs={{2,0},{4,2},{6,4},{8,6},{10,8},{12,10},{14,12},{16,14},{18,16},{20... | collective-permute-start | bytes 43016 | tf_op jit(solution)/shard_map/ppermute | solution.py:28
  995.7 3.1 copy-start.23
  1028.2 5.2 copy-start.2
  1033.4 2.6 copy-start.8
  1036.0 3.9 copy-start.1
  1036.0 3.9 copy-start.27
  1036.0 3.9 copy-start.29
  1061.6 2562.3 %reduce-scatter.15.cloned.1.call-start = ((), (), s32[]{:S(2)}) async-start(), calls=%async_computation.19 | async-start | bytes 60555264
  1093.1 69.0 %copy-start.35 = (f32[384]{0:T(512)S(1)}, f32[384]{0:T(512)}, u32[]{:S(2)}) copy-start(f32[384]{0:T(512)} %copy-done.34) | copy-start | bytes 4612
  3628.4 47.6 %copy-start.38 = (f32[56,5]{0,1:T(8,128)S(1)}, f32[56,5]{0,1:T(8,128)}, u32[]{:S(2)}) copy-start(f32[56,5]{0,1:T(8,128)} %param.30) | copy-start | bytes 3364
  3628.4 47.6 %copy-start.43 = (f32[56,5]{0,1:T(8,128)S(1)}, f32[56,5]{0,1:T(8,128)}, u32[]{:S(2)}) copy-start(f32[56,5]{0,1:T(8,128)} %param.35) | copy-start | bytes 3364
  3628.4 47.6 %copy-start.44 = (f32[56,5]{0,1:T(8,128)S(1)}, f32[56,5]{0,1:T(8,128)}, u32[]{:S(2)}) copy-start(f32[56,5]{0,1:T(8,128)} %param.40) | copy-start | bytes 3364
  3628.5 48.3 %copy-start.13 = (f32[128,1792]{1,0:T(8,128)S(1)}, f32[128,1792]{1,0:T(8,128)}, u32[]{:S(2)}) copy-start(f32[128,1792]{1,0:T(8,128)} %param.29) | copy-start | bytes 2752516
  3628.5 48.3 %copy-start.14 = (f32[128,1792]{1,0:T(8,128)S(1)}, f32[128,1792]{1,0:T(8,128)}, u32[]{:S(2)}) copy-start(f32[128,1792]{1,0:T(8,128)} %reduce-scatter.13.cloned.1.call-done) | copy-start | bytes 2752516
  3676.8 3.6 copy-start.6
  3676.8 3.6 copy-start.7
  3676.8 3.8 copy-start.17
  3680.6 5.1 copy-start.18
  3680.6 5.1 copy-start.19
  3680.6 5.1 copy-start.24
  3680.6 5.2 copy-start.25
  3680.6 6.4 copy-start.21
  3680.6 6.4 copy-start.22
  (15 other events, 27.1 us)
Sparse Core Ops, SparseCore 0:
  11.5 138.1 all-gather.5
  153.1 91.1 all-gather.7
  247.8 173.9 all-gather.9
  425.1 115.8 all-gather.11
  605.0 273.8 reduce-scatter.10
  881.0 621.1 reduce-scatter.12
  1504.6 887.0 reduce-scatter.8
  2394.0 1229.8 reduce-scatter.14
where the time goes:
time: 3710 us; the launch traced here: 3700 us
  waiting for transfers between devices  2660 us (72%)
  matrix products  401 us (11%)
  local copies, waits for them, and re-layouts  232 us (6%)
  blocking collectives  164 us (4%)
  other arithmetic  133 us (4%)
  starting transfers between devices  52.9 us (1%)
    unnamed x9, waiting for transfers between devices  1230 us
    reduce_scatter x1, waiting for transfers between devices, per_device(): lax.psum_scatter(mixer_grad, ('seq', 'fsdp'), scatter_dimension=0, tiled=...  887 us
    reduce_scatter x1, waiting for transfers between devices, per_device(): lax.psum_scatter(down_grad, ('seq', 'fsdp'), scatter_dimension=0, tiled=T...  338 us
  transfers between devices with their start and end apart: 18, of which 14 were waited for; matrix products, arithmetic and copies ran while one was open for 18% of the time, Pallas kernels for 0%

commit v1 on v0

v1 whole, which is shorter than its diff:
```python
import functools

import jax
import jax.numpy as jnp
import numpy as np
from jax import lax
from jax.experimental import pallas as pl
from jax.experimental.layout import Layout, with_layout_constraint
from jax.experimental.pallas import tpu as pltpu
from jax.sharding import Mesh
from jax.sharding import PartitionSpec as P

D = 1792
HEADS = 16
FEAT = 16
FF = 4096
STEP = 10
HALF_HEADS = HEADS // 2
HEAD_WIDTH = D // HEADS
PHI = 160
LANES = 128
TILE = 256

norm_eps = 1e-06
beta_one = 0.9
beta_two = 0.95
adam_eps = 1e-08
rate_matrix = 0.05
rate_gain = 1.5
decay_rate = 0.1
clip_level = 1.0

bf16 = jnp.bfloat16
f32 = jnp.float32
VMEM_LIMIT = 48 * 1024 * 1024
GATHER_PACE = (-2.0, -1.2, 0.0, 1.1)
REDUCE_PACE = (0.0, 1.5, 2.6, 3.7, 4.8)


def feature_tables():
    first = np.zeros((FEAT, PHI), np.float32)
    second = np.zeros((FEAT, PHI), np.float32)
    bias = np.zeros((2, PHI), np.float32)
    scale = np.zeros((PHI,), np.float32)
    bias[:, 0] = 1.0
    scale[0] = 1.0
    at = 1
    for a in range(FEAT):
        first[a, at] = 1.0
        bias[1, at] = 1.0
        scale[at] = FEAT**-0.5
        at += 1
    for a in range(FEAT):
        for b in range(a, FEAT):
            first[a, at] = 1.0
            second[b, at] = 1.0
            scale[at] = (1.0 if a == b else 2.0) / (2.0 * FEAT)
            at += 1
    return first, second, bias, scale


def dot_nn(a, b):
    return lax.dot_general(a, b, (((1,), (0,)), ((), ())), preferred_element_type=f32)


def dot_tn(a, b):
    return lax.dot_general(a, b, (((0,), (0,)), ((), ())), preferred_element_type=f32)


def dot_nt(a, b):
    return lax.dot_general(a, b, (((1,), (1,)), ((), ())), preferred_element_type=f32)


def bits_of(size):
    return size.bit_length() - 1


def other(axis, bit):
    me = lax.axis_index(axis)
    return {axis: me + (1 - 2 * ((me // 2**bit) % 2)) * 2**bit}


def greet(partners):
    barrier = pltpu.get_barrier_semaphore()
    for partner in partners:
        pl.semaphore_signal(barrier, inc=1, device_id=partner, device_id_type=pl.DeviceIdType.MESH)
    pl.semaphore_wait(barrier, len(partners))


def gather_kernel(ring, groups, parts, orders, count, shared, *refs):
    in_refs, out_refs = refs[:count], refs[count : 2 * count]
    send_sem, recv_sem, own_sem = refs[2 * count :]
    ring_bits, group_bits = bits_of(ring), bits_of(groups)
    every = [("ring", b) for b in reversed(range(ring_bits))] + [("fsdp", b) for b in reversed(range(group_bits))]
    partners = {key: other(*key) for key in every}
    core_partner = other("core", 0)
    greet(list(partners.values()) + [core_partner])
    core = lax.axis_index("core")
    bit = {(axis, b): (lax.axis_index(axis) // 2**b) % 2 for axis, b in every}

    def view(ref, have, columns):
        spots = [slice(None) if key in have else pl.ds(bit[key], 1) for key in every]
        spots.insert(ring_bits, slice(None))
        return ref.at[tuple(spots) + (slice(None), columns)]

    def placed(part):
        index, at, width = parts[part]
        if index not in shared:
            return pl.ds(at, width)
        return pl.ds(pl.multiple_of(core * in_refs[index].shape[-1] + at, LANES), width)

    steps = len(every)
    events = []
    for part in range(len(parts)):
        for step in range(steps):
            late = GATHER_PACE[min(max(step + 4 - steps, 0), 3)]
            events.append((part // 2 + late, part, step))
    copies, owns = {}, []
    for index in range(count):
        everything = slice(None)
        if index in shared:
            columns = in_refs[index].shape[-1]
            everything = pl.ds(pl.multiple_of(core * columns, LANES), columns)
        owns.append(
            pltpu.make_async_copy(in_refs[index], view(out_refs[index], (), everything), own_sem.at[index])
        )
    owned = False
    for _, part, step in sorted(events):
        if step and not owned:
            owned = True
            for own in owns:
                own.start()
            for own in owns:
                own.wait()
        order = orders[part % len(orders)]
        if step:
            copies[part, step - 1].wait_recv()
        index, at, width = parts[part]
        ndim = in_refs[index].ndim
        here = view(out_refs[index], order[:step], placed(part))
        source = in_refs[index].at[(slice(None),) * (ndim - 1) + (pl.ds(at, width),)] if step == 0 else here
        copies[part, step] = pltpu.make_async_remote_copy(
            src_ref=source,
            dst_ref=here,
            send_sem=send_sem.at[part, step],
            recv_sem=recv_sem.at[part, step],
            device_id=partners[order[step]],
            device_id_type=pl.DeviceIdType.MESH,
        )
        copies[part, step].start()
    for part in range(len(parts)):
        copies[part, steps - 1].wait_recv()
        if parts[part][0] in shared:
            here = view(out_refs[parts[part][0]], every, placed(part))
            copies[part, steps] = pltpu.make_async_remote_copy(
                src_ref=here,
                dst_ref=here,
                send_sem=send_sem.at[part, steps],
                recv_sem=recv_sem.at[part, steps],
                device_id=core_partner,
                device_id_type=pl.DeviceIdType.MESH,
            )
            copies[part, steps].start()
    for part in range(len(parts)):
        if parts[part][0] in shared:
            copies[part, steps].wait_recv()
    for copy in copies.values():
        copy.wait_send()


def gather_rows(blocks, cuts, shared, ring, groups):
    ring_bits, group_bits = bits_of(ring), bits_of(groups)
    near, far = [("ring", 0)], [("ring", b) for b in reversed(range(1, ring_bits))]
    group = [("fsdp", b) for b in reversed(range(group_bits))]
    orders = (far + near + group, far + group + near)
    parts = []
    for index, widths in enumerate(cuts):
        at = 0
        for width in widths:
            parts.append((index, at, width))
            at += width
    steps = ring_bits + group_bits
    ins, shapes, size = [], [], 0
    for block in blocks:
        cores, rows, columns = block.shape
        ins.append(block.reshape((1,) * ring_bits + (cores,) + (1,) * group_bits + (rows, columns)))
        width = 2 * columns if len(ins) - 1 in shared else columns
        shape = (2,) * ring_bits + (cores,) + (2,) * group_bits + (rows, width)
        shapes.append(jax.ShapeDtypeStruct(shape, block.dtype))
        size += 2 * block.size * ring * groups
    outs = pl.pallas_call(
        functools.partial(gather_kernel, ring, groups, parts, orders, len(blocks), shared),
        in_specs=[pl.BlockSpec(memory_space=pl.ANY)] * len(blocks),
        out_specs=[pl.BlockSpec(memory_space=pl.ANY)] * len(blocks),
        out_shape=shapes,
        scratch_shapes=[
            pltpu.SemaphoreType.DMA((len(parts), steps + 1)),
            pltpu.SemaphoreType.DMA((len(parts), steps + 1)),
            pltpu.SemaphoreType.DMA((len(blocks),)),
        ],
        compiler_params=pltpu.CompilerParams(collective_id=0, has_side_effects=True),
        cost_estimate=pl.CostEstimate(flops=0, bytes_accessed=20 * size, transcendentals=0),
        name="gather_rows",
    )(*ins)
    return [o.reshape((2 * ring * groups if b.shape[0] == 2 else ring * groups) * b.shape[1], o.shape[-1])
            for o, b in zip(outs, blocks)]


def reduce_kernel(chains, partners, pairs, *refs):
    refs = list(refs)

    def take(number):
        taken = refs[:number]
        del refs[:number]
        return taken

    in_refs, out_refs = take(pairs), take(len(chains))
    own_refs = take(len(chains))
    recv_refs = [take(len(chain[4])) for chain in chains]
    send_refs = [take(len(chain[4]) - 1) for chain in chains]
    send_sem, recv_sem, own_sem = take(3)
    greet([other(*key) for key in partners])
    mine = {(axis, b): (lax.axis_index(axis) // 2**b) % 2 for axis, b in partners}
    copies = {}

    def start(c, step, source):
        copies[c, step] = pltpu.make_async_remote_copy(
            src_ref=source,
            dst_ref=recv_refs[c][step],
            send_sem=send_sem.at[c, step],
            recv_sem=recv_sem.at[c, step],
            device_id=other(*chains[c][4][step]),
            device_id_type=pl.DeviceIdType.MESH,
        )
        copies[c, step].start()

    def first_half(c, side):
        source, at, width, keys, order, rank = chains[c]
        spots = tuple(side if key == order[0] else slice(None) for key in keys)
        return in_refs[source].at[spots + (slice(None), pl.ds(at, width))]

    def add_up(c, step, target):
        keys, order = chains[c][3], chains[c][4]
        left = [key for key in keys if key not in order[: step + 1]]
        rows = target.shape[-2]
        tile = 16 if rows % 16 == 0 else rows
        for spot in np.ndindex(*(2,) * len(left)):
            spot = tuple(int(i) for i in spot)
            free = dict(zip(left, spot))

            def where(key):
                if key in free:
                    return free[key]
                return 1 - mine[key] if step < len(order) and key == order[step] else mine[key]

            def body(i, carry):
                at = pl.ds(pl.multiple_of(i * tile, tile), tile)
                total = None
                for t in range(step + 1):
                    ref = own_refs[c] if t == 0 else recv_refs[c][t - 1]
                    index = tuple(where(key) for key in keys if key not in order[: max(t, 1)])
                    term = ref[index + (at, slice(None))].astype(f32)
                    total = term if total is None else total + term
                target[spot + (at, slice(None))] = total.astype(target.dtype)
                return carry

            lax.fori_loop(0, rows // tile, body, 0)

    owns = []
    for c in range(len(chains)):
        own = pltpu.make_async_copy(first_half(c, mine[chains[c][4][0]]), own_refs[c], own_sem.at[c])
        own.start()
        owns.append(own)
    events = []
    for c, chain in enumerate(chains):
        for step in range(len(chain[4]) + 1):
            events.append((chain[5] + REDUCE_PACE[min(step, 4)], c, step))
    for _, c, step in sorted(events):
        order = chains[c][4]
        if step == 0:
            start(c, 0, first_half(c, 1 - mine[order[0]]))
            continue
        if step == 1:
            owns[c].wait()
        copies[c, step - 1].wait_recv()
        if step < len(order):
            add_up(c, step, send_refs[c][step - 1])
            start(c, step, send_refs[c][step - 1])
        else:
            add_up(c, step, out_refs[c])
    for copy in copies.values():
        copy.wait_send()


def reduce_rest(arrays, specs):
    outs, owns, recvs, sends = [], [], [], []
    steps = 0
    for source, at, width, keys, order, rank in specs:
        rows = arrays[source].shape[-2]
        steps = max(steps, len(order))
        outs.append(jax.ShapeDtypeStruct((rows, width), f32))
        shapes = [(2,) * (len(keys) - step - 1) + (rows, width) for step in range(len(order))]
        owns.append(pltpu.VMEM(shapes[0], bf16))
        recvs += [pltpu.VMEM(shape, bf16) for shape in shapes]
        sends += [pltpu.VMEM(shape, bf16) for shape in shapes[1:]]
    partners = sorted({key for spec in specs for key in spec[4]})
    sems = (len(specs), steps)
    return pl.pallas_call(
        functools.partial(reduce_kernel, specs, partners, len(arrays)),
        in_specs=[pl.BlockSpec(memory_space=pl.ANY)] * len(arrays),
        out_specs=[pl.BlockSpec(memory_space=pltpu.VMEM)] * len(specs),
        out_shape=outs,
        scratch_shapes=owns
        + recvs
        + sends
        + [
            pltpu.SemaphoreType.DMA(sems),
            pltpu.SemaphoreType.DMA(sems),
            pltpu.SemaphoreType.DMA((len(specs),)),
        ],
        compiler_params=pltpu.CompilerParams(
            collective_id=2, has_side_effects=True, vmem_limit_bytes=58 * 1024 * 1024
        ),
        name="reduce_rest",
    )(*arrays)


def sum_kernel(partners, in_ref, out_ref, held, got, send_sem, recv_sem):
    partners = [other(*key) for key in partners]
    greet(partners)
    held[0] = in_ref[...]
    for step, partner in enumerate(partners):
        copy = pltpu.make_async_remote_copy(
            src_ref=held.at[step],
            dst_ref=got.at[step],
            send_sem=send_sem.at[step],
            recv_sem=recv_sem.at[step],
            device_id=partner,
            device_id_type=pl.DeviceIdType.MESH,
        )
        copy.start()
        copy.wait()
        total = held[step] + got[step]
        if step + 1 < len(partners):
            held[step + 1] = total
        else:
            out_ref[...] = total


def sum_everywhere(block, ring, groups):
    partners = [("core", 0)] + [("ring", b) for b in range(bits_of(ring))] + [("fsdp", b) for b in range(bits_of(groups))]
    steps = len(partners)
    return pl.pallas_call(
        functools.partial(sum_kernel, partners),
        in_specs=[pl.BlockSpec(memory_space=pltpu.VMEM)],
        out_specs=pl.BlockSpec(memory_space=pltpu.VMEM),
        out_shape=jax.ShapeDtypeStruct(block.shape, f32),
        scratch_shapes=[
            pltpu.VMEM((steps,) + block.shape, f32),
            pltpu.VMEM((steps,) + block.shape, f32),
            pltpu.SemaphoreType.DMA((steps,)),
            pltpu.SemaphoreType.DMA((steps,)),
        ],
        compiler_params=pltpu.CompilerParams(collective_id=1, has_side_effects=True),
        name="sum_everywhere",
    )(block)


def exchange(source, target, send_sem, recv_sem):
    ring = source.shape[0]
    me = lax.axis_index("ring")
    copies = []
    for away in range(1, ring):
        peer = (me + away) % ring
        copy = pltpu.make_async_remote_copy(
            src_ref=source.at[peer],
            dst_ref=target.at[me],
            send_sem=send_sem.at[away],
            recv_sem=recv_sem.at[away],
            device_id={"ring": peer},
            device_id_type=pl.DeviceIdType.MESH,
        )
        copy.start()
        copies.append(copy)
    target[me] = source[me]
    return copies


def pass_along(source, target, away, send_sem, recv_sem):
    ring = lax.axis_size("ring")
    copy = pltpu.make_async_remote_copy(
        src_ref=source,
        dst_ref=target,
        send_sem=send_sem,
        recv_sem=recv_sem,
        device_id={"ring": (lax.axis_index("ring") + ring + away) % ring},
        device_id_type=pl.DeviceIdType.MESH,
    )
    copy.start()
    return copy


def arrive(copies):
    for copy in copies:
        copy.wait_recv()


def leave(copies):
    for copy in copies:
        copy.wait_send()


def greet_ring(ring):
    me = lax.axis_index("ring")
    greet([{"ring": (me + away) % ring} for away in range(1, ring)])


def put_state(buffer, head, state):
    ring, piece = buffer.shape[0], buffer.shape[1]
    share = ring // HALF_HEADS
    for part in range(share):
        buffer[head * share + part] = state[part * piece : (part + 1) * piece].astype(bf16)


def get_state(buffer, head):
    share = buffer.shape[0] // HALF_HEADS
    if share == 1:
        return buffer[head]
    return jnp.concatenate([buffer[head * share + part] for part in range(share)], axis=0)


def linked(states, link_ref, target, backward):
    ring = states.shape[0]
    for d in range(ring):
        total = jnp.zeros(states.shape[1:], f32)
        for e in range(d + 1, ring) if backward else range(d):
            weight = link_ref[e, d] if backward else link_ref[d, e]
            total = total + weight * states[e].astype(f32)
        target[d] = total.astype(bf16)


def attend_kernel(
    ring, link_ref, q_ref, kt_ref, v_ref, allow_ref, on_ref, fresh_ref, first_ref, second_ref, row_ref,
    first_t_ref, second_t_ref, col_ref, edge_ref, att_ref, den_ref, carry_ref, halo_ref,
    num_ref, one_ref, two_ref, three_ref, send_sem, recv_sem,
):
    count = q_ref.shape[0]
    lane = lax.broadcasted_iota(jnp.int32, (1, LANES), 1)
    rows, cols = row_ref[...], col_ref[...]
    greet_ring(ring)
    halo = [pass_along(edge_ref, halo_ref, 1, send_sem.at[0, 0], recv_sem.at[0, 0])]

    def local_state(head, none):
        kt = kt_ref[pl.ds(pl.multiple_of(head * FEAT, FEAT), FEAT), :]
        one = dot_nn(first_t_ref[...], kt) + cols[:, 0:1]
        two = dot_nn(second_t_ref[...], kt) + cols[:, 1:2]
        phi = (one * two * cols[:, 2:3] * fresh_ref[...]).astype(bf16)
        put_state(one_ref, head, dot_nn(phi, v_ref[head]))
        return none

    lax.fori_loop(0, HALF_HEADS, local_state, 0)

    def within(head, none):
        mine = (lane // FEAT == head).astype(bf16)
        for i in range(count // TILE):
            at = slice(i * TILE, (i + 1) * TILE)
            q = q_ref[at, :] * mine
            num = jnp.zeros((TILE, LANES), f32)
            for j in range(i + 1):
                to = slice(j * TILE, (j + 1) * TILE)
                dots = dot_nn(q, kt_ref[:, to]) * FEAT**-0.5 + 1.0
                score = (0.5 * dots * dots + 0.5) * allow_ref[at, to].astype(f32)
                num = num + dot_nn(score.astype(bf16), v_ref[head, to, :])
            num_ref[head, at, :] = num
        return none

    copies = exchange(one_ref, two_ref, send_sem.at[0], recv_sem.at[0])
    lax.fori_loop(0, HALF_HEADS // 2, within, 0)
    arrive(copies)
    linked(two_ref, link_ref, three_ref, False)
    back = exchange(three_ref, carry_ref, send_sem.at[1], recv_sem.at[1])
    lax.fori_loop(HALF_HEADS // 2, HALF_HEADS, within, 0)
    arrive(back)
    den_ref[...] = jnp.zeros_like(den_ref)

    def finish(head, none):
        mine = (lane // FEAT == head).astype(bf16)
        carry = get_state(carry_ref, head)
        for i in range(count // TILE):
            at = slice(i * TILE, (i + 1) * TILE)
            q = q_ref[at, :] * mine
            phi = (dot_nn(q, first_ref[...]) + rows[0:1]) * (dot_nn(q, second_ref[...]) + rows[1:2])
            num = num_ref[head, at, :] + dot_nn(phi.astype(bf16), carry) * on_ref[at, :]
            den = num[:, HEAD_WIDTH : HEAD_WIDTH + 1] + 1.0
            att_ref[head, at, :] = (num / den).astype(bf16)
            den_ref[at, :] += jnp.where(lane == head, den, 0.0)
        return none

    lax.fori_loop(0, HALF_HEADS, finish, 0)
    arrive(halo)
    leave(copies + back + halo)


def attend_back_kernel(
    ring, after, link_ref, q_ref, k_ref, qt_ref, kt_ref, v_ref, up_ref, att_ref, den_ref, carry_ref, allow_ref,
    on_ref, on_row_ref, fresh_ref, first_ref, second_ref, row_ref, first_t_ref, second_t_ref, col_ref, edge_ref, *refs,
):
    dq_ref, dk_ref, dv_ref, halo_ref = refs[after : after + 4]
    a_ref, dvs_ref, one_ref, two_ref, three_ref, later_ref, send_sem, recv_sem = refs[after + 4 :]
    count = q_ref.shape[0]
    tiles = count // TILE
    lane = lax.broadcasted_iota(jnp.int32, (1, LANES), 1)
    rows, cols = row_ref[...], col_ref[...]
    first, second = first_ref[...], second_ref[...]
    greet_ring(ring)
    halo = [pass_along(edge_ref, halo_ref, -1, send_sem.at[0, 0], recv_sem.at[0, 0])]
    dq_ref[...] = jnp.zeros_like(dq_ref)
    dk_ref[...] = jnp.zeros_like(dk_ref)

    def query_state(head, none):
        den = jnp.sum(jnp.where(lane == head, den_ref[...], 0.0), axis=1, keepdims=True)
        g = jnp.where(lane < HEAD_WIDTH, up_ref[head].astype(f32) / den, 0.0)
        back = jnp.sum(g * att_ref[head].astype(f32), axis=1, keepdims=True)
        a = jnp.where(lane == HEAD_WIDTH, -back, g).astype(bf16)
        a_ref[head] = a
        qt = qt_ref[pl.ds(pl.multiple_of(head * FEAT, FEAT), FEAT), :]
        one = dot_nn(first_t_ref[...], qt) + cols[:, 0:1]
        two = dot_nn(second_t_ref[...], qt) + cols[:, 1:2]
        phi = (one * two * on_row_ref[...]).astype(bf16)
        put_state(one_ref, head, dot_nn(phi, a))
        return none

    lax.fori_loop(0, HALF_HEADS, query_state, 0)

    def through(vec, d_phi):
        one = dot_nn(vec, first) + rows[0:1]
        two = dot_nn(vec, second) + rows[1:2]
        grad = dot_nt((d_phi * two).astype(bf16), first) + dot_nt((d_phi * one).astype(bf16), second)
        return grad, one * two

    def within(head, none):
        here = lane // FEAT == head
        mine = here.astype(bf16)
        carry = get_state(carry_ref, head)
        q = [q_ref[i * TILE : (i + 1) * TILE, :] * mine for i in range(tiles)]
        k = [k_ref[i * TILE : (i + 1) * TILE, :] * mine for i in range(tiles)]
        dk, dv = [None] * tiles, [None] * tiles
        for i in reversed(range(tiles)):
            at = slice(i * TILE, (i + 1) * TILE)
            a = a_ref[head, at, :]
            dq = through(q[i], dot_nt(a, carry) * on_ref[at, :])[0]
            for j in range(i + 1):
                to = slice(j * TILE, (j + 1) * TILE)
                allow = allow_ref[at, to].astype(f32)
                dots = dot_nn(q[i], kt_ref[:, to]) * FEAT**-0.5 + 1.0
                score = ((0.5 * dots * dots + 0.5) * allow).astype(bf16)
                d_dots = dot_nt(a, v_ref[head, to, :]) * dots * allow * FEAT**-0.5
                d_dots = d_dots.astype(bf16)
                dq = dq + dot_nn(d_dots, k[j])
                dk_more, dv_more = dot_tn(d_dots, q[i]), dot_tn(score, a)
                dk[j] = dk_more if dk[j] is None else dk[j] + dk_more
                dv[j] = dv_more if dv[j] is None else dv[j] + dv_more
            dq_ref[at, :] += jnp.where(here, dq, 0.0)
        for j in range(tiles):
            to = slice(j * TILE, (j + 1) * TILE)
            dk_ref[to, :] += jnp.where(here, dk[j], 0.0)
            dvs_ref[head, to, :] = dv[j]
        return none

    copies = exchange(one_ref, two_ref, send_sem.at[0], recv_sem.at[0])
    lax.fori_loop(0, HALF_HEADS // 2, within, 0)
    arrive(copies)
    linked(two_ref, link_ref, three_ref, True)
    back = exchange(three_ref, later_ref, send_sem.at[1], recv_sem.at[1])
    lax.fori_loop(HALF_HEADS // 2, HALF_HEADS, within, 0)
    arrive(back)

    def finish(head, none):
        here = lane // FEAT == head
        mine = here.astype(bf16)
        later = get_state(later_ref, head)
        for i in range(tiles):
            at = slice(i * TILE, (i + 1) * TILE)
            d_phi = dot_nt(v_ref[head, at, :], later) * rows[2:3] * fresh_ref[at, :]
            grad, phi = through(k_ref[at, :] * mine, d_phi)
            dk_ref[at, :] += jnp.where(here, grad, 0.0)
            phi = (phi * rows[2:3] * fresh_ref[at, :]).astype(bf16)
            dv_ref[head, at, :] = (dvs_ref[head, at, :] + dot_nn(phi, later)).astype(bf16)
        return none

    lax.fori_loop(0, HALF_HEADS, finish, 0)
    arrive(halo)
    leave(copies + back + halo)


def state_blocks(ring):
    return (ring, HALF_HEADS * PHI // ring, LANES)


def attend(link, q, kt, values, allow, on_col, fresh_row, edge, tables, ring):
    count = q.shape[0]
    vmem, smem = pl.BlockSpec(memory_space=pltpu.VMEM), pl.BlockSpec(memory_space=pltpu.SMEM)
    blocks = state_blocks(ring)
    return pl.pallas_call(
        functools.partial(attend_kernel, ring),
        in_specs=[smem] + [vmem] * 13,
        out_specs=[vmem] * 4,
        out_shape=[
            jax.ShapeDtypeStruct((HALF_HEADS, count, LANES), bf16),
            jax.ShapeDtypeStruct((count, LANES), f32),
            jax.ShapeDtypeStruct(blocks, bf16),
            jax.ShapeDtypeStruct(edge.shape, edge.dtype),
        ],
        scratch_shapes=[
            pltpu.VMEM((HALF_HEADS, count, LANES), f32),
            pltpu.VMEM(blocks, bf16),
            pltpu.VMEM(blocks, bf16),
            pltpu.VMEM(blocks, bf16),
            pltpu.SemaphoreType.DMA((2, ring)),
            pltpu.SemaphoreType.DMA((2, ring)),
        ],
        compiler_params=pltpu.CompilerParams(collective_id=3, has_side_effects=True, vmem_limit_bytes=VMEM_LIMIT),
        name="attend",
    )(link, q, kt, values, allow, on_col, fresh_row, tables["first"], tables["second"], tables["rows"],
      tables["first_t"], tables["second_t"], tables["cols"], edge)


def attend_back(link, q, k, qt, kt, values, upstream, att, den, carry, allow, on_col, on_row, fresh_col, edge, tables, ring, after):
    count = q.shape[0]
    vmem, smem = pl.BlockSpec(memory_space=pltpu.VMEM), pl.BlockSpec(memory_space=pltpu.SMEM)
    blocks = state_blocks(ring)
    return pl.pallas_call(
        functools.partial(attend_back_kernel, ring, len(after)),
        in_specs=[smem] + [vmem] * 20 + [pl.BlockSpec(memory_space=pl.ANY)] * len(after),
        out_specs=[vmem] * 4,
        out_shape=[
            jax.ShapeDtypeStruct((count, LANES), f32),
            jax.ShapeDtypeStruct((count, LANES), f32),
            jax.ShapeDtypeStruct((HALF_HEADS, count, LANES), bf16),
            jax.ShapeDtypeStruct(edge.shape, edge.dtype),
        ],
        scratch_shapes=[
            pltpu.VMEM((HALF_HEADS, count, LANES), bf16),
            pltpu.VMEM((HALF_HEADS, count, LANES), f32),
            pltpu.VMEM(blocks, bf16),
            pltpu.VMEM(blocks, bf16),
            pltpu.VMEM(blocks, bf16),
            pltpu.VMEM(blocks, bf16),
            pltpu.SemaphoreType.DMA((2, ring)),
            pltpu.SemaphoreType.DMA((2, ring)),
        ],
        compiler_params=pltpu.CompilerParams(collective_id=4, has_side_effects=True, vmem_limit_bytes=VMEM_LIMIT),
        name="attend_back",
    )(link, q, k, qt, kt, values, upstream, att, den, carry, allow, on_col, on_row, fresh_col,
      tables["first"], tables["second"], tables["rows"], tables["first_t"], tables["second_t"], tables["cols"], edge,
      *after)


def make_tables():
    first, second, bias, scale = feature_tables()
    rows = np.concatenate([bias, scale[None]], axis=0)
    return {
        "first": jnp.asarray(np.tile(first, (HALF_HEADS, 1)), bf16),
        "second": jnp.asarray(np.tile(second, (HALF_HEADS, 1)), bf16),
        "first_t": jnp.asarray(first.T, bf16),
        "second_t": jnp.asarray(second.T, bf16),
        "rows": jnp.asarray(rows, f32),
        "cols": jnp.asarray(rows.T, f32),
    }


def row_major(array):
    return with_layout_constraint(array, Layout(major_to_minor=tuple(range(array.ndim))))


def swap(block):
    return lax.ppermute(block, "core", [(0, 1), (1, 0)])


def in_order(core, mine, theirs):
    return jnp.stack([jnp.where(core == 0, mine, theirs), jnp.where(core == 0, theirs, mine)])


def choose(core, zero, one):
    return jnp.where(core == 0, zero, one)


def tie(block, after):
    if after is None:
        return block
    zero = lax.slice(after, (0,) * after.ndim, (1,) * after.ndim).reshape((1,) * block.ndim) * 0
    return block + zero.astype(block.dtype)


class Halving:
    def __init__(self, parts, orders):
        ring, groups = lax.axis_size("ring"), lax.axis_size("fsdp")
        ring_bits, group_bits = bits_of(ring), bits_of(groups)
        self.place = {("ring", b): ring_bits - 1 - b for b in range(ring_bits)}
        self.place.update({("fsdp", b): ring_bits + group_bits - 1 - b for b in range(group_bits)})
        self.index = {axis: lax.axis_index(axis) for axis in ("ring", "fsdp")}
        shape = (2,) * (ring_bits + group_bits)
        self.parts = [[part.reshape(shape + part.shape[2:])] for part in parts]
        self.orders = orders
        self.at = 0

    def step(self, after=None):
        sent, self.got = [], []
        for which, order in enumerate(self.orders):
            axis, bit = order[self.at]
            dim = self.place[axis, bit]
            mine = (self.index[axis] >> bit) & 1

            def half(term, side):
                return lax.dynamic_slice_in_dim(term, side, 1, axis=dim)

            terms = self.parts[which]
            send = functools.reduce(jnp.add, [half(t, 1 - mine).astype(f32) for t in terms]).astype(bf16)
            send = tie(send, after)
            size = lax.axis_size(axis)
            got = lax.ppermute(send, axis, [(i, i ^ (1 << bit)) for i in range(size)])
            self.parts[which] = [half(t, mine) for t in terms] + [got]
            sent.append(send)
            self.got.append(got)
        self.at += 1
        return sent

    def rest(self):
        found = []
        for terms, order in zip(self.parts, self.orders):
            gone = [self.place[key] for key in order[: self.at]]
            total = functools.reduce(jnp.add, [t.astype(f32) for t in terms]).astype(bf16)
            left = total.reshape([n for dim, n in enumerate(total.shape) if dim not in gone])
            keys = sorted(order[self.at :], key=self.place.get)
            found.append((left, keys, order[self.at :]))
        return found


    def result(self):
        while self.at < len(self.orders[0]):
            self.step()
        totals = []
        for terms in self.parts:
            total = functools.reduce(jnp.add, [t.astype(f32) for t in terms])
            totals.append(total.reshape(total.shape[-2:]))
        return jnp.concatenate(totals, axis=-1)


def both_orders(ring, groups):
    ring_bits = [("ring", b) for b in range(ring.bit_length() - 1)]
    group_bits = [("fsdp", b) for b in reversed(range(groups.bit_length() - 1))]
    near, far = ring_bits[:1], ring_bits[1:]
    return near + group_bits + far, group_bits + near + far


def norm_scale(values, gain):
    return values * lax.rsqrt(jnp.mean(values * values, axis=-1, keepdims=True) + norm_eps) * gain


def segment_ends(lengths_row, order_row):
    count = lengths_row.shape[0]
    picks = order_row[:, None] == jnp.arange(count, dtype=jnp.int32)[None, :]
    ordered = jnp.sum(jnp.where(picks, lengths_row[None, :], 0), axis=1)
    upto = jnp.arange(count)[:, None] >= jnp.arange(count)[None, :]
    return jnp.sum(jnp.where(upto, ordered[None, :], 0), axis=1)


def segment_of(ends, positions):
    found = jnp.sum((positions[:, None] >= ends[None, :]).astype(jnp.int32), axis=1)
    return jnp.where(positions < 0, -1, found)


def adam_step(weight, first, second, grad, rate, decay):
    momentum = beta_one * first + (1.0 - beta_one) * grad
    variance = beta_two * second + (1.0 - beta_two) * grad * grad
    corrected = momentum / (1.0 - beta_one**STEP)
    scaled = variance / (1.0 - beta_two**STEP)
    return (
        weight - rate * (corrected / (jnp.sqrt(scaled) + adam_eps) + decay * weight),
        momentum,
        variance,
    )


def short_conv(extended, taps, same):
    count = same[0].shape[0]
    result = 0.0
    for shift_by in range(3):
        piece = lax.slice_in_dim(extended, 2 - shift_by, 2 - shift_by + count, axis=0)
        result = result + taps[shift_by][None, :] * piece * same[shift_by]
    return result


def per_device(
    hidden_in, cotangent, mixer_weight, output_weight, updown_weight, down_weight, gain_weight,
    mixer_first, output_first, updown_first, down_first, gain_first,
    mixer_second, output_second, updown_second, down_second, gain_second,
    lengths, seq_order, pad_mask,
):
    ring, groups = lax.axis_size("ring"), lax.axis_size("fsdp")
    ring_id, core = lax.axis_index("ring"), lax.axis_index("core")
    local_rows = hidden_in.shape[1]
    count = 2 * local_rows
    qk_cols = HEADS * FEAT
    half_d, half_qk = D // 2, qk_cols // 2
    d_rows, f_rows = mixer_weight.shape[0], down_weight.shape[0]
    pair_ff = 2 * FF // (2 * ring) // 2
    tables = make_tables()

    def gather(block):
        return lax.all_gather(block, ("ring", "fsdp"), axis=0, tiled=False)

    def to_owner(array):
        blocks = array.reshape(array.shape[:-1] + (ring, 2, groups, d_rows))
        return row_major(blocks.swapaxes(-3, -2).reshape(array.shape))

    def from_owner(array):
        blocks = array.reshape(array.shape[:-1] + (ring, groups, 2, d_rows))
        return row_major(blocks.swapaxes(-3, -2).reshape(array.shape))

    def exchanged(halves):
        return in_order(core, choose(core, *halves), swap(choose(core, *halves[::-1])))

    def column_half(weight, c):
        pieces, at = [], 0
        for width in (qk_cols, qk_cols, D, D, D):
            pieces.append(weight[:, at + c * width // 2 : at + (c + 1) * width // 2])
            at += width
        return jnp.concatenate(pieces, axis=1)

    gain_low = jnp.pad(gain_weight.astype(bf16), ((0, 0), (0, LANES - gain_weight.shape[1])))
    mixer_low = mixer_weight.astype(bf16)
    halves = [jnp.concatenate([column_half(mixer_low, c), gain_low], axis=1) for c in range(2)]
    packed = exchanged(halves).reshape(1, 2 * d_rows, -1)
    updown_low = updown_weight.astype(bf16).reshape(d_rows, 2, ring, 2, pair_ff)
    packed_gate, packed_up = [
        exchanged([updown_low[:, which, :, c].reshape(d_rows, FF // 2) for c in range(2)]) for which in range(2)
    ]
    output_low = to_owner(output_weight.astype(bf16))
    packed_output = exchanged([output_low[:, :half_d], output_low[:, half_d:]])
    gate_w = gather(packed_gate).reshape(D, FF // 2)
    mixer_all, output_w = gather_rows(
        [tie(packed, packed_gate), packed_output],
        [[256, 256] + [512] * 4 + [256, 256], [512, 384]],
        [1],
        ring,
        groups,
    )
    mixer_w, gains = mixer_all[:, : 2 * half_qk + 3 * half_d], mixer_all[:, 2 * half_qk + 3 * half_d :].astype(f32)
    up_w = gather(tie(packed_up, mixer_all)).reshape(D, FF // 2)

    hidden_own, upstream_own = to_owner(hidden_in[0]), to_owner(cotangent[0])
    tokens = in_order(core, hidden_own, swap(hidden_own)).reshape(count, D).astype(f32)
    upstream = in_order(core, upstream_own, swap(upstream_own)).reshape(count, D)

    ends = segment_ends(lengths[0], seq_order[0])
    start = ring_id * count
    segment = segment_of(ends, start + jnp.arange(-2, count, dtype=jnp.int32))
    seg = segment[2:]
    keep = lax.dynamic_slice_in_dim(pad_mask[0], start, count).astype(f32)
    tails = segment_of(ends, jnp.arange(1, ring + 1, dtype=jnp.int32) * count - 1)
    on = (seg == segment[1]).astype(f32)
    fresh = jnp.where(seg == seg[count - 1], keep, 0.0)
    row_ids = lax.broadcasted_iota(jnp.int32, (count, count), 0)
    col_ids = lax.broadcasted_iota(jnp.int32, (count, count), 1)
    allow = jnp.where((seg[:, None] == seg[None, :]) & (col_ids <= row_ids), keep[None, :], 0.0).astype(bf16)
    same = [(segment[2 - s : 2 - s + count] == seg).astype(f32)[:, None] for s in range(3)]
    before = jnp.concatenate([jnp.full((1,), -1, jnp.int32), tails[:-1]])
    chips = jnp.arange(ring)
    link = ((before[:, None] == tails[None, :]) & (chips[None, :] < chips[:, None])).astype(f32)

    def per_head(block):
        wide = block.reshape(count, HALF_HEADS, HEAD_WIDTH).transpose(1, 0, 2)
        return jnp.pad(wide, ((0, 0), (0, 0), (0, LANES - HEAD_WIDTH)))

    def from_heads(block):
        return block[:, :, :HEAD_WIDTH].transpose(1, 0, 2).reshape(count, half_d)

    normed_f, norm1_back = jax.vjp(norm_scale, tokens, gains[:, 0])
    normed = normed_f.astype(bf16)
    proj = jnp.dot(normed, mixer_w, preferred_element_type=f32)
    down_w = gather(tie(to_owner(down_weight.astype(bf16)), proj)).reshape(FF // 2, D)
    query = proj[:, :half_qk].astype(bf16)
    key_vecs = proj[:, half_qk : 2 * half_qk].astype(bf16)
    value = proj[:, 2 * half_qk : 2 * half_qk + half_d].astype(bf16)
    conv_in = proj[:, 2 * half_qk + half_d : 2 * half_qk + 2 * half_d].astype(bf16)
    gate = proj[:, 2 * half_qk + 2 * half_d :]
    key_t = key_vecs.T
    lane = jnp.arange(LANES)
    values = jnp.where(lane == HEAD_WIDTH, jnp.ones((), bf16), per_head(value))
    att, den, carry, halo = attend(
        link, tie(query, gate_w), key_t, values, allow, on[:, None], fresh[None, :], conv_in[count - 16 :],
        tables, ring,
    )
    halo = jnp.where(ring_id == 0, jnp.zeros((), bf16), halo[14:])
    extended = jnp.concatenate([halo, conv_in], axis=0).astype(f32)
    taps = lax.dynamic_slice_in_dim(from_owner(gains[:, 2:5].T), core * half_d, half_d, axis=1)

    def gating(ext_in, taps_in, gate_in):
        return short_conv(ext_in, taps_in, same) * jax.nn.sigmoid(gate_in)

    gated, gate_back = jax.vjp(gating, extended, taps, gate)
    mix_half = (from_heads(att).astype(f32) + gated).astype(bf16)
    mix_other = swap(mix_half)
    output_half = lax.dynamic_slice_in_dim(output_w, core * half_d, half_d, axis=0)
    output_other = lax.dynamic_slice_in_dim(output_w, (1 - core) * half_d, half_d, axis=0)
    branch = dot_nn(mix_half, output_half) + dot_nn(mix_other, output_other)
    middle = tokens + branch
    normed2_f, norm2_back = jax.vjp(norm_scale, middle, gains[:, 1])
    normed2 = normed2_f.astype(bf16)
    gate_in, up_in = dot_nn(normed2, gate_w), dot_nn(normed2, up_w)

    def swiglu(gate_part, up_part):
        return jax.nn.silu(gate_part) * up_part

    inner_f, inner_back = jax.vjp(swiglu, gate_in, up_in)
    inner = inner_f.astype(bf16)
    feed_part = jnp.dot(inner, down_w, preferred_element_type=f32)

    def own_rows(block):
        return lax.dynamic_slice_in_dim(block, core * local_rows, local_rows, axis=0)

    def other_rows(block):
        return lax.dynamic_slice_in_dim(block, (1 - core) * local_rows, local_rows, axis=0)

    def by_owner(grad, rows):
        blocks = grad.reshape(ring, groups, rows, grad.shape[-1])
        return jnp.pad(blocks, ((0, 0), (0, 0), (0, -rows % 16), (0, 0)))

    def inner_dot(left_mat, right_mat):
        return dot_tn(left_mat, right_mat).astype(bf16)

    orders = both_orders(ring, groups)

    def column_parts(left_mat, right_mat, rows):
        cut = right_mat.shape[1] // 2
        return [by_owner(inner_dot(left_mat, part), rows) for part in (right_mat[:, :cut], right_mat[:, cut:])]

    down_chain = Halving(column_parts(inner, upstream, f_rows), orders)
    down_chain.step()
    upstream_after = upstream
    for one in down_chain.step():
        upstream_after = tie(upstream_after, one)
    inner_grad = dot_nt(upstream_after, down_w).astype(bf16)
    gate_part_grad, up_part_grad = [g.astype(bf16) for g in inner_back(inner_grad.astype(f32))]
    updown_parts = [by_owner(inner_dot(normed2, g), 2 * d_rows) for g in (gate_part_grad, up_part_grad)]
    updown_chain = Halving(updown_parts, orders)
    updown_sent = updown_chain.step()
    for one in updown_sent + down_chain.step(updown_sent[1]):
        gate_part_grad = tie(gate_part_grad, one)
    normed2_part = (dot_nt(gate_part_grad, gate_w) + dot_nt(up_part_grad, up_w)).astype(bf16)
    normed2_grad = normed2_part.astype(f32) + swap(normed2_part).astype(f32)
    middle_part, gain2_grad = norm2_back(normed2_grad)
    middle_grad = upstream.astype(f32) + middle_part
    branch_grad = middle_grad.astype(bf16)
    output_part = inner_dot(mix_half, branch_grad).reshape(ring // 2, 2, groups * d_rows, D)
    output_keep = lax.dynamic_index_in_dim(output_part, core, axis=1, keepdims=False)
    output_send = lax.dynamic_index_in_dim(output_part, 1 - core, axis=1, keepdims=False)
    output_part = in_order(core, output_keep, swap(output_send)).reshape(ring, groups, d_rows, D)
    output_part = jnp.concatenate([output_part[..., :half_d], output_part[..., half_d:]], axis=2)
    output_part = by_owner(output_part.reshape(D, half_d), 2 * d_rows)
    mix_grad = dot_nt(branch_grad, output_half).astype(bf16)
    ext_grad, taps_grad, gate_grad = gate_back(mix_grad.astype(f32))
    query_g, key_g, value_g, after = attend_back(
        link, query, key_vecs, query.T, key_t, values, per_head(mix_grad), att, den, carry, allow, on[:, None],
        on[None, :], fresh[:, None], ext_grad[:8], tables, ring, [],
    )
    sent = updown_chain.step(key_g) + down_chain.step(key_g)
    after = jnp.where(ring_id == ring - 1, 0.0, after[:2])
    conv_grad = ext_grad[2:] + jnp.pad(after, ((count - 2, 0), (0, 0)))
    proj_grad = jnp.concatenate(
        [
            query_g.astype(bf16), key_g.astype(bf16), from_heads(value_g),
            conv_grad.astype(bf16), gate_grad.astype(bf16),
        ],
        axis=1,
    )
    for one in sent:
        proj_grad = tie(proj_grad, one)
    mixer_part = by_owner(inner_dot(normed, proj_grad), 2 * d_rows)
    normed_part = dot_nt(proj_grad, mixer_w)
    normed_grad = own_rows(normed_part) + swap(other_rows(normed_part))
    tokens_own = own_rows(tokens)
    ignored, norm1_back_own = jax.vjp(norm_scale, tokens_own, gains[:, 0])
    input_part, gain1_grad = norm1_back_own(normed_grad)
    input_grad = from_owner(own_rows(middle_grad) + input_part)

    keys = sorted(updown_chain.place, key=updown_chain.place.get)

    def by_bits(partial):
        return partial.reshape((2,) * len(keys) + partial.shape[2:])

    arrays, specs, widths = [], [], []

    def add_chains(array, columns, chain_keys, chain_orders, ranks):
        at = 0
        for number, width in enumerate(columns):
            specs.append((len(arrays), at, width, chain_keys, chain_orders[number % len(chain_orders)], ranks[number]))
            at += width
        arrays.append(array)
        widths.append(len(columns))

    for number, (left, left_keys, order) in enumerate(updown_chain.rest()):
        add_chains(left, [FF // 4, FF // 4], left_keys, [order], [number / 2, 1 + number / 2])
    add_chains(by_bits(mixer_part), [512] * 5 + [384], keys, orders, [0.0, 0.0, 1.0, 1.0, 2.0, 2.0])
    add_chains(by_bits(output_part), [512, 384], keys, orders, [3.0, 3.0])
    summed = reduce_rest(arrays, specs)
    wholes = []
    for number in widths:
        wholes.append(jnp.concatenate(summed[:number], axis=1))
        summed = summed[number:]
    updown_sum = jnp.concatenate(wholes[:2], axis=1)
    down_sum = from_owner(down_chain.result()[:f_rows])
    mixer_sum = wholes[2]
    output_sum = from_owner(
        wholes[3][: 2 * d_rows].reshape(2, d_rows, half_d).transpose(1, 0, 2).reshape(d_rows, D)
    )

    feed = own_rows(feed_part) + swap(tie(other_rows(feed_part), key_g))
    middle_own = own_rows(middle)
    layer = from_owner((middle_own + feed).astype(bf16))
    branch_own = own_rows(branch)
    stats = jnp.stack([jnp.sum(middle_own * middle_own), jnp.sum(branch_own * branch_own), jnp.sum(feed * feed)])

    taps_wide = lax.dynamic_update_slice(jnp.zeros((3, D), f32), taps_grad, (0, core * half_d))
    gain_grad = jnp.concatenate([from_owner(jnp.stack([gain1_grad, 0.5 * gain2_grad])), taps_wide], axis=0)

    square = functools.reduce(jnp.add, [jnp.sum(g * g) for g in (mixer_sum, updown_sum, down_sum, output_sum)])
    spots = jnp.arange(D)[None, :]
    numbers = functools.reduce(
        jnp.add, [jnp.where(spots == i, n, 0.0) for i, n in enumerate((square, stats[0], stats[1], stats[2]))]
    )
    sums = sum_everywhere(jnp.concatenate([gain_grad, numbers, jnp.zeros((2, D), f32)], axis=0), ring, groups)
    gain_total = sums[:5]
    total_sq = sums[5, 0] + jnp.sum(gain_total * gain_total)
    stat_sum = sums[5, 1:4]
    place = (ring_id * 2 + core) * groups + lax.axis_index("fsdp")
    gain_sum = lax.dynamic_index_in_dim(
        gain_total.reshape(5, 2 * ring * groups, d_rows), place, axis=1, keepdims=False
    ).T

    def own_whole(summed):
        blocks = summed[: 2 * d_rows].reshape(2, d_rows, summed.shape[-1])
        keep_rows = lax.dynamic_index_in_dim(blocks, core, axis=0, keepdims=False)
        send_rows = lax.dynamic_index_in_dim(blocks, 1 - core, axis=0, keepdims=False)
        return in_order(core, keep_rows, swap(send_rows))

    mixer_own = own_whole(mixer_sum)
    pieces, at = [], 0
    for width in (half_qk, half_qk, half_d, half_d, half_d):
        pieces += [mixer_own[0, :, at : at + width], mixer_own[1, :, at : at + width]]
        at += width
    mixer_own = jnp.concatenate(pieces, axis=1)
    updown_own = own_whole(updown_sum).reshape(2, d_rows, 2, ring, pair_ff)
    updown_own = updown_own.transpose(1, 2, 3, 0, 4).reshape(d_rows, 2 * FF)
    grad_list = (mixer_own, output_sum, updown_own, down_sum, gain_sum)
    grad_norm = jnp.sqrt(total_sq)
    factor = jnp.minimum(1.0, clip_level / grad_norm)
    masters = (mixer_weight, output_weight, updown_weight, down_weight, gain_weight)
    firsts = (mixer_first, output_first, updown_first, down_first, gain_first)
    seconds = (mixer_second, output_second, updown_second, down_second, gain_second)
    nexts, moms, varis = ([], [], [])
    for index in range(5):
        rate = rate_gain if index == 4 else rate_matrix
        decay = 0.0 if index == 4 else decay_rate
        new_w, new_m, new_v = adam_step(
            masters[index], firsts[index], seconds[index], grad_list[index] * factor, rate, decay
        )
        nexts.append(new_w)
        moms.append(new_m)
        varis.append(new_v)
    layer_rms = jnp.sqrt(stat_sum / (count * ring * groups * D))
    return (layer[None], input_grad[None], *nexts, *moms, *varis, grad_norm, layer_rms)


def solution(mesh):
    shards, groups = mesh.shape["seq"], mesh.shape["fsdp"]
    split = Mesh(mesh.devices.reshape(shards // 2, 2, groups), ("ring", "core", "fsdp"))
    tokens = P("fsdp", ("ring", "core"), None)
    rows = P(("ring", "core", "fsdp"), None)
    pack = P("fsdp", None)
    return jax.shard_map(
        per_device,
        mesh=split,
        in_specs=(tokens,) * 2 + (rows,) * 15 + (pack,) * 3,
        out_specs=(tokens,) * 2 + (rows,) * 15 + (P(), P()),
        check_vma=False,
    )
```

time: 3710 us -> 1050 us (0.28)
  waiting for transfers between devices: 2660 us -> 53.2 us
  Pallas kernels: 0 us -> 489 us
  matrix products: 401 us -> 161 us
  blocking collectives: 164 us -> 0 us
  local copies, waits for them, and re-layouts: 232 us -> 146 us
    unnamed x9 -> x3, waiting for transfers between devices: 1230 us -> 0.05 us
    reduce_scatter x3 -> x0, waiting for transfers between devices: 1230 us -> none  [the longest x1 887 us: per_device(): lax.psum_scatter(mixer_grad, ('seq', 'fsdp'), scatter_dimension=0, tiled=...]
    pallas_call x0 -> x5, Pallas kernels: none -> 489 us  [the longest x1 218 us: gather_rows(): pl.pallas_call(functools.partial(gather_kernel, ring, groups, parts, orde...]
    dot_general x228 -> x17, matrix products: 401 us -> 161 us  [the longest x5 57.6 us: dot_nt(): lax.dot_general(a, b, (((1,), (1,)), ((), ())), preferred_element_type=f32)]
    all_to_all x8 -> x0, waiting for transfers between devices: 122 us -> none  [the longest x1 39.1 us: per_device(): lax.all_to_all(value.reshape(local_rows, shards, v_width), 'seq', split_a...]
    all_gather x4 -> x3, waiting for transfers between devices: 83.5 us -> 0.01 us  [gather(): return lax.all_gather(block, ('ring', 'fsdp'), axis=0, tiled=False)]
    all_gather x1 -> x0, blocking collectives: 71.3 us -> none  [per_device(): lax.all_gather(gain_weight.astype(jnp.bfloat16), ('seq', 'fsdp'), axis=0,...]
    dynamic_slice x84 -> x6, local copies, waits for them, and re-layouts: 65.1 us -> 5.6 us  [the longest x1 3.49 us: other_rows(): lax.dynamic_slice_in_dim(block, (1 - core) * local_rows, local_rows, axis=0)]
  transfers between devices with their start and end apart: 18 -> 28, of which waited for: 14 -> 2; matrix products, arithmetic and copies ran while one was open for 18% -> 36% of each run, Pallas kernels for 0% -> 47%
where the time goes in v1:
time: 1050 us
  Pallas kernels  489 us (47%)
  matrix products  161 us (15%)
  other arithmetic  147 us (14%)
  local copies, waits for them, and re-layouts  146 us (14%)
  waiting for transfers between devices  53.2 us (5%)
  between operations  31.6 us (3%)
  starting transfers between devices  19.5 us (2%)
    pallas_call x1, Pallas kernels, gather_rows(): pl.pallas_call(functools.partial(gather_kernel, ring, groups, parts, orde...  218 us
    pallas_call x1, Pallas kernels, reduce_rest(): pl.pallas_call(functools.partial(reduce_kernel, specs, partners, len(arra...  143 us
    pallas_call x1, Pallas kernels, attend_back(): pl.pallas_call(functools.partial(attend_back_kernel, ring, len(after)), i...  68.8 us
    dot_general x5, matrix products, dot_nt(): lax.dot_general(a, b, (((1,), (1,)), ((), ())), preferred_element_type=f32)  57.6 us
    ppermute x12, waiting for transfers between devices, step(): got = lax.ppermute(send, axis, [(i, i ^ 1 << bit) for i in range(size)])  52.1 us
    unnamed x292, local copies, waits for them, and re-layouts  47.6 us
    dot_general x6, matrix products, dot_tn(): lax.dot_general(a, b, (((0,), (0,)), ((), ())), preferred_element_type=f32)  42.4 us
    pallas_call x1, Pallas kernels, attend(): pl.pallas_call(functools.partial(attend_kernel, ring), in_specs=[smem] +...  41 us
  transfers between devices with their start and end apart: 28, of which 2 were waited for; matrix products, arithmetic and copies ran while one was open for 36% of the time, Pallas kernels for 47%

profile of v1, /device:TPU:0, one launch (start us, length us, event | category | flops | bytes accessed | tf_op | source)
XLA Modules:
  0.0 1046.3 jit_solution(12663015000911686521)
XLA Ops:
  20.7 217.9 %gather_rows.1 = (bf16[2,2,2,1,2,112,3072]{6,5,4,3,2,1,0:T(8,128)(2,1)}, bf16[2,2,2,2,2,56,1792]{6,5,4,3,2,1,0:T(8,128)(2,1)}) custom-call(bf16[1,1,1,1,1,112,3072]{6,5,4,3,2,1,0:T(8,128)(2,1)} %bitcast.333, bf16[1,1,1,2,1,56,896]{6,5,4,3,2,1,0:T(8,128)(2,1)} %maximum_bitcast_fusion.1.refs_1_), custom_call_target="tpu_custom_call" | custom-call | bytes 284426240 | tf_op jit(solution)/shard_map/gather_rows/pallas_call | solution.py:191
  263.4 4.5 select_bitcast_fusion.1
  274.5 13.9 %fusion.106 = (bf16[768,2944]{1,0:T(8,128)(2,1)}, f32[768,2944]{1,0:T(8,128)S(1)}) fusion(bf16[768,1792]{1,0:T(8,128)(2,1)S(1)} %multiply_convert_fusion.2, bf16[1792,3072]{1,0:T(8,128)(2,1)} %bitcast.356), kind=kOutput, calls=%fused_computation.316 | convolution fusion | flops 8105656320 | bytes 26869760 | tf_op jit(solution)/shard_map/dot_general | solution.py:881
  288.9 2.9 copy-done.50
  291.8 3.1 fusion.101
  296.4 2.6 copy.197
  313.5 41.0 %attend.1 = (bf16[8,768,128]{2,1,0:T(8,128)(2,1)S(1)}, f32[768,128]{1,0:T(8,128)S(1)}, bf16[8,160,128]{2,1,0:T(8,128)(2,1)S(1)}, bf16[16,896]{1,0:T(8,128)(2,1)S(1)}) custom-call(f32[8,8]{1,0:T(8,128)S(1)} %fusion.85.link_ref, bf16[768,128]{1,0:T(8,128)(2,1)S(1)} %get-tuple-element.101.q_ref, bf16[128,768]{1,0:T(8,128)(2,1)S(1)} %copy.198.kt_ref, ...), custom_call_target="tpu_custom_call" | custom-call | tf_op jit(solution)/shard_map/attend/pallas_call | solution.py:604
  359.6 3.4 copy.200
  363.0 3.4 copy.202
  368.4 5.0 add_convert_fusion.6
  373.5 3.3 pad_maximum_fusion.2
  376.8 5.4 fusion.19
  382.3 7.9 multiply_reduce_fusion.2
  394.4 9.9 fusion.107
  404.4 12.2 %multiply_convert_fusion = (bf16[768,2048]{1,0:T(8,128)(2,1)S(1)}, f32[768,2048]{1,0:T(8,128)}) fusion(f32[768,2048]{1,0:T(8,128)} %fusion.107, bf16[768,1792]{1,0:T(8,128)(2,1)} %copy-done.54, bf16[1792,2048]{1,0:T(8,128)(2,1)} %bitcast.364), kind=kOutput, calls=%fused_computation.15 | convolution fusion | flops 5646581760 | bytes 25821184 | tf_op jit(solution)/shard_map/dot_general | solution.py:63
  416.6 3.7 convolution_convert_fusion.4
  423.8 3.7 convolution_convert_fusion.5
  429.9 3.5 collective-permute-start.7
  433.4 52.1 %collective-permute-done.8 = bf16[2,2,2,1,128,896]{5,4,1,0,3,2:T(8,128)(2,1)} collective-permute-done((bf16[2,2,2,1,128,896]{5,4,1,0,3,2:T(8,128)(2,1)}, bf16[2,2,2,1,128,896]{5,4,1,0,3,2:T(8,128)(2,1)}, u32[]{:S(2)}, u32[]{:S(2)}) %collective-permute-start.8) | collective-permute-done | bytes 1835040 | tf_op jit(solution)/shard_map/ppermute | solution.py:721
  485.5 2.6 add_convert_fusion.7
  490.7 2.6 add_convert_fusion.8
  498.2 13.2 %fusion.7 = (bf16[768,2048]{1,0:T(8,128)(2,1)S(1)}, bf16[768,2048]{1,0:T(8,128)(2,1)S(1)}) fusion(f32[768,2048]{1,0:T(8,128)} %fusion.107, f32[768,2048]{1,0:T(8,128)} %get-tuple-element.159, bf16[768,1792]{1,0:T(8,128)(2,1)} %bitcast.332, bf16[2048,1792]{1,0:T(8,128)(2,1)} %all-gather.10.cloned.1.call-done), kind=kOutput, calls=%fused_computation.14 | convolution fusion | flops 5657591808 | bytes 28966912 | tf_op jit(solution)/shard_map/dot_general | solution.py:71
  511.4 11.5 %convolution_convert_fusion.1 = bf16[1792,2048]{1,0:T(8,128)(2,1)S(1)} fusion(bf16[768,1792]{1,0:T(8,128)(2,1)S(1)} %copy-done.55, bf16[768,2048]{1,0:T(8,128)(2,1)S(1)} %get-tuple-element.161, f32[768,2048]{1,0:T(8,128)} %fusion.107), kind=kOutput, calls=%fused_computation.9 | convolution fusion | flops 5651824640 | bytes 19529728 | tf_op jit(solution)/shard_map/dot_general | solution.py:67
  522.9 6.1 convolution_convert_fusion.2
  529.5 2.5 copy-done.41
  536.5 2.4 copy.259
  541.4 2.4 fusion.64
  549.9 7.6 fusion.12
  557.5 13.0 %add_convert_fusion = bf16[768,1792]{1,0:T(8,128)(2,1)} fusion(f32[768,1792]{1,0:T(8,128)} %fusion.12, bf16[1792,2048]{1,0:T(8,128)(2,1)S(1)} %bitcast.367, bf16[768,2048]{1,0:T(8,128)(2,1)} %copy-done.110, f32[768,2048]{1,0:T(8,128)} %fusion.107), kind=kOutput, calls=%fused_computation.22 | convolution fusion | flops 5650907136 | bytes 25034752 | tf_op jit(solution)/shard_map/dot_general | solution.py:71
  574.2 3.3 multiply_reduce_fusion.5
  577.4 11.2 %fusion.108 = f32[768,1792]{1,0:T(8,128)} fusion(bf16[768,2048]{1,0:T(8,128)(2,1)} %copy-done.109, bf16[2048,1792]{1,0:T(8,128)(2,1)} %all-gather.10.cloned.1.call-done), kind=kOutput, calls=%fused_computation.318 | convolution fusion | flops 5637144576 | bytes 15990784 | tf_op jit(solution)/shard_map/dot_general | solution.py:918
  592.7 4.1 multiply_reduce_fusion
  596.8 4.0 fusion.9
  600.9 9.6 multiply_reduce_fusion.9
  610.6 5.7 multiply_multiply_fusion.2
  616.3 2.7 copy.219
  619.0 2.5 copy.220
  621.5 3.1 pad.35.up_ref
  625.9 68.8 %attend_back.1 = (f32[768,128]{1,0:T(8,128)S(1)}, f32[768,128]{1,0:T(8,128)S(1)}, bf16[8,768,128]{2,1,0:T(8,128)(2,1)S(1)}, f32[8,896]{1,0:T(8,128)S(1)}) custom-call(f32[8,8]{1,0:T(8,128)S(1)} %fusion.85.link_ref, bf16[768,128]{1,0:T(8,128)(2,1)S(1)} %copy-done.3, bf16[768,128]{1,0:T(8,128)(2,1)S(1)} %copy-done.2, bf16[128,768]{1,0:T(8,128)(2,1)S(1)} %copy.221.qt_ref, ...), custom_call_target="tpu_custom_call" | custom-call | tf_op jit(solution)/shard_map/attend_back/pallas_call | solution.py:632
  705.4 4.1 fusion.39
  712.2 5.8 convolution_convert_fusion.3
  717.9 4.1 fusion.40
  730.4 3.5 fusion.53
  734.2 2.8 fusion.54
  737.0 14.2 %fusion = f32[768,1792]{1,0:T(8,128)} fusion(bf16[1792,3072]{1,0:T(8,128)(2,1)} %bitcast.357, bf16[768,2944]{1,0:T(8,128)(2,1)S(1)} %fusion.54, bf16[]{:T(256)} %bitcast.70, bf16[]{:T(256)} %bitcast.69, bf16[]{:T(256)} %bitcast.68, bf16[]{:T(256)} %bitcast.67), kind=kOutput, calls=%fused_computation.2 | convolution fusion | flops 8112439296 | bytes 20580352 | tf_op jit(solution)/shard_map/dot_general | solution.py:71
  751.2 11.5 %convolution_convert_fusion = bf16[1792,2944]{1,0:T(8,128)(2,1)} fusion(bf16[768,1792]{1,0:T(8,128)(2,1)S(1)} %copy-done.53, bf16[768,2944]{1,0:T(8,128)(2,1)S(1)} %fusion.54, bf16[]{:T(256)} %bitcast.70, bf16[]{:T(256)} %bitcast.69, bf16[]{:T(256)} %bitcast.68, bf16[]{:T(256)} %bitcast.67), kind=kOutput, calls=%fused_computation | convolution fusion | flops 8117714944 | bytes 17825800 | tf_op jit(solution)/shard_map/dot_general | solution.py:67
  764.8 3.5 constant_dynamic-slice_fusion
  768.3 3.5 dynamic-slice_add_fusion.1
  781.1 5.0 fusion.41.refs_0_
  786.2 5.0 fusion.42.refs_1_
  791.2 143.4 %reduce_rest.1 = (f32[112,1024]{1,0:T(8,128)}, f32[112,1024]{1,0:T(8,128)}, f32[112,1024]{1,0:T(8,128)}, f32[112,1024]{1,0:T(8,128)}, f32[112,512]{1,0:T(8,128)}...) custom-call(bf16[2,2,112,2048]{3,2,1,0:T(8,128)(2,1)} %fusion.41.ref, ...), custom_call_target="tpu_custom_call" | custom-call | tf_op jit(solution)/shard_map/reduce_rest/pallas_call | solution.py:308
  943.0 2.7 reshape_reshape.3
  945.7 2.6 copy.247
  948.3 2.5 reshape.535
  959.2 4.3 multiply_reduce_fusion.10
  963.7 4.9 multiply_reduce_fusion.4
  970.5 5.7 fusion.23
  977.8 2.7 copy.226
  980.5 2.5 copy.227
  990.4 17.7 %sum_everywhere.1 = f32[8,1792]{1,0:T(8,128)} custom-call(f32[8,1792]{1,0:T(8,128)} %maximum_maximum_fusion.in_ref), custom_call_target="tpu_custom_call" | custom-call | tf_op jit(solution)/shard_map/sum_everywhere/pallas_call | solution.py:353
  1018.0 3.0 fusion.43
  1021.0 2.8 mul.730
  1030.8 2.6 multiply_subtract_fusion.1
  1034.8 3.4 multiply_subtract_fusion
  (514 shorter events, 172.5 us)
Async XLA Ops:
  7.2 296.6 %all-gather.8.cloned.1.call-start = ((), (), s32[]{:S(2)}) async-start(), calls=%async_computation.1 | async-start | bytes 7798784 | tf_op jit(solution)/shard_map/all_gather | solution.py:811
  11.7 1.6 collective-permute-start.2
  14.2 390.2 %all-gather.6.cloned.1.call-start = ((), (), s32[]{:S(2)}) async-start(), calls=%async_computation | async-start | bytes 7798784 | tf_op jit(solution)/shard_map/all_gather | solution.py:811
  16.1 1.6 collective-permute-start.3
  17.0 2.7 collective-permute-start.1
  17.2 2.4 collective-permute-start.5
  19.7 222.1 %copy-start.63 = (bf16[1,384,1792]{2,1,0:T(8,128)(2,1)S(1)}, bf16[1,384,1792]{2,1,0:T(8,128)(2,1)}, u32[]{:S(2)}) copy-start(bf16[1,384,1792]{2,1,0:T(8,128)(2,1)} %param.27) | copy-start | bytes 4128772
  241.3 256.9 %all-gather.10.cloned.1.call-start = ((), (), s32[]{:S(2)}) async-start(), calls=%async_computation.2 | async-start | bytes 7798784 | tf_op jit(solution)/shard_map/all_gather | solution.py:811
  244.4 19.0 %collective-permute-start.6 = (bf16[384,1792]{1,0:T(8,128)(2,1)}, bf16[384,1792]{1,0:T(8,128)(2,1)}, u32[]{:S(2)}, u32[]{:S(2)}) collective-permute-start(bf16[384,1792]{1,0:T(8,128)(2,1)} %copy.210), channel_id=1, source_target_pairs={{0,2},{2,0},{1,3},{3,1},{4,6},{6,4},{5,7},{7,5},{8,10},{10,8},{9,1... | collective-permute-start | bytes 4128776 | tf_op jit(solution)/shard_map/ppermute | solution.py:677
  247.7 9.1 copy-start.44
  247.7 15.7 %collective-permute-start = (bf16[384,1792]{1,0:T(8,128)(2,1)S(1)}, bf16[384,1792]{1,0:T(8,128)(2,1)}, u32[]{:S(2)}, u32[]{:S(2)}) collective-permute-start(bf16[384,1792]{1,0:T(8,128)(2,1)S(1)} %copy.189), channel_id=1, source_target_pairs={{0,2},{2,0},{1,3},{3,1},{4,6},{6,4},{5,7},{7,5},{8,10},{10,8},{9,1... | collective-permute-start | bytes 4128776 | tf_op jit(solution)/shard_map/ppermute | solution.py:677
  251.7 116.0 %copy-start.88 = (f32[768]{0:T(1024)}, f32[768]{0:T(1024)S(1)}, u32[]{:S(2)}) copy-start(f32[768]{0:T(1024)S(1)} %get-tuple-element.150) | copy-start | bytes 9220
  263.4 8.2 copy-start.78
  274.5 13.9 %copy-start.52 = (bf16[768,1792]{1,0:T(8,128)(2,1)}, bf16[768,1792]{1,0:T(8,128)(2,1)S(1)}, u32[]{:S(2)}) copy-start(bf16[768,1792]{1,0:T(8,128)(2,1)S(1)} %multiply_convert_fusion.2) | copy-start | bytes 8257540
  300.5 8.1 copy-start.19
  302.4 52.1 %copy-start = (bf16[8,768,128]{2,1,0:T(8,128)(2,1)}, bf16[8,768,128]{2,1,0:T(8,128)(2,1)S(1)}, u32[]{:S(2)}) copy-start(bf16[8,768,128]{2,1,0:T(8,128)(2,1)S(1)} %pad_select_fusion.v_ref) | copy-start | bytes 4718596
  373.5 8.8 collective-permute-start.4
  373.5 8.8 slice-start
  404.4 12.2 %copy-start.33 = (bf16[2,384,1792]{2,1,0:T(8,128)(2,1)S(1)}, bf16[2,384,1792]{2,1,0:T(8,128)(2,1)}, u32[]{:S(2)}) copy-start(bf16[2,384,1792]{2,1,0:T(8,128)(2,1)} %pad_maximum_fusion.2) | copy-start | bytes 8257540
  422.7 62.8 %collective-permute-start.8 = (bf16[2,2,2,1,128,896]{5,4,1,0,3,2:T(8,128)(2,1)}, bf16[2,2,2,1,128,896]{5,4,1,0,3,2:T(8,128)(2,1)}, u32[]{:S(2)}, u32[]{:S(2)}) collective-permute-start(bf16[2,2,2,1,128,896]{5,4,1,0,3,2:T(8,128)(2,1)} %copy.257), channel_id=1, source_target_pairs={{0,1},{1,0},{2,3},{3,2},{4,5},{5,4},{6,7},{7,6},{8,9},{9,8},{10,11... | collective-permute-start | bytes 5505032 | tf_op jit(solution)/shard_map/ppermute | solution.py:721
  429.9 60.8 %collective-permute-start.7 = (bf16[2,2,1,2,128,896]{5,4,1,0,3,2:T(8,128)(2,1)}, bf16[2,2,1,2,128,896]{5,4,1,0,3,2:T(8,128)(2,1)}, u32[]{:S(2)}, u32[]{:S(2)}) collective-permute-start(bf16[2,2,1,2,128,896]{5,4,1,0,3,2:T(8,128)(2,1)} %copy.255), channel_id=1, source_target_pairs={{0,4},{4,0},{8,12},{12,8},{16,20},{20,16},{24,28},{28,24},{1,5},{5... | collective-permute-start | bytes 5505032 | tf_op jit(solution)/shard_map/ppermute | solution.py:721
  433.4 63.0 %copy-start.29 = (bf16[1,384,1792]{2,1,0:T(8,128)(2,1)S(1)}, bf16[1,384,1792]{2,1,0:T(8,128)(2,1)}, u32[]{:S(2)}) copy-start(bf16[1,384,1792]{2,1,0:T(8,128)(2,1)} %get-tuple-element.115) | copy-start | bytes 4128772
  489.3 52.1 %collective-permute-start.10 = (bf16[2,2,1,1,128,896]{5,4,1,0,3,2:T(8,128)(2,1)}, bf16[2,2,1,1,128,896]{5,4,1,0,3,2:T(8,128)(2,1)}, u32[]{:S(2)}, u32[]{:S(2)}) collective-permute-start(bf16[2,2,1,1,128,896]{5,4,1,0,3,2:T(8,128)(2,1)} %add_convert_fusion.7), channel_id=1, source_target_pairs={{0,4},{4,0},{8,12},{12,8},{16,20},{20,16},{24,28},{28,24},{1,5},{5... | collective-permute-start | bytes 2752520 | tf_op jit(solution)/shard_map/ppermute | solution.py:721
  494.5 51.2 %collective-permute-start.9 = (bf16[2,2,1,1,128,896]{5,4,1,0,3,2:T(8,128)(2,1)}, bf16[2,2,1,1,128,896]{5,4,1,0,3,2:T(8,128)(2,1)}, u32[]{:S(2)}, u32[]{:S(2)}) collective-permute-start(bf16[2,2,1,1,128,896]{5,4,1,0,3,2:T(8,128)(2,1)} %add_convert_fusion.8), channel_id=1, source_target_pairs={{0,1},{1,0},{2,3},{3,2},{4,5},{5,4},{6,7},{7,6},{8,9},{9,8},{10,11... | collective-permute-start | bytes 2752520 | tf_op jit(solution)/shard_map/ppermute | solution.py:721
  498.2 13.2 %copy-start.55 = (bf16[768,1792]{1,0:T(8,128)(2,1)S(1)}, bf16[768,1792]{1,0:T(8,128)(2,1)}, u32[]{:S(2)}) copy-start(bf16[768,1792]{1,0:T(8,128)(2,1)} %copy-done.54) | copy-start | bytes 8257540
  511.4 11.5 %copy-start.110 = (bf16[768,2048]{1,0:T(8,128)(2,1)}, bf16[768,2048]{1,0:T(8,128)(2,1)S(1)}, u32[]{:S(2)}) copy-start(bf16[768,2048]{1,0:T(8,128)(2,1)S(1)} %get-tuple-element.161) | copy-start | bytes 9437188
  511.4 11.5 %copy-start.111 = (bf16[768,2048]{1,0:T(8,128)(2,1)}, bf16[768,2048]{1,0:T(8,128)(2,1)S(1)}, u32[]{:S(2)}) copy-start(bf16[768,2048]{1,0:T(8,128)(2,1)S(1)} %get-tuple-element.160) | copy-start | bytes 9437188
  522.9 13.2 %copy-start.40 = (bf16[1792,2048]{1,0:T(8,128)(2,1)}, bf16[1792,2048]{1,0:T(8,128)(2,1)S(1)}, u32[]{:S(2)}) copy-start(bf16[1792,2048]{1,0:T(8,128)(2,1)S(1)} %convolution_convert_fusion.1) | copy-start | bytes 22020100
  536.1 13.8 %slice-start.11 = ((s8[7340032]{0:T(1024)(128)(4,1)}), s8[3145728]{0:T(1024)(128)(4,1)S(1)}, s32[]{:S(2)}) async-start(s8[7340032]{0:T(1024)(128)(4,1)} %bitcast.361), calls=%async_computation.14 | async-start | bytes 6291456
  536.5 13.3 %slice-start.12 = ((s8[7340032]{0:T(1024)(128)(4,1)}), s8[4194304]{0:T(1024)(128)(4,1)S(1)}, s32[]{:S(2)}) async-start(s8[7340032]{0:T(1024)(128)(4,1)} %bitcast.361), calls=%async_computation.15 | async-start | bytes 8388608
  539.0 10.9 %copy-start.112 = (bf16[768,2048]{1,0:T(8,128)(2,1)S(1)}, bf16[768,2048]{1,0:T(8,128)(2,1)}, u32[]{:S(2)}) copy-start(bf16[768,2048]{1,0:T(8,128)(2,1)} %copy-done.111) | copy-start | bytes 9437188
  541.4 16.1 %slice-start.13 = ((s8[7340032]{0:T(1024)(128)(4,1)}), s8[4194304]{0:T(1024)(128)(4,1)S(1)}, s32[]{:S(2)}) async-start(s8[7340032]{0:T(1024)(128)(4,1)} %bitcast.365), calls=%async_computation.16 | async-start | bytes 8388608
  557.5 13.0 %copy-start.87 = (f32[768]{0:T(1024)S(1)}, f32[768]{0:T(1024)}, u32[]{:S(2)}) copy-start(f32[768]{0:T(1024)} %copy-done.86) | copy-start | bytes 9220
  557.5 13.0 %copy-start.85 = (f32[768]{0:T(1024)S(1)}, f32[768]{0:T(1024)}, u32[]{:S(2)}) copy-start(f32[768]{0:T(1024)} %copy-done.84) | copy-start | bytes 9220
  570.5 22.1 %collective-permute-start.11 = (bf16[768,1792]{1,0:T(8,128)(2,1)}, bf16[768,1792]{1,0:T(8,128)(2,1)}, u32[]{:S(2)}, u32[]{:S(2)}) collective-permute-start(bf16[768,1792]{1,0:T(8,128)(2,1)} %add_convert_fusion), channel_id=1, source_target_pairs={{0,2},{2,0},{1,3},{3,1},{4,6},{6,4},{5,7},{7,5},{8,10},{10,8},{9,1... | collective-permute-start | bytes 8257544 | tf_op jit(solution)/shard_map/ppermute | solution.py:677
  573.4 15.2 %copy-start.98 = (f32[384]{0:T(512)}, f32[384]{0:T(512)S(1)}, u32[]{:S(2)}) copy-start(f32[384]{0:T(512)S(1)} %multiply_reduce_fusion.12) | copy-start | bytes 4612
  574.1 18.5 %slice-start.4 = ((s8[5505024]{0:T(1024)(128)(4,1)}), s8[4194304]{0:T(1024)(128)(4,1)S(1)}, s32[]{:S(2)}) async-start(s8[5505024]{0:T(1024)(128)(4,1)} %bitcast.282), calls=%async_computation.7 | async-start | bytes 8388608
  577.4 15.3 %slice-start.5 = ((s8[5505024]{0:T(1024)(128)(4,1)}), s8[1310720]{0:T(1024)(128)(4,1)S(1)}, s32[]{:S(2)}) async-start(s8[5505024]{0:T(1024)(128)(4,1)} %bitcast.282), calls=%async_computation.8 | async-start | bytes 2621440
  588.6 8.2 copy-start.34
  588.6 116.8 %collective-permute-start.13 = (bf16[2,2,1,2,112,2048]{5,4,1,0,3,2:T(8,128)(2,1)}, bf16[2,2,1,2,112,2048]{5,4,1,0,3,2:T(8,128)(2,1)}, u32[]{:S(2)}, u32[]{:S(2)}) collective-permute-start(bf16[2,2,1,2,112,2048]{5,4,1,0,3,2:T(8,128)(2,1)} %copy.258), channel_id=1, source_target_pairs={{0,4},{4,0},{8,12},{12,8},{16,20},{20,16},{24,28},{28,24},{1,5},{5... | collective-permute-start | bytes 11010056 | tf_op jit(solution)/shard_map/ppermute | solution.py:721
  588.9 129.0 %collective-permute-start.14 = (bf16[2,2,2,1,112,2048]{5,4,1,0,3,2:T(8,128)(2,1)}, bf16[2,2,2,1,112,2048]{5,4,1,0,3,2:T(8,128)(2,1)}, u32[]{:S(2)}, u32[]{:S(2)}) collective-permute-start(bf16[2,2,2,1,112,2048]{5,4,1,0,3,2:T(8,128)(2,1)} %copy.259), channel_id=1, source_target_pairs={{0,1},{1,0},{2,3},{3,2},{4,5},{5,4},{6,7},{7,6},{8,9},{9,8},{10,11... | collective-permute-start | bytes 11010056 | tf_op jit(solution)/shard_map/ppermute | solution.py:721
  590.6 105.3 %collective-permute-start.15 = (bf16[2,1,1,1,128,896]{5,4,1,0,3,2:T(8,128)(2,1)}, bf16[2,1,1,1,128,896]{5,4,1,0,3,2:T(8,128)(2,1)}, u32[]{:S(2)}, u32[]{:S(2)}) collective-permute-start(bf16[2,1,1,1,128,896]{5,4,1,0,3,2:T(8,128)(2,1)} %fusion.63), channel_id=1, source_target_pairs={{0,8},{4,12},{8,0},{12,4},{16,24},{20,28},{24,16},{28,20},{1,9},{5... | collective-permute-start | bytes 1376264 | tf_op jit(solution)/shard_map/ppermute | solution.py:721
  592.1 109.5 %collective-permute-start.16 = (bf16[2,1,1,1,128,896]{5,4,1,0,3,2:T(8,128)(2,1)}, bf16[2,1,1,1,128,896]{5,4,1,0,3,2:T(8,128)(2,1)}, u32[]{:S(2)}, u32[]{:S(2)}) collective-permute-start(bf16[2,1,1,1,128,896]{5,4,1,0,3,2:T(8,128)(2,1)} %fusion.64), channel_id=1, source_target_pairs={{0,8},{4,12},{8,0},{12,4},{16,24},{20,28},{24,16},{28,20},{1,9},{5... | collective-permute-start | bytes 1376264 | tf_op jit(solution)/shard_map/ppermute | solution.py:721
  592.7 8.2 slice-start.8
  592.7 8.2 slice-start.9
  600.9 9.7 copy-start.27
  600.9 9.7 copy-start.93
  600.9 9.7 copy-start.95
  600.9 9.7 copy-start.97
  624.7 87.5 %slice-start.6 = ((s8[5505024]{0:T(1024)(128)(4,1)}), s8[4194304]{0:T(1024)(128)(4,1)S(1)}, s32[]{:S(2)}) async-start(s8[5505024]{0:T(1024)(128)(4,1)} %bitcast.286), calls=%async_computation.9 | async-start | bytes 8388608
  625.9 86.3 %slice-start.7 = ((s8[5505024]{0:T(1024)(128)(4,1)}), s8[1310720]{0:T(1024)(128)(4,1)S(1)}, s32[]{:S(2)}) async-start(s8[5505024]{0:T(1024)(128)(4,1)} %bitcast.286), calls=%async_computation.10 | async-start | bytes 2621440
  699.2 72.5 %collective-permute-start.22 = (bf16[1,1,1,1,128,896]{5,4,1,0,3,2:T(8,128)(2,1)}, bf16[1,1,1,1,128,896]{5,4,1,0,3,2:T(8,128)(2,1)}, u32[]{:S(2)}, u32[]{:S(2)}) collective-permute-start(bf16[1,1,1,1,128,896]{5,4,1,0,3,2:T(8,128)(2,1)} %fusion.66), channel_id=1, source_target_pairs={{0,16},{4,20},{8,24},{12,28},{16,0},{20,4},{24,8},{28,12},{1,17},{... | collective-permute-start | bytes 688136 | tf_op jit(solution)/shard_map/ppermute | solution.py:721
  704.9 68.8 %collective-permute-start.23 = (bf16[1,1,1,1,128,896]{5,4,1,0,3,2:T(8,128)(2,1)}, bf16[1,1,1,1,128,896]{5,4,1,0,3,2:T(8,128)(2,1)S(1)}, u32[]{:S(2)}, u32[]{:S(2)}) collective-permute-start(bf16[1,1,1,1,128,896]{5,4,1,0,3,2:T(8,128)(2,1)} %fusion.67), channel_id=1, source_target_pairs={{0,16},{4,20},{8,24},{12,28},{16,0},{20,4},{24,8},{28,12},{1,17},{... | collective-permute-start | bytes 688136 | tf_op jit(solution)/shard_map/ppermute | solution.py:721
  710.7 70.4 %collective-permute-start.18 = (bf16[2,2,1,1,112,2048]{5,4,1,0,3,2:T(8,128)(2,1)}, bf16[2,2,1,1,112,2048]{5,4,1,0,3,2:T(8,128)(2,1)}, u32[]{:S(2)}, u32[]{:S(2)}) collective-permute-start(bf16[2,2,1,1,112,2048]{5,4,1,0,3,2:T(8,128)(2,1)} %fusion.39), channel_id=1, source_target_pairs={{0,1},{1,0},{2,3},{3,2},{4,5},{5,4},{6,7},{7,6},{8,9},{9,8},{10,11... | collective-permute-start | bytes 5505032 | tf_op jit(solution)/shard_map/ppermute | solution.py:721
  723.2 62.9 %collective-permute-start.19 = (bf16[2,2,1,1,112,2048]{5,4,1,0,3,2:T(8,128)(2,1)}, bf16[2,2,1,1,112,2048]{5,4,1,0,3,2:T(8,128)(2,1)}, u32[]{:S(2)}, u32[]{:S(2)}) collective-permute-start(bf16[2,2,1,1,112,2048]{5,4,1,0,3,2:T(8,128)(2,1)} %fusion.40), channel_id=1, source_target_pairs={{0,4},{4,0},{8,12},{12,8},{16,20},{20,16},{24,28},{28,24},{1,5},{5... | collective-permute-start | bytes 5505032 | tf_op jit(solution)/shard_map/ppermute | solution.py:721
  737.0 14.2 %copy-start.53 = (bf16[768,1792]{1,0:T(8,128)(2,1)S(1)}, bf16[768,1792]{1,0:T(8,128)(2,1)}, u32[]{:S(2)}) copy-start(bf16[768,1792]{1,0:T(8,128)(2,1)} %copy-done.52) | copy-start | bytes 8257540
  751.2 11.5 %copy-start.51 = (bf16[896,1792]{1,0:T(8,128)(2,1)S(1)}, bf16[896,1792]{1,0:T(8,128)(2,1)}, u32[]{:S(2)}) copy-start(bf16[896,1792]{1,0:T(8,128)(2,1)} %convolution_convert_fusion.3) | copy-start | bytes 9633796
  764.0 12.9 %collective-permute-start.20 = (bf16[4,112,1792]{2,1,0:T(8,128)(2,1)}, bf16[4,112,1792]{2,1,0:T(8,128)(2,1)S(1)}, u32[]{:S(2)}, u32[]{:S(2)}) collective-permute-start(bf16[4,112,1792]{2,1,0:T(8,128)(2,1)} %dynamic-slice_bitcast_fusion), channel_id=1, source_target_pairs={{0,2},{2,0},{1,3},{3,1},{4,6},{6,4},{5,7},{7,5},{8,10},{10,8},{9,1... | collective-permute-start | bytes 4816904 | tf_op jit(solution)/shard_map/ppermute | solution.py:677
  771.7 191.9 %collective-permute-start.12 = (f32[384,1792]{1,0:T(8,128)}, f32[384,1792]{1,0:T(8,128)}, u32[]{:S(2)}, u32[]{:S(2)}) collective-permute-start(f32[384,1792]{1,0:T(8,128)} %dynamic-slice_add_fusion.1), channel_id=1, source_target_pairs={{0,2},{2,0},{1,3},{3,1},{4,6},{6,4},{5,7},{7,5},{8,10},{10,8},{9,1... | collective-permute-start | bytes 8257544 | tf_op jit(solution)/shard_map/ppermute | solution.py:677
  773.8 185.5 %collective-permute-start.17 = (f32[384,1792]{1,0:T(8,128)}, f32[384,1792]{1,0:T(8,128)}, u32[]{:S(2)}, u32[]{:S(2)}) collective-permute-start(f32[384,1792]{1,0:T(8,128)} %constant_dynamic-slice_fusion), channel_id=1, source_target_pairs={{0,2},{2,0},{1,3},{3,1},{4,6},{6,4},{5,7},{7,5},{8,10},{10,8},{9,1... | collective-permute-start | bytes 8257544 | tf_op jit(solution)/shard_map/ppermute | solution.py:677
  941.5 15.3 %collective-permute-start.21 = (f32[56,2944]{1,0:T(8,128)}, f32[56,2944]{1,0:T(8,128)}, u32[]{:S(2)}, u32[]{:S(2)}) collective-permute-start(f32[56,2944]{1,0:T(8,128)} %dynamic-slice_bitcast_fusion.2), channel_id=1, source_target_pairs={{0,2},{2,0},{1,3},{3,1},{4,6},{6,4},{5,7},{7,5},{8,10},{10,8},{9,1... | collective-permute-start | bytes 1978376 | tf_op jit(solution)/shard_map/ppermute | solution.py:677
  941.7 10.7 %copy-start.36 = (f32[112,4096]{1,0:T(8,128)}, f32[112,4096]{1,0:T(8,128)S(1)}, u32[]{:S(2)}) copy-start(f32[112,4096]{1,0:T(8,128)S(1)} %constant_dynamic-update-slice_fusion.17) | copy-start | bytes 5505028
  950.9 63.3 %collective-permute-start.24 = (f32[56,4096]{1,0:T(8,128)}, f32[56,4096]{1,0:T(8,128)}, u32[]{:S(2)}, u32[]{:S(2)}) collective-permute-start(f32[56,4096]{1,0:T(8,128)} %dynamic-slice_bitcast_fusion.1), channel_id=1, source_target_pairs={{0,2},{2,0},{1,3},{3,1},{4,6},{6,4},{5,7},{7,5},{8,10},{10,8},{9,1... | collective-permute-start | bytes 2752520 | tf_op jit(solution)/shard_map/ppermute | solution.py:677
  959.2 11.3 %slice-start.2 = ((s8[5505024]{0:T(1024)(128)(4,1)}), s8[1310720]{0:T(1024)(128)(4,1)S(1)}, s32[]{:S(2)}) async-start(s8[5505024]{0:T(1024)(128)(4,1)} %bitcast.279), calls=%async_computation.5 | async-start | bytes 2621440
  (92 other events, 285.2 us)
Sparse Core Ops, SparseCore 0:
  14.3 151.0 all-gather.7
  241.4 115.5 all-gather.5
  360.4 119.2 all-gather.9

commit v2 on v1

--- a/solution.py
+++ b/solution.py
@@ -961,8 +961,11 @@
     output_part = by_owner(output_part.reshape(D, half_d), 2 * d_rows)
     mix_grad = dot_nt(branch_grad, output_half).astype(bf16)
     ext_grad, taps_grad, gate_grad = gate_back(mix_grad.astype(f32))
+    head_grad = mix_grad
+    for got in updown_chain.got:
+        head_grad = tie(head_grad, got)
     query_g, key_g, value_g, after = attend_back(
-        link, query, key_vecs, query.T, key_t, values, per_head(mix_grad), att, den, carry, allow, on[:, None],
+        link, query, key_vecs, query.T, key_t, values, per_head(head_grad), att, den, carry, allow, on[:, None],
         on[None, :], fresh[:, None], ext_grad[:8], tables, ring, [],
     )
     sent = updown_chain.step(key_g) + down_chain.step(key_g)

time: 1050 us -> 1050 us (level)
  Pallas kernels: 489 us -> 462 us
  waiting for transfers between devices: 53.2 us -> 75.8 us
    pallas_call x1, Pallas kernels: 68.8 us -> 43.6 us  [attend_back(): pl.pallas_call(functools.partial(attend_back_kernel, ring, len(after)), i...]
    ppermute x12, waiting for transfers between devices: 52.1 us -> 74.6 us  [step(): got = lax.ppermute(send, axis, [(i, i ^ 1 << bit) for i in range(size)])]
    unnamed x292 -> x298, local copies, waits for them, and re-layouts: 47.6 us -> 54.4 us
  transfers between devices with their start and end apart: 28 -> 28, of which waited for: 2 -> 4; matrix products, arithmetic and copies ran while one was open for 36% -> 38% of each run, Pallas kernels for 47% -> 44%
where the time goes in v2:
time: 1050 us; the launch traced here: 1040 us
  Pallas kernels  462 us (44%)
  local copies, waits for them, and re-layouts  155 us (15%)
  matrix products  153 us (15%)
  other arithmetic  146 us (14%)
  waiting for transfers between devices  75.8 us (7%)
  between operations  32.9 us (3%)
  starting transfers between devices  20.2 us (2%)
    pallas_call x1, Pallas kernels, gather_rows(): pl.pallas_call(functools.partial(gather_kernel, ring, groups, parts, orde...  218 us
    pallas_call x1, Pallas kernels, reduce_rest(): pl.pallas_call(functools.partial(reduce_kernel, specs, partners, len(arra...  141 us
    ppermute x12, waiting for transfers between devices, step(): got = lax.ppermute(send, axis, [(i, i ^ 1 << bit) for i in range(size)])  74.6 us
    unnamed x298, local copies, waits for them, and re-layouts  54.4 us
    dot_general x5, matrix products, dot_nt(): lax.dot_general(a, b, (((1,), (1,)), ((), ())), preferred_element_type=f32)  52.1 us
    pallas_call x1, Pallas kernels, attend_back(): pl.pallas_call(functools.partial(attend_back_kernel, ring, len(after)), i...  43.6 us
    dot_general x6, matrix products, dot_tn(): lax.dot_general(a, b, (((0,), (0,)), ((), ())), preferred_element_type=f32)  40.6 us
    pallas_call x1, Pallas kernels, attend(): pl.pallas_call(functools.partial(attend_kernel, ring), in_specs=[smem] +...  40 us
  transfers between devices with their start and end apart: 28, of which 4 were waited for; matrix products, arithmetic and copies ran while one was open for 38% of the time, Pallas kernels for 44%

profile of v2, /device:TPU:0, one launch (start us, length us, event | category | flops | bytes accessed | tf_op | source)
XLA Modules:
  0.0 1045.0 jit_solution(6621657814244924467)
XLA Ops:
  20.7 217.9 %gather_rows.1 = (bf16[2,2,2,1,2,112,3072]{6,5,4,3,2,1,0:T(8,128)(2,1)}, bf16[2,2,2,2,2,56,1792]{6,5,4,3,2,1,0:T(8,128)(2,1)}) custom-call(bf16[1,1,1,1,1,112,3072]{6,5,4,3,2,1,0:T(8,128)(2,1)} %bitcast.333, bf16[1,1,1,2,1,56,896]{6,5,4,3,2,1,0:T(8,128)(2,1)} %maximum_bitcast_fusion.1.refs_1_), custom_call_target="tpu_custom_call" | custom-call | bytes 284426240 | tf_op jit(solution)/shard_map/gather_rows/pallas_call | solution.py:191
  263.4 4.5 select_bitcast_fusion.1
  274.5 13.9 %fusion.106 = (bf16[768,2944]{1,0:T(8,128)(2,1)}, f32[768,2944]{1,0:T(8,128)S(1)}) fusion(bf16[768,1792]{1,0:T(8,128)(2,1)S(1)} %multiply_convert_fusion.2, bf16[1792,3072]{1,0:T(8,128)(2,1)} %bitcast.358), kind=kOutput, calls=%fused_computation.317 | convolution fusion | flops 8105656320 | bytes 26869760 | tf_op jit(solution)/shard_map/dot_general | solution.py:881
  288.3 3.4 copy-done.42
  292.3 3.1 fusion.101
  296.9 2.6 copy.197
  314.0 40.0 %attend.1 = (bf16[8,768,128]{2,1,0:T(8,128)(2,1)S(1)}, f32[768,128]{1,0:T(8,128)S(1)}, bf16[8,160,128]{2,1,0:T(8,128)(2,1)S(1)}, bf16[16,896]{1,0:T(8,128)(2,1)S(1)}) custom-call(f32[8,8]{1,0:T(8,128)S(1)} %fusion.85.link_ref, bf16[768,128]{1,0:T(8,128)(2,1)S(1)} %get-tuple-element.101.q_ref, bf16[128,768]{1,0:T(8,128)(2,1)S(1)} %copy.198.kt_ref, ...), custom_call_target="tpu_custom_call" | custom-call | tf_op jit(solution)/shard_map/attend/pallas_call | solution.py:604
  359.1 3.4 copy.200
  362.5 3.4 copy.202
  367.8 5.1 add_convert_fusion.6
  372.9 3.3 pad_maximum_fusion.2
  376.2 5.4 fusion.19
  381.7 7.9 multiply_reduce_fusion.2
  393.7 9.8 fusion.107
  403.5 12.3 %multiply_convert_fusion = (bf16[768,2048]{1,0:T(8,128)(2,1)S(1)}, f32[768,2048]{1,0:T(8,128)}) fusion(f32[768,2048]{1,0:T(8,128)} %fusion.107, bf16[768,1792]{1,0:T(8,128)(2,1)} %copy-done.58, bf16[1792,2048]{1,0:T(8,128)(2,1)} %bitcast.366), kind=kOutput, calls=%fused_computation.15 | convolution fusion | flops 5646581760 | bytes 25821184 | tf_op jit(solution)/shard_map/dot_general | solution.py:63
  415.8 3.7 convolution_convert_fusion.4
  423.8 3.7 convolution_convert_fusion.5
  430.0 3.4 collective-permute-start.7
  433.4 52.1 %collective-permute-done.8 = bf16[2,2,2,1,128,896]{5,4,1,0,3,2:T(8,128)(2,1)} collective-permute-done((bf16[2,2,2,1,128,896]{5,4,1,0,3,2:T(8,128)(2,1)}, bf16[2,2,2,1,128,896]{5,4,1,0,3,2:T(8,128)(2,1)}, u32[]{:S(2)}, u32[]{:S(2)}) %collective-permute-start.8) | collective-permute-done | bytes 1835040 | tf_op jit(solution)/shard_map/ppermute | solution.py:721
  485.5 2.6 add_convert_fusion.7
  490.8 2.6 add_convert_fusion.8
  498.2 13.1 %fusion.7 = (bf16[768,2048]{1,0:T(8,128)(2,1)S(1)}, bf16[768,2048]{1,0:T(8,128)(2,1)S(1)}) fusion(f32[768,2048]{1,0:T(8,128)} %fusion.107, f32[768,2048]{1,0:T(8,128)} %get-tuple-element.159, bf16[768,1792]{1,0:T(8,128)(2,1)} %bitcast.332, bf16[2048,1792]{1,0:T(8,128)(2,1)} %all-gather.10.cloned.1.call-done), kind=kOutput, calls=%fused_computation.14 | convolution fusion | flops 5657591808 | bytes 28966912 | tf_op jit(solution)/shard_map/dot_general | solution.py:71
  511.4 6.6 convolution_convert_fusion.2
  524.8 9.3 convolution_convert_fusion.1
  534.5 3.3 copy-done.44
  553.0 7.6 fusion.12
  560.6 13.0 %add_convert_fusion = bf16[768,1792]{1,0:T(8,128)(2,1)} fusion(f32[768,1792]{1,0:T(8,128)} %fusion.12, bf16[1792,2048]{1,0:T(8,128)(2,1)S(1)} %bitcast.369, bf16[768,2048]{1,0:T(8,128)(2,1)} %copy-done.114, f32[768,2048]{1,0:T(8,128)} %fusion.107), kind=kOutput, calls=%fused_computation.22 | convolution fusion | flops 5650907136 | bytes 25034752 | tf_op jit(solution)/shard_map/dot_general | solution.py:71
  577.1 3.3 multiply_reduce_fusion.5
  580.4 11.2 %fusion.108 = f32[768,1792]{1,0:T(8,128)} fusion(bf16[768,2048]{1,0:T(8,128)(2,1)} %copy-done.113, bf16[2048,1792]{1,0:T(8,128)(2,1)} %all-gather.10.cloned.1.call-done), kind=kOutput, calls=%fused_computation.319 | convolution fusion | flops 5637144576 | bytes 15990784 | tf_op jit(solution)/shard_map/dot_general | solution.py:918
  593.6 11.8 %collective-permute-done.12 = bf16[2,2,1,2,112,2048]{5,4,1,0,3,2:T(8,128)(2,1)} collective-permute-done((bf16[2,2,1,2,112,2048]{5,4,1,0,3,2:T(8,128)(2,1)}, bf16[2,2,1,2,112,2048]{5,4,1,0,3,2:T(8,128)(2,1)}, u32[]{:S(2)}, u32[]{:S(2)}) %collective-permute-start.12) | collective-permute-done | bytes 3670048 | tf_op jit(solution)/shard_map/ppermute | solution.py:721
  607.3 4.1 multiply_reduce_fusion
  611.4 10.7 %collective-permute-done.13 = bf16[2,2,2,1,112,2048]{5,4,1,0,3,2:T(8,128)(2,1)} collective-permute-done((bf16[2,2,2,1,112,2048]{5,4,1,0,3,2:T(8,128)(2,1)}, bf16[2,2,2,1,112,2048]{5,4,1,0,3,2:T(8,128)(2,1)}, u32[]{:S(2)}, u32[]{:S(2)}) %collective-permute-start.13) | collective-permute-done | bytes 3670048 | tf_op jit(solution)/shard_map/ppermute | solution.py:721
  624.0 4.1 fusion.9
  628.1 4.1 add_add_fusion.6
  632.3 4.9 multiply_reduce_fusion.9
  637.2 2.5 copy.219
  639.7 2.8 copy.220
  642.5 3.1 pad.35.up_ref
  650.0 43.6 %attend_back.1 = (f32[768,128]{1,0:T(8,128)S(1)}, f32[768,128]{1,0:T(8,128)S(1)}, bf16[8,768,128]{2,1,0:T(8,128)(2,1)S(1)}, f32[8,896]{1,0:T(8,128)S(1)}) custom-call(f32[8,8]{1,0:T(8,128)S(1)} %fusion.85.link_ref, bf16[768,128]{1,0:T(8,128)(2,1)S(1)} %copy-done.3, bf16[768,128]{1,0:T(8,128)(2,1)S(1)} %copy-done.2, bf16[128,768]{1,0:T(8,128)(2,1)S(1)} %copy.221.qt_ref, ...), custom_call_target="tpu_custom_call" | custom-call | tf_op jit(solution)/shard_map/attend_back/pallas_call | solution.py:632
  698.7 5.8 convolution_convert_fusion.3
  710.1 4.1 fusion.39
  716.9 4.1 fusion.40
  729.4 3.5 fusion.53
  733.2 2.8 fusion.54
  736.0 14.2 %fusion = f32[768,1792]{1,0:T(8,128)} fusion(bf16[1792,3072]{1,0:T(8,128)(2,1)} %bitcast.359, bf16[768,2944]{1,0:T(8,128)(2,1)S(1)} %fusion.54, bf16[]{:T(256)} %bitcast.72, bf16[]{:T(256)} %bitcast.71, bf16[]{:T(256)} %bitcast.70, bf16[]{:T(256)} %bitcast.69), kind=kOutput, calls=%fused_computation.2 | convolution fusion | flops 8112439296 | bytes 20580352 | tf_op jit(solution)/shard_map/dot_general | solution.py:71
  750.2 11.5 %convolution_convert_fusion = bf16[1792,2944]{1,0:T(8,128)(2,1)} fusion(bf16[768,1792]{1,0:T(8,128)(2,1)S(1)} %copy-done.57, bf16[768,2944]{1,0:T(8,128)(2,1)S(1)} %fusion.54, bf16[]{:T(256)} %bitcast.72, bf16[]{:T(256)} %bitcast.71, bf16[]{:T(256)} %bitcast.70, bf16[]{:T(256)} %bitcast.69), kind=kOutput, calls=%fused_computation | convolution fusion | flops 8117714944 | bytes 17825800 | tf_op jit(solution)/shard_map/dot_general | solution.py:67
  763.7 3.6 constant_dynamic-slice_fusion
  767.3 3.5 dynamic-slice_add_fusion.1
  780.2 5.0 fusion.41.refs_0_
  785.2 5.0 fusion.42.refs_1_
  790.2 141.5 %reduce_rest.1 = (f32[112,1024]{1,0:T(8,128)}, f32[112,1024]{1,0:T(8,128)}, f32[112,1024]{1,0:T(8,128)}, f32[112,1024]{1,0:T(8,128)}, f32[112,512]{1,0:T(8,128)}...) custom-call(bf16[2,2,112,2048]{3,2,1,0:T(8,128)(2,1)} %fusion.41.ref, ...), custom_call_target="tpu_custom_call" | custom-call | tf_op jit(solution)/shard_map/reduce_rest/pallas_call | solution.py:308
  940.1 2.7 reshape_reshape.3
  942.8 2.6 copy.247
  945.4 2.5 reshape.543
  956.3 4.3 multiply_reduce_fusion.10
  960.8 4.9 multiply_reduce_fusion.4
  967.6 5.7 fusion.23
  974.9 2.7 copy.226
  977.6 2.5 copy.227
  987.5 19.3 %sum_everywhere.1 = f32[8,1792]{1,0:T(8,128)} custom-call(f32[8,1792]{1,0:T(8,128)} %maximum_maximum_fusion.in_ref), custom_call_target="tpu_custom_call" | custom-call | tf_op jit(solution)/shard_map/sum_everywhere/pallas_call | solution.py:353
  1016.6 3.0 fusion.43
  1019.7 2.8 mul.740
  1029.4 2.6 multiply_subtract_fusion.1
  1033.4 3.4 multiply_subtract_fusion
  (523 shorter events, 185.3 us)
Async XLA Ops:
  7.2 297.0 %all-gather.8.cloned.1.call-start = ((), (), s32[]{:S(2)}) async-start(), calls=%async_computation.1 | async-start | bytes 7798784 | tf_op jit(solution)/shard_map/all_gather | solution.py:811
  11.7 1.6 collective-permute-start.2
  14.2 389.3 %all-gather.6.cloned.1.call-start = ((), (), s32[]{:S(2)}) async-start(), calls=%async_computation | async-start | bytes 7798784 | tf_op jit(solution)/shard_map/all_gather | solution.py:811
  16.1 1.6 collective-permute-start.3
  17.0 2.7 collective-permute-start.1
  17.2 2.4 collective-permute-start.5
  19.7 222.1 %copy-start.67 = (bf16[1,384,1792]{2,1,0:T(8,128)(2,1)S(1)}, bf16[1,384,1792]{2,1,0:T(8,128)(2,1)}, u32[]{:S(2)}) copy-start(bf16[1,384,1792]{2,1,0:T(8,128)(2,1)} %param.27) | copy-start | bytes 4128772
  241.3 256.9 %all-gather.10.cloned.1.call-start = ((), (), s32[]{:S(2)}) async-start(), calls=%async_computation.2 | async-start | bytes 7798784 | tf_op jit(solution)/shard_map/all_gather | solution.py:811
  244.4 19.0 %collective-permute-start.6 = (bf16[384,1792]{1,0:T(8,128)(2,1)}, bf16[384,1792]{1,0:T(8,128)(2,1)}, u32[]{:S(2)}, u32[]{:S(2)}) collective-permute-start(bf16[384,1792]{1,0:T(8,128)(2,1)} %copy.210), channel_id=1, source_target_pairs={{0,2},{2,0},{1,3},{3,1},{4,6},{6,4},{5,7},{7,5},{8,10},{10,8},{9,1... | collective-permute-start | bytes 4128776 | tf_op jit(solution)/shard_map/ppermute | solution.py:677
  247.7 9.1 copy-start.47
  247.7 15.7 %collective-permute-start = (bf16[384,1792]{1,0:T(8,128)(2,1)S(1)}, bf16[384,1792]{1,0:T(8,128)(2,1)}, u32[]{:S(2)}, u32[]{:S(2)}) collective-permute-start(bf16[384,1792]{1,0:T(8,128)(2,1)S(1)} %copy.189), channel_id=1, source_target_pairs={{0,2},{2,0},{1,3},{3,1},{4,6},{6,4},{5,7},{7,5},{8,10},{10,8},{9,1... | collective-permute-start | bytes 4128776 | tf_op jit(solution)/shard_map/ppermute | solution.py:677
  251.7 115.4 %copy-start.88 = (f32[768]{0:T(1024)}, f32[768]{0:T(1024)S(1)}, u32[]{:S(2)}) copy-start(f32[768]{0:T(1024)S(1)} %get-tuple-element.150) | copy-start | bytes 9220
  263.4 8.2 copy-start.82
  274.5 13.9 %copy-start.56 = (bf16[768,1792]{1,0:T(8,128)(2,1)}, bf16[768,1792]{1,0:T(8,128)(2,1)S(1)}, u32[]{:S(2)}) copy-start(bf16[768,1792]{1,0:T(8,128)(2,1)S(1)} %multiply_convert_fusion.2) | copy-start | bytes 8257540
  301.0 8.1 copy-start.19
  302.8 51.2 %copy-start = (bf16[8,768,128]{2,1,0:T(8,128)(2,1)}, bf16[8,768,128]{2,1,0:T(8,128)(2,1)S(1)}, u32[]{:S(2)}) copy-start(bf16[8,768,128]{2,1,0:T(8,128)(2,1)S(1)} %pad_select_fusion.v_ref) | copy-start | bytes 4718596
  372.8 8.8 collective-permute-start.4
  372.9 8.8 slice-start
  381.6 7.9 copy-start.81
  403.5 12.3 %copy-start.36 = (bf16[2,384,1792]{2,1,0:T(8,128)(2,1)S(1)}, bf16[2,384,1792]{2,1,0:T(8,128)(2,1)}, u32[]{:S(2)}) copy-start(bf16[2,384,1792]{2,1,0:T(8,128)(2,1)} %pad_maximum_fusion.2) | copy-start | bytes 8257540
  415.8 8.0 copy-start.113
  422.0 63.5 %collective-permute-start.8 = (bf16[2,2,2,1,128,896]{5,4,1,0,3,2:T(8,128)(2,1)}, bf16[2,2,2,1,128,896]{5,4,1,0,3,2:T(8,128)(2,1)}, u32[]{:S(2)}, u32[]{:S(2)}) collective-permute-start(bf16[2,2,2,1,128,896]{5,4,1,0,3,2:T(8,128)(2,1)} %copy.257), channel_id=1, source_target_pairs={{0,1},{1,0},{2,3},{3,2},{4,5},{5,4},{6,7},{7,6},{8,9},{9,8},{10,11... | collective-permute-start | bytes 5505032 | tf_op jit(solution)/shard_map/ppermute | solution.py:721
  430.0 60.8 %collective-permute-start.7 = (bf16[2,2,1,2,128,896]{5,4,1,0,3,2:T(8,128)(2,1)}, bf16[2,2,1,2,128,896]{5,4,1,0,3,2:T(8,128)(2,1)}, u32[]{:S(2)}, u32[]{:S(2)}) collective-permute-start(bf16[2,2,1,2,128,896]{5,4,1,0,3,2:T(8,128)(2,1)} %copy.255), channel_id=1, source_target_pairs={{0,4},{4,0},{8,12},{12,8},{16,20},{20,16},{24,28},{28,24},{1,5},{5... | collective-permute-start | bytes 5505032 | tf_op jit(solution)/shard_map/ppermute | solution.py:721
  433.4 63.1 %copy-start.31 = (bf16[1,384,1792]{2,1,0:T(8,128)(2,1)S(1)}, bf16[1,384,1792]{2,1,0:T(8,128)(2,1)}, u32[]{:S(2)}) copy-start(bf16[1,384,1792]{2,1,0:T(8,128)(2,1)} %get-tuple-element.115) | copy-start | bytes 4128772
  489.3 55.2 %collective-permute-start.10 = (bf16[2,2,1,1,128,896]{5,4,1,0,3,2:T(8,128)(2,1)}, bf16[2,2,1,1,128,896]{5,4,1,0,3,2:T(8,128)(2,1)}, u32[]{:S(2)}, u32[]{:S(2)}) collective-permute-start(bf16[2,2,1,1,128,896]{5,4,1,0,3,2:T(8,128)(2,1)} %add_convert_fusion.7), channel_id=1, source_target_pairs={{0,4},{4,0},{8,12},{12,8},{16,20},{20,16},{24,28},{28,24},{1,5},{5... | collective-permute-start | bytes 2752520 | tf_op jit(solution)/shard_map/ppermute | solution.py:721
  494.6 54.2 %collective-permute-start.9 = (bf16[2,2,1,1,128,896]{5,4,1,0,3,2:T(8,128)(2,1)}, bf16[2,2,1,1,128,896]{5,4,1,0,3,2:T(8,128)(2,1)}, u32[]{:S(2)}, u32[]{:S(2)}) collective-permute-start(bf16[2,2,1,1,128,896]{5,4,1,0,3,2:T(8,128)(2,1)} %add_convert_fusion.8), channel_id=1, source_target_pairs={{0,1},{1,0},{2,3},{3,2},{4,5},{5,4},{6,7},{7,6},{8,9},{9,8},{10,11... | collective-permute-start | bytes 2752520 | tf_op jit(solution)/shard_map/ppermute | solution.py:721
  498.2 13.2 %copy-start.59 = (bf16[768,1792]{1,0:T(8,128)(2,1)S(1)}, bf16[768,1792]{1,0:T(8,128)(2,1)}, u32[]{:S(2)}) copy-start(bf16[768,1792]{1,0:T(8,128)(2,1)} %copy-done.58) | copy-start | bytes 8257540
  511.4 13.4 %copy-start.114 = (bf16[768,2048]{1,0:T(8,128)(2,1)}, bf16[768,2048]{1,0:T(8,128)(2,1)S(1)}, u32[]{:S(2)}) copy-start(bf16[768,2048]{1,0:T(8,128)(2,1)S(1)} %get-tuple-element.161) | copy-start | bytes 9437188
  524.4 80.9 %collective-permute-start.12 = (bf16[2,2,1,2,112,2048]{5,4,1,0,3,2:T(8,128)(2,1)}, bf16[2,2,1,2,112,2048]{5,4,1,0,3,2:T(8,128)(2,1)}, u32[]{:S(2)}, u32[]{:S(2)}) collective-permute-start(bf16[2,2,1,2,112,2048]{5,4,1,0,3,2:T(8,128)(2,1)} %copy.258), channel_id=1, source_target_pairs={{0,4},{4,0},{8,12},{12,8},{16,20},{20,16},{24,28},{28,24},{1,5},{5... | collective-permute-start | bytes 11010056 | tf_op jit(solution)/shard_map/ppermute | solution.py:721
  534.1 18.9 %slice-start.10 = ((s8[7340032]{0:T(1024)(128)(4,1)}), s8[4194304]{0:T(1024)(128)(4,1)S(1)}, s32[]{:S(2)}) async-start(s8[7340032]{0:T(1024)(128)(4,1)} %bitcast.363), calls=%async_computation.13 | async-start | bytes 8388608
  537.8 15.2 %slice-start.11 = ((s8[7340032]{0:T(1024)(128)(4,1)}), s8[3145728]{0:T(1024)(128)(4,1)S(1)}, s32[]{:S(2)}) async-start(s8[7340032]{0:T(1024)(128)(4,1)} %bitcast.363), calls=%async_computation.14 | async-start | bytes 6291456
  540.1 12.8 %copy-start.116 = (bf16[768,2048]{1,0:T(8,128)(2,1)S(1)}, bf16[768,2048]{1,0:T(8,128)(2,1)}, u32[]{:S(2)}) copy-start(bf16[768,2048]{1,0:T(8,128)(2,1)} %copy-done.115) | copy-start | bytes 9437188
  541.4 80.7 %collective-permute-start.13 = (bf16[2,2,2,1,112,2048]{5,4,1,0,3,2:T(8,128)(2,1)}, bf16[2,2,2,1,112,2048]{5,4,1,0,3,2:T(8,128)(2,1)}, u32[]{:S(2)}, u32[]{:S(2)}) collective-permute-start(bf16[2,2,2,1,112,2048]{5,4,1,0,3,2:T(8,128)(2,1)} %copy.259), channel_id=1, source_target_pairs={{0,1},{1,0},{2,3},{3,2},{4,5},{5,4},{6,7},{7,6},{8,9},{9,8},{10,11... | collective-permute-start | bytes 11010056 | tf_op jit(solution)/shard_map/ppermute | solution.py:721
  544.5 16.1 %slice-start.12 = ((s8[7340032]{0:T(1024)(128)(4,1)}), s8[4194304]{0:T(1024)(128)(4,1)S(1)}, s32[]{:S(2)}) async-start(s8[7340032]{0:T(1024)(128)(4,1)} %bitcast.367), calls=%async_computation.15 | async-start | bytes 8388608
  553.0 7.6 slice-start.13
  560.6 13.0 %copy-start.95 = (f32[768]{0:T(1024)S(1)}, f32[768]{0:T(1024)}, u32[]{:S(2)}) copy-start(f32[768]{0:T(1024)} %copy-done.94) | copy-start | bytes 9220
  560.6 13.0 %copy-start.93 = (f32[768]{0:T(1024)S(1)}, f32[768]{0:T(1024)}, u32[]{:S(2)}) copy-start(f32[768]{0:T(1024)} %copy-done.92) | copy-start | bytes 9220
  573.5 33.7 %collective-permute-start.11 = (bf16[768,1792]{1,0:T(8,128)(2,1)}, bf16[768,1792]{1,0:T(8,128)(2,1)}, u32[]{:S(2)}, u32[]{:S(2)}) collective-permute-start(bf16[768,1792]{1,0:T(8,128)(2,1)} %add_convert_fusion), channel_id=1, source_target_pairs={{0,2},{2,0},{1,3},{3,1},{4,6},{6,4},{5,7},{7,5},{8,10},{10,8},{9,1... | collective-permute-start | bytes 8257544 | tf_op jit(solution)/shard_map/ppermute | solution.py:677
  577.1 30.1 %slice-start.4 = ((s8[5505024]{0:T(1024)(128)(4,1)}), s8[4194304]{0:T(1024)(128)(4,1)S(1)}, s32[]{:S(2)}) async-start(s8[5505024]{0:T(1024)(128)(4,1)} %bitcast.284), calls=%async_computation.7 | async-start | bytes 8388608
  580.4 26.9 %slice-start.5 = ((s8[5505024]{0:T(1024)(128)(4,1)}), s8[1310720]{0:T(1024)(128)(4,1)S(1)}, s32[]{:S(2)}) async-start(s8[5505024]{0:T(1024)(128)(4,1)} %bitcast.284), calls=%async_computation.8 | async-start | bytes 2621440
  591.6 103.2 %collective-permute-start.15 = (bf16[2,1,1,1,128,896]{5,4,1,0,3,2:T(8,128)(2,1)}, bf16[2,1,1,1,128,896]{5,4,1,0,3,2:T(8,128)(2,1)}, u32[]{:S(2)}, u32[]{:S(2)}) collective-permute-start(bf16[2,1,1,1,128,896]{5,4,1,0,3,2:T(8,128)(2,1)} %fusion.63), channel_id=1, source_target_pairs={{0,8},{4,12},{8,0},{12,4},{16,24},{20,28},{24,16},{28,20},{1,9},{5... | collective-permute-start | bytes 1376264 | tf_op jit(solution)/shard_map/ppermute | solution.py:721
  593.1 111.4 %collective-permute-start.16 = (bf16[2,1,1,1,128,896]{5,4,1,0,3,2:T(8,128)(2,1)}, bf16[2,1,1,1,128,896]{5,4,1,0,3,2:T(8,128)(2,1)}, u32[]{:S(2)}, u32[]{:S(2)}) collective-permute-start(bf16[2,1,1,1,128,896]{5,4,1,0,3,2:T(8,128)(2,1)} %fusion.64), channel_id=1, source_target_pairs={{0,8},{4,12},{8,0},{12,4},{16,24},{20,28},{24,16},{28,20},{1,9},{5... | collective-permute-start | bytes 1376264 | tf_op jit(solution)/shard_map/ppermute | solution.py:721
  607.2 16.7 %copy-start.37 = (bf16[2,384,1792]{2,1,0:T(8,128)(2,1)S(1)}, bf16[2,384,1792]{2,1,0:T(8,128)(2,1)}, u32[]{:S(2)}) copy-start(bf16[2,384,1792]{2,1,0:T(8,128)(2,1)} %pad_maximum_fusion.2) | copy-start | bytes 8257540
  607.3 20.8 %slice-start.8 = ((s8[6422528]{0:T(1024)(128)(4,1)}), s8[4194304]{0:T(1024)(128)(4,1)S(1)}, s32[]{:S(2)}) async-start(s8[6422528]{0:T(1024)(128)(4,1)} %bitcast.341), calls=%async_computation.11 | async-start | bytes 8388608
  646.3 52.4 %slice-start.6 = ((s8[5505024]{0:T(1024)(128)(4,1)}), s8[1310720]{0:T(1024)(128)(4,1)S(1)}, s32[]{:S(2)}) async-start(s8[5505024]{0:T(1024)(128)(4,1)} %bitcast.288), calls=%async_computation.9 | async-start | bytes 2621440
  650.0 48.8 %slice-start.7 = ((s8[5505024]{0:T(1024)(128)(4,1)}), s8[4194304]{0:T(1024)(128)(4,1)S(1)}, s32[]{:S(2)}) async-start(s8[5505024]{0:T(1024)(128)(4,1)} %bitcast.288), calls=%async_computation.10 | async-start | bytes 8388608
  698.1 72.7 %collective-permute-start.22 = (bf16[1,1,1,1,128,896]{5,4,1,0,3,2:T(8,128)(2,1)}, bf16[1,1,1,1,128,896]{5,4,1,0,3,2:T(8,128)(2,1)}, u32[]{:S(2)}, u32[]{:S(2)}) collective-permute-start(bf16[1,1,1,1,128,896]{5,4,1,0,3,2:T(8,128)(2,1)} %fusion.66), channel_id=1, source_target_pairs={{0,16},{4,20},{8,24},{12,28},{16,0},{20,4},{24,8},{28,12},{1,17},{... | collective-permute-start | bytes 688136 | tf_op jit(solution)/shard_map/ppermute | solution.py:721
  707.8 65.0 %collective-permute-start.23 = (bf16[1,1,1,1,128,896]{5,4,1,0,3,2:T(8,128)(2,1)}, bf16[1,1,1,1,128,896]{5,4,1,0,3,2:T(8,128)(2,1)S(1)}, u32[]{:S(2)}, u32[]{:S(2)}) collective-permute-start(bf16[1,1,1,1,128,896]{5,4,1,0,3,2:T(8,128)(2,1)} %fusion.67), channel_id=1, source_target_pairs={{0,16},{4,20},{8,24},{12,28},{16,0},{20,4},{24,8},{28,12},{1,17},{... | collective-permute-start | bytes 688136 | tf_op jit(solution)/shard_map/ppermute | solution.py:721
  715.4 64.8 %collective-permute-start.18 = (bf16[2,2,1,1,112,2048]{5,4,1,0,3,2:T(8,128)(2,1)}, bf16[2,2,1,1,112,2048]{5,4,1,0,3,2:T(8,128)(2,1)}, u32[]{:S(2)}, u32[]{:S(2)}) collective-permute-start(bf16[2,2,1,1,112,2048]{5,4,1,0,3,2:T(8,128)(2,1)} %fusion.39), channel_id=1, source_target_pairs={{0,1},{1,0},{2,3},{3,2},{4,5},{5,4},{6,7},{7,6},{8,9},{9,8},{10,11... | collective-permute-start | bytes 5505032 | tf_op jit(solution)/shard_map/ppermute | solution.py:721
  722.1 63.1 %collective-permute-start.19 = (bf16[2,2,1,1,112,2048]{5,4,1,0,3,2:T(8,128)(2,1)}, bf16[2,2,1,1,112,2048]{5,4,1,0,3,2:T(8,128)(2,1)}, u32[]{:S(2)}, u32[]{:S(2)}) collective-permute-start(bf16[2,2,1,1,112,2048]{5,4,1,0,3,2:T(8,128)(2,1)} %fusion.40), channel_id=1, source_target_pairs={{0,4},{4,0},{8,12},{12,8},{16,20},{20,16},{24,28},{28,24},{1,5},{5... | collective-permute-start | bytes 5505032 | tf_op jit(solution)/shard_map/ppermute | solution.py:721
  736.0 14.2 %copy-start.57 = (bf16[768,1792]{1,0:T(8,128)(2,1)S(1)}, bf16[768,1792]{1,0:T(8,128)(2,1)}, u32[]{:S(2)}) copy-start(bf16[768,1792]{1,0:T(8,128)(2,1)} %copy-done.56) | copy-start | bytes 8257540
  750.2 11.5 %copy-start.55 = (bf16[896,1792]{1,0:T(8,128)(2,1)S(1)}, bf16[896,1792]{1,0:T(8,128)(2,1)}, u32[]{:S(2)}) copy-start(bf16[896,1792]{1,0:T(8,128)(2,1)} %convolution_convert_fusion.3) | copy-start | bytes 9633796
  763.0 13.1 %collective-permute-start.20 = (bf16[4,112,1792]{2,1,0:T(8,128)(2,1)}, bf16[4,112,1792]{2,1,0:T(8,128)(2,1)S(1)}, u32[]{:S(2)}, u32[]{:S(2)}) collective-permute-start(bf16[4,112,1792]{2,1,0:T(8,128)(2,1)} %dynamic-slice_bitcast_fusion), channel_id=1, source_target_pairs={{0,2},{2,0},{1,3},{3,1},{4,6},{6,4},{5,7},{7,5},{8,10},{10,8},{9,1... | collective-permute-start | bytes 4816904 | tf_op jit(solution)/shard_map/ppermute | solution.py:677
  770.8 190.0 %collective-permute-start.14 = (f32[384,1792]{1,0:T(8,128)}, f32[384,1792]{1,0:T(8,128)}, u32[]{:S(2)}, u32[]{:S(2)}) collective-permute-start(f32[384,1792]{1,0:T(8,128)} %dynamic-slice_add_fusion.1), channel_id=1, source_target_pairs={{0,2},{2,0},{1,3},{3,1},{4,6},{6,4},{5,7},{7,5},{8,10},{10,8},{9,1... | collective-permute-start | bytes 8257544 | tf_op jit(solution)/shard_map/ppermute | solution.py:677
  772.8 183.5 %collective-permute-start.17 = (f32[384,1792]{1,0:T(8,128)}, f32[384,1792]{1,0:T(8,128)}, u32[]{:S(2)}, u32[]{:S(2)}) collective-permute-start(f32[384,1792]{1,0:T(8,128)} %constant_dynamic-slice_fusion), channel_id=1, source_target_pairs={{0,2},{2,0},{1,3},{3,1},{4,6},{6,4},{5,7},{7,5},{8,10},{10,8},{9,1... | collective-permute-start | bytes 8257544 | tf_op jit(solution)/shard_map/ppermute | solution.py:677
  931.7 6.8 copy-start.78
  931.7 6.9 copy-start.77
  938.5 15.3 %collective-permute-start.21 = (f32[56,2944]{1,0:T(8,128)}, f32[56,2944]{1,0:T(8,128)}, u32[]{:S(2)}, u32[]{:S(2)}) collective-permute-start(f32[56,2944]{1,0:T(8,128)} %dynamic-slice_bitcast_fusion.2), channel_id=1, source_target_pairs={{0,2},{2,0},{1,3},{3,1},{4,6},{6,4},{5,7},{7,5},{8,10},{10,8},{9,1... | collective-permute-start | bytes 1978376 | tf_op jit(solution)/shard_map/ppermute | solution.py:677
  938.7 10.7 %copy-start.39 = (f32[112,4096]{1,0:T(8,128)}, f32[112,4096]{1,0:T(8,128)S(1)}, u32[]{:S(2)}) copy-start(f32[112,4096]{1,0:T(8,128)S(1)} %constant_dynamic-update-slice_fusion.17) | copy-start | bytes 5505028
  947.9 64.9 %collective-permute-start.24 = (f32[56,4096]{1,0:T(8,128)}, f32[56,4096]{1,0:T(8,128)}, u32[]{:S(2)}, u32[]{:S(2)}) collective-permute-start(f32[56,4096]{1,0:T(8,128)} %dynamic-slice_bitcast_fusion.1), channel_id=1, source_target_pairs={{0,2},{2,0},{1,3},{3,1},{4,6},{6,4},{5,7},{7,5},{8,10},{10,8},{9,1... | collective-permute-start | bytes 2752520 | tf_op jit(solution)/shard_map/ppermute | solution.py:677
  956.3 11.3 %slice-start.2 = ((s8[5505024]{0:T(1024)(128)(4,1)}), s8[1310720]{0:T(1024)(128)(4,1)S(1)}, s32[]{:S(2)}) async-start(s8[5505024]{0:T(1024)(128)(4,1)} %bitcast.281), calls=%async_computation.5 | async-start | bytes 2621440
  960.7 6.8 slice-start.3
  960.7 6.8 copy-start.84
  960.7 6.8 copy-start.105
  (95 other events, 295.8 us)
Sparse Core Ops, SparseCore 0:
  14.3 151.0 all-gather.7
  241.4 115.5 all-gather.5
  360.5 120.0 all-gather.9

commit v3 on v2

--- a/solution.py
+++ b/solution.py
@@ -962,8 +962,8 @@
     mix_grad = dot_nt(branch_grad, output_half).astype(bf16)
     ext_grad, taps_grad, gate_grad = gate_back(mix_grad.astype(f32))
     head_grad = mix_grad
-    for got in updown_chain.got:
-        head_grad = tie(head_grad, got)
+    for one in updown_chain.step():
+        head_grad = tie(head_grad, one)
     query_g, key_g, value_g, after = attend_back(
         link, query, key_vecs, query.T, key_t, values, per_head(head_grad), att, den, carry, allow, on[:, None],
         on[None, :], fresh[:, None], ext_grad[:8], tables, ring, [],

time: 1050 us -> 1070 us (1.019)
    ppermute x12 -> x14, waiting for transfers between devices: 74.6 us -> 77.5 us  [step(): got = lax.ppermute(send, axis, [(i, i ^ 1 << bit) for i in range(size)])]
    unnamed x298 -> x318, local copies, waits for them, and re-layouts: 54.4 us -> 56.4 us
  transfers between devices with their start and end apart: 28 -> 30, of which waited for: 4 -> 4; matrix products, arithmetic and copies ran while one was open for 38% -> 36% of each run, Pallas kernels for 44% -> 42%
where the time goes in v3:
time: 1070 us; the launch traced here: 1060 us
  Pallas kernels  462 us (43%)
  local copies, waits for them, and re-layouts  161 us (15%)
  matrix products  157 us (15%)
  other arithmetic  150 us (14%)
  waiting for transfers between devices  78.6 us (7%)
  between operations  32.9 us (3%)
  starting transfers between devices  22.3 us (2%)
    pallas_call x1, Pallas kernels, gather_rows(): pl.pallas_call(functools.partial(gather_kernel, ring, groups, parts, orde...  218 us
    pallas_call x1, Pallas kernels, reduce_rest(): pl.pallas_call(functools.partial(reduce_kernel, specs, partners, len(arra...  143 us
    ppermute x14, waiting for transfers between devices, step(): got = lax.ppermute(send, axis, [(i, i ^ 1 << bit) for i in range(size)])  77.5 us
    unnamed x318, local copies, waits for them, and re-layouts  56.4 us
    dot_general x5, matrix products, dot_nt(): lax.dot_general(a, b, (((1,), (1,)), ((), ())), preferred_element_type=f32)  51.8 us
    dot_general x6, matrix products, dot_tn(): lax.dot_general(a, b, (((0,), (0,)), ((), ())), preferred_element_type=f32)  45.2 us
    pallas_call x1, Pallas kernels, attend_back(): pl.pallas_call(functools.partial(attend_back_kernel, ring, len(after)), i...  42.8 us
    pallas_call x1, Pallas kernels, attend(): pl.pallas_call(functools.partial(attend_kernel, ring), in_specs=[smem] +...  40.7 us
  transfers between devices with their start and end apart: 30, of which 4 were waited for; matrix products, arithmetic and copies ran while one was open for 36% of the time, Pallas kernels for 42%

profile of v3, /device:TPU:0, one launch (start us, length us, event | category | flops | bytes accessed | tf_op | source)
XLA Modules:
  0.0 1063.0 jit_solution(16318263269380791968)
XLA Ops:
  20.7 217.9 %gather_rows.1 = (bf16[2,2,2,1,2,112,3072]{6,5,4,3,2,1,0:T(8,128)(2,1)}, bf16[2,2,2,2,2,56,1792]{6,5,4,3,2,1,0:T(8,128)(2,1)}) custom-call(bf16[1,1,1,1,1,112,3072]{6,5,4,3,2,1,0:T(8,128)(2,1)} %bitcast.333, bf16[1,1,1,2,1,56,896]{6,5,4,3,2,1,0:T(8,128)(2,1)} %maximum_bitcast_fusion.1.refs_1_), custom_call_target="tpu_custom_call" | custom-call | bytes 284426240 | tf_op jit(solution)/shard_map/gather_rows/pallas_call | solution.py:191
  263.4 4.6 select_bitcast_fusion.1
  274.5 13.9 %fusion.106 = (bf16[768,2944]{1,0:T(8,128)(2,1)}, f32[768,2944]{1,0:T(8,128)S(1)}) fusion(bf16[768,1792]{1,0:T(8,128)(2,1)S(1)} %multiply_convert_fusion.2, bf16[1792,3072]{1,0:T(8,128)(2,1)} %bitcast.358), kind=kOutput, calls=%fused_computation.323 | convolution fusion | flops 8105656320 | bytes 26869760 | tf_op jit(solution)/shard_map/dot_general | solution.py:881
  288.4 3.5 copy-done.50
  292.4 3.1 fusion.101
  297.0 2.6 copy.201
  314.1 40.7 %attend.1 = (bf16[8,768,128]{2,1,0:T(8,128)(2,1)S(1)}, f32[768,128]{1,0:T(8,128)S(1)}, bf16[8,160,128]{2,1,0:T(8,128)(2,1)S(1)}, bf16[16,896]{1,0:T(8,128)(2,1)S(1)}) custom-call(f32[8,8]{1,0:T(8,128)S(1)} %fusion.85.link_ref, bf16[768,128]{1,0:T(8,128)(2,1)S(1)} %get-tuple-element.101.q_ref, bf16[128,768]{1,0:T(8,128)(2,1)S(1)} %copy.202.kt_ref, ...), custom_call_target="tpu_custom_call" | custom-call | tf_op jit(solution)/shard_map/attend/pallas_call | solution.py:604
  359.9 3.4 copy.204
  363.3 3.4 copy.206
  368.7 5.0 add_convert_fusion.4
  373.7 3.3 pad_maximum_fusion.2
  377.1 5.5 fusion.19
  382.6 7.9 multiply_reduce_fusion.2
  394.5 9.8 fusion.107
  404.3 12.2 %multiply_convert_fusion = (bf16[768,2048]{1,0:T(8,128)(2,1)S(1)}, f32[768,2048]{1,0:T(8,128)}) fusion(f32[768,2048]{1,0:T(8,128)} %fusion.107, bf16[768,1792]{1,0:T(8,128)(2,1)} %copy-done.65, bf16[1792,2048]{1,0:T(8,128)(2,1)} %bitcast.366), kind=kOutput, calls=%fused_computation.15 | convolution fusion | flops 5646581760 | bytes 25821184 | tf_op jit(solution)/shard_map/dot_general | solution.py:63
  416.5 3.7 convolution_convert_fusion.4
  423.6 3.7 convolution_convert_fusion.5
  429.8 3.4 collective-permute-start.7
  434.7 2.6 multiply_reduce_fusion.12
  437.3 48.2 %collective-permute-done.8 = bf16[2,2,2,1,128,896]{5,4,0,3,2,1:T(8,128)(2,1)} collective-permute-done((bf16[2,2,2,1,128,896]{5,4,0,3,2,1:T(8,128)(2,1)}, bf16[2,2,2,1,128,896]{5,4,0,3,2,1:T(8,128)(2,1)}, u32[]{:S(2)}, u32[]{:S(2)}) %collective-permute-start.8) | collective-permute-done | bytes 1835040 | tf_op jit(solution)/shard_map/ppermute | solution.py:721
  485.5 2.6 add_convert_fusion.9
  490.8 2.6 add_convert_fusion.10
  498.3 13.2 %fusion.7 = (bf16[768,2048]{1,0:T(8,128)(2,1)S(1)}, bf16[768,2048]{1,0:T(8,128)(2,1)S(1)}) fusion(f32[768,2048]{1,0:T(8,128)} %fusion.107, f32[768,2048]{1,0:T(8,128)} %get-tuple-element.159, bf16[768,1792]{1,0:T(8,128)(2,1)} %bitcast.332, bf16[2048,1792]{1,0:T(8,128)(2,1)} %all-gather.10.cloned.1.call-done), kind=kOutput, calls=%fused_computation.14 | convolution fusion | flops 5657591808 | bytes 28966912 | tf_op jit(solution)/shard_map/dot_general | solution.py:71
  511.6 6.6 convolution_convert_fusion.2
  524.9 9.3 convolution_convert_fusion.1
  534.6 3.3 copy-done.52
  550.1 7.6 fusion.12
  557.8 13.0 %add_convert_fusion = bf16[768,1792]{1,0:T(8,128)(2,1)} fusion(f32[768,1792]{1,0:T(8,128)} %fusion.12, bf16[1792,2048]{1,0:T(8,128)(2,1)S(1)} %bitcast.369, bf16[768,2048]{1,0:T(8,128)(2,1)} %copy-done.122, f32[768,2048]{1,0:T(8,128)} %fusion.107), kind=kOutput, calls=%fused_computation.22 | convolution fusion | flops 5650907136 | bytes 25034752 | tf_op jit(solution)/shard_map/dot_general | solution.py:71
  571.5 3.3 multiply_reduce_fusion.5
  574.8 11.2 %fusion.108 = f32[768,1792]{1,0:T(8,128)} fusion(bf16[768,2048]{1,0:T(8,128)(2,1)} %copy-done.121, bf16[2048,1792]{1,0:T(8,128)(2,1)} %all-gather.10.cloned.1.call-done), kind=kOutput, calls=%fused_computation.325 | convolution fusion | flops 5637144576 | bytes 15990784 | tf_op jit(solution)/shard_map/dot_general | solution.py:918
  588.1 17.4 %collective-permute-done.12 = bf16[2,2,1,2,112,2048]{5,4,0,3,2,1:T(8,128)(2,1)} collective-permute-done((bf16[2,2,1,2,112,2048]{5,4,0,3,2,1:T(8,128)(2,1)}, bf16[2,2,1,2,112,2048]{5,4,0,3,2,1:T(8,128)(2,1)}, u32[]{:S(2)}, u32[]{:S(2)}) %collective-permute-start.12) | collective-permute-done | bytes 3670048 | tf_op jit(solution)/shard_map/ppermute | solution.py:721
  605.5 4.1 add_convert_fusion.2
  612.2 11.9 %collective-permute-done.13 = bf16[2,2,2,1,112,2048]{5,4,0,3,2,1:T(8,128)(2,1)} collective-permute-done((bf16[2,2,2,1,112,2048]{5,4,0,3,2,1:T(8,128)(2,1)}, bf16[2,2,2,1,112,2048]{5,4,0,3,2,1:T(8,128)(2,1)}, u32[]{:S(2)}, u32[]{:S(2)}) %collective-permute-start.13) | collective-permute-done | bytes 3670048 | tf_op jit(solution)/shard_map/ppermute | solution.py:721
  624.1 4.1 add_convert_fusion.1
  631.8 4.1 multiply_reduce_fusion
  636.6 4.1 fusion.9
  640.8 4.1 add_add_fusion.6
  644.9 4.9 multiply_reduce_fusion.9
  655.0 3.1 pad.35.up_ref
  662.9 42.8 %attend_back.1 = (f32[768,128]{1,0:T(8,128)S(1)}, f32[768,128]{1,0:T(8,128)S(1)}, bf16[8,768,128]{2,1,0:T(8,128)(2,1)S(1)}, f32[8,896]{1,0:T(8,128)S(1)}) custom-call(f32[8,8]{1,0:T(8,128)S(1)} %fusion.85.link_ref, bf16[768,128]{1,0:T(8,128)(2,1)S(1)} %copy-done.5, bf16[768,128]{1,0:T(8,128)(2,1)S(1)} %copy-done.4, bf16[128,768]{1,0:T(8,128)(2,1)S(1)} %copy.227.qt_ref, ...), custom_call_target="tpu_custom_call" | custom-call | tf_op jit(solution)/shard_map/attend_back/pallas_call | solution.py:632
  709.6 5.8 convolution_convert_fusion.3
  720.4 2.7 dynamic-slice_bitcast_fusion
  725.7 2.6 copy.234
  731.9 3.7 fusion.49
  735.9 2.8 fusion.50
  751.5 3.3 fusion.57
  756.6 3.2 fusion.58
  763.7 13.9 %fusion = f32[768,1792]{1,0:T(8,128)S(1)} fusion(bf16[1792,3072]{1,0:T(8,128)(2,1)} %bitcast.359, bf16[768,2944]{1,0:T(8,128)(2,1)} %copy-done.115, bf16[]{:T(256)} %bitcast.72, bf16[]{:T(256)} %bitcast.71, bf16[]{:T(256)} %bitcast.70, bf16[]{:T(256)} %bitcast.69), kind=kOutput, calls=%fused_computation.2 | convolution fusion | flops 8112439296 | bytes 20580352 | tf_op jit(solution)/shard_map/dot_general | solution.py:71
  777.7 16.0 %convolution_convert_fusion = bf16[1792,2944]{1,0:T(8,128)(2,1)} fusion(bf16[768,1792]{1,0:T(8,128)(2,1)} %copy-done.64, bf16[768,2944]{1,0:T(8,128)(2,1)} %copy-done.115, bf16[]{:T(256)} %bitcast.72, bf16[]{:T(256)} %bitcast.71, bf16[]{:T(256)} %bitcast.70, bf16[]{:T(256)} %bitcast.69), kind=kOutput, calls=%fused_computation | convolution fusion | flops 8117714944 | bytes 17825800 | tf_op jit(solution)/shard_map/dot_general | solution.py:67
  795.4 5.0 multiply_reduce_fusion.4
  808.0 3.6 fusion.59.refs_0_
  811.6 3.6 fusion.60.refs_1_
  815.1 143.2 %reduce_rest.1 = (f32[112,1024]{1,0:T(8,128)}, f32[112,1024]{1,0:T(8,128)}, f32[112,1024]{1,0:T(8,128)}, f32[112,1024]{1,0:T(8,128)}, f32[112,512]{1,0:T(8,128)}...) custom-call(bf16[2,112,2048]{2,1,0:T(8,128)(2,1)} %fusion.59.refs_0_, ...), custom_call_target="tpu_custom_call" | custom-call | tf_op jit(solution)/shard_map/reduce_rest/pallas_call | solution.py:308
  959.6 2.7 reshape_reshape.3
  962.4 2.6 copy.253
  984.5 2.6 bitcast_select_fusion.3
  987.0 3.2 stack.110
  990.2 3.2 stack.111
  993.5 4.4 multiply_reduce_fusion.10
  998.9 16.9 %sum_everywhere.1 = f32[8,1792]{1,0:T(8,128)} custom-call(f32[8,1792]{1,0:T(8,128)} %maximum_maximum_fusion.in_ref), custom_call_target="tpu_custom_call" | custom-call | tf_op jit(solution)/shard_map/sum_everywhere/pallas_call | solution.py:353
  1019.6 4.9 fusion.23
  1033.2 4.5 fusion.39
  1037.7 2.8 mul.740
  1051.5 3.4 multiply_subtract_fusion
  (550 shorter events, 198.1 us)
Async XLA Ops:
  7.2 297.1 %all-gather.8.cloned.1.call-start = ((), (), s32[]{:S(2)}) async-start(), calls=%async_computation.1 | async-start | bytes 7798784 | tf_op jit(solution)/shard_map/all_gather | solution.py:811
  11.7 1.6 collective-permute-start.2
  14.2 390.2 %all-gather.6.cloned.1.call-start = ((), (), s32[]{:S(2)}) async-start(), calls=%async_computation | async-start | bytes 7798784 | tf_op jit(solution)/shard_map/all_gather | solution.py:811
  16.1 1.6 collective-permute-start.3
  17.0 2.7 collective-permute-start.1
  17.2 2.4 collective-permute-start.5
  19.7 222.1 %copy-start.74 = (bf16[1,384,1792]{2,1,0:T(8,128)(2,1)S(1)}, bf16[1,384,1792]{2,1,0:T(8,128)(2,1)}, u32[]{:S(2)}) copy-start(bf16[1,384,1792]{2,1,0:T(8,128)(2,1)} %param.27) | copy-start | bytes 4128772
  241.3 257.1 %all-gather.10.cloned.1.call-start = ((), (), s32[]{:S(2)}) async-start(), calls=%async_computation.2 | async-start | bytes 7798784 | tf_op jit(solution)/shard_map/all_gather | solution.py:811
  244.4 19.0 %collective-permute-start.6 = (bf16[384,1792]{1,0:T(8,128)(2,1)}, bf16[384,1792]{1,0:T(8,128)(2,1)}, u32[]{:S(2)}, u32[]{:S(2)}) collective-permute-start(bf16[384,1792]{1,0:T(8,128)(2,1)} %copy.214), channel_id=1, source_target_pairs={{0,2},{2,0},{1,3},{3,1},{4,6},{6,4},{5,7},{7,5},{8,10},{10,8},{9,1... | collective-permute-start | bytes 4128776 | tf_op jit(solution)/shard_map/ppermute | solution.py:677
  247.7 9.1 copy-start.56
  247.7 15.7 %collective-permute-start = (bf16[384,1792]{1,0:T(8,128)(2,1)S(1)}, bf16[384,1792]{1,0:T(8,128)(2,1)}, u32[]{:S(2)}, u32[]{:S(2)}) collective-permute-start(bf16[384,1792]{1,0:T(8,128)(2,1)S(1)} %copy.193), channel_id=1, source_target_pairs={{0,2},{2,0},{1,3},{3,1},{4,6},{6,4},{5,7},{7,5},{8,10},{10,8},{9,1... | collective-permute-start | bytes 4128776 | tf_op jit(solution)/shard_map/ppermute | solution.py:677
  251.7 116.3 %copy-start.95 = (f32[768]{0:T(1024)}, f32[768]{0:T(1024)S(1)}, u32[]{:S(2)}) copy-start(f32[768]{0:T(1024)S(1)} %get-tuple-element.150) | copy-start | bytes 9220
  263.4 8.2 copy-start.90
  274.5 13.9 %copy-start.64 = (bf16[768,1792]{1,0:T(8,128)(2,1)}, bf16[768,1792]{1,0:T(8,128)(2,1)S(1)}, u32[]{:S(2)}) copy-start(bf16[768,1792]{1,0:T(8,128)(2,1)S(1)} %multiply_convert_fusion.2) | copy-start | bytes 8257540
  302.9 51.9 %copy-start = (bf16[8,768,128]{2,1,0:T(8,128)(2,1)}, bf16[8,768,128]{2,1,0:T(8,128)(2,1)S(1)}, u32[]{:S(2)}) copy-start(bf16[8,768,128]{2,1,0:T(8,128)(2,1)S(1)} %pad_select_fusion.v_ref) | copy-start | bytes 4718596
  373.7 8.8 collective-permute-start.4
  373.7 8.8 slice-start
  404.3 12.2 %copy-start.43 = (bf16[2,384,1792]{2,1,0:T(8,128)(2,1)S(1)}, bf16[2,384,1792]{2,1,0:T(8,128)(2,1)}, u32[]{:S(2)}) copy-start(bf16[2,384,1792]{2,1,0:T(8,128)(2,1)} %pad_maximum_fusion.2) | copy-start | bytes 8257540
  422.7 62.8 %collective-permute-start.8 = (bf16[2,2,2,1,128,896]{5,4,0,3,2,1:T(8,128)(2,1)}, bf16[2,2,2,1,128,896]{5,4,0,3,2,1:T(8,128)(2,1)}, u32[]{:S(2)}, u32[]{:S(2)}) collective-permute-start(bf16[2,2,2,1,128,896]{5,4,0,3,2,1:T(8,128)(2,1)} %copy.263), channel_id=1, source_target_pairs={{0,1},{1,0},{2,3},{3,2},{4,5},{5,4},{6,7},{7,6},{8,9},{9,8},{10,11... | collective-permute-start | bytes 5505032 | tf_op jit(solution)/shard_map/ppermute | solution.py:721
  429.8 61.0 %collective-permute-start.7 = (bf16[2,2,1,2,128,896]{5,4,0,3,2,1:T(8,128)(2,1)}, bf16[2,2,1,2,128,896]{5,4,0,3,2,1:T(8,128)(2,1)}, u32[]{:S(2)}, u32[]{:S(2)}) collective-permute-start(bf16[2,2,1,2,128,896]{5,4,0,3,2,1:T(8,128)(2,1)} %copy.261), channel_id=1, source_target_pairs={{0,4},{4,0},{8,12},{12,8},{16,20},{20,16},{24,28},{28,24},{1,5},{5... | collective-permute-start | bytes 5505032 | tf_op jit(solution)/shard_map/ppermute | solution.py:721
  437.3 59.1 %copy-start.38 = (bf16[1,384,1792]{2,1,0:T(8,128)(2,1)S(1)}, bf16[1,384,1792]{2,1,0:T(8,128)(2,1)}, u32[]{:S(2)}) copy-start(bf16[1,384,1792]{2,1,0:T(8,128)(2,1)} %get-tuple-element.115) | copy-start | bytes 4128772
  489.3 55.3 %collective-permute-start.10 = (bf16[2,2,1,1,128,896]{5,4,0,3,2,1:T(8,128)(2,1)}, bf16[2,2,1,1,128,896]{5,4,0,3,2,1:T(8,128)(2,1)}, u32[]{:S(2)}, u32[]{:S(2)}) collective-permute-start(bf16[2,2,1,1,128,896]{5,4,0,3,2,1:T(8,128)(2,1)} %add_convert_fusion.9), channel_id=1, source_target_pairs={{0,4},{4,0},{8,12},{12,8},{16,20},{20,16},{24,28},{28,24},{1,5},{5... | collective-permute-start | bytes 2752520 | tf_op jit(solution)/shard_map/ppermute | solution.py:721
  494.6 52.9 %collective-permute-start.9 = (bf16[2,2,1,1,128,896]{5,4,0,3,2,1:T(8,128)(2,1)}, bf16[2,2,1,1,128,896]{5,4,0,3,2,1:T(8,128)(2,1)}, u32[]{:S(2)}, u32[]{:S(2)}) collective-permute-start(bf16[2,2,1,1,128,896]{5,4,0,3,2,1:T(8,128)(2,1)} %add_convert_fusion.10), channel_id=1, source_target_pairs={{0,1},{1,0},{2,3},{3,2},{4,5},{5,4},{6,7},{7,6},{8,9},{9,8},{10,11... | collective-permute-start | bytes 2752520 | tf_op jit(solution)/shard_map/ppermute | solution.py:721
  498.3 13.2 %copy-start.66 = (bf16[768,1792]{1,0:T(8,128)(2,1)S(1)}, bf16[768,1792]{1,0:T(8,128)(2,1)}, u32[]{:S(2)}) copy-start(bf16[768,1792]{1,0:T(8,128)(2,1)} %copy-done.65) | copy-start | bytes 8257540
  511.5 13.4 %copy-start.122 = (bf16[768,2048]{1,0:T(8,128)(2,1)}, bf16[768,2048]{1,0:T(8,128)(2,1)S(1)}, u32[]{:S(2)}) copy-start(bf16[768,2048]{1,0:T(8,128)(2,1)S(1)} %get-tuple-element.161) | copy-start | bytes 9437188
  524.6 80.9 %collective-permute-start.12 = (bf16[2,2,1,2,112,2048]{5,4,0,3,2,1:T(8,128)(2,1)}, bf16[2,2,1,2,112,2048]{5,4,0,3,2,1:T(8,128)(2,1)}, u32[]{:S(2)}, u32[]{:S(2)}) collective-permute-start(bf16[2,2,1,2,112,2048]{5,4,0,3,2,1:T(8,128)(2,1)} %copy.264), channel_id=1, source_target_pairs={{0,4},{4,0},{8,12},{12,8},{16,20},{20,16},{24,28},{28,24},{1,5},{5... | collective-permute-start | bytes 11010056 | tf_op jit(solution)/shard_map/ppermute | solution.py:721
  534.2 15.9 %slice-start.12 = ((s8[7340032]{0:T(1024)(128)(4,1)}), s8[4194304]{0:T(1024)(128)(4,1)S(1)}, s32[]{:S(2)}) async-start(s8[7340032]{0:T(1024)(128)(4,1)} %bitcast.363), calls=%async_computation.15 | async-start | bytes 8388608
  537.9 12.2 %slice-start.13 = ((s8[7340032]{0:T(1024)(128)(4,1)}), s8[3145728]{0:T(1024)(128)(4,1)S(1)}, s32[]{:S(2)}) async-start(s8[7340032]{0:T(1024)(128)(4,1)} %bitcast.363), calls=%async_computation.16 | async-start | bytes 6291456
  540.2 9.9 copy-start.124
  541.5 82.6 %collective-permute-start.13 = (bf16[2,2,2,1,112,2048]{5,4,0,3,2,1:T(8,128)(2,1)}, bf16[2,2,2,1,112,2048]{5,4,0,3,2,1:T(8,128)(2,1)}, u32[]{:S(2)}, u32[]{:S(2)}) collective-permute-start(bf16[2,2,2,1,112,2048]{5,4,0,3,2,1:T(8,128)(2,1)} %copy.265), channel_id=1, source_target_pairs={{0,1},{1,0},{2,3},{3,2},{4,5},{5,4},{6,7},{7,6},{8,9},{9,8},{10,11... | collective-permute-start | bytes 11010056 | tf_op jit(solution)/shard_map/ppermute | solution.py:721
  544.6 13.2 %slice-start.14 = ((s8[7340032]{0:T(1024)(128)(4,1)}), s8[4194304]{0:T(1024)(128)(4,1)S(1)}, s32[]{:S(2)}) async-start(s8[7340032]{0:T(1024)(128)(4,1)} %bitcast.367), calls=%async_computation.17 | async-start | bytes 8388608
  557.8 13.0 %copy-start.110 = (f32[384]{0:T(512)S(1)}, f32[384]{0:T(512)}, u32[]{:S(2)}) copy-start(f32[384]{0:T(512)} %multiply_reduce_fusion.12) | copy-start | bytes 4612
  557.8 13.6 %copy-start.81 = (bf16[128,768]{0,1:T(8,128)(2,1)S(1)}, bf16[128,768]{0,1:T(8,128)(2,1)}, u32[]{:S(2)}) copy-start(bf16[128,768]{0,1:T(8,128)(2,1)} %get-tuple-element.100) | copy-start | bytes 589828
  570.8 61.0 %collective-permute-start.11 = (bf16[768,1792]{1,0:T(8,128)(2,1)}, bf16[768,1792]{1,0:T(8,128)(2,1)}, u32[]{:S(2)}, u32[]{:S(2)}) collective-permute-start(bf16[768,1792]{1,0:T(8,128)(2,1)} %add_convert_fusion), channel_id=1, source_target_pairs={{0,2},{2,0},{1,3},{3,1},{4,6},{6,4},{5,7},{7,5},{8,10},{10,8},{9,1... | collective-permute-start | bytes 8257544 | tf_op jit(solution)/shard_map/ppermute | solution.py:677
  571.5 60.3 %slice-start.2 = ((s8[5505024]{0:T(1024)(128)(4,1)}), s8[4194304]{0:T(1024)(128)(4,1)S(1)}, s32[]{:S(2)}) async-start(s8[5505024]{0:T(1024)(128)(4,1)} %bitcast.278), calls=%async_computation.5 | async-start | bytes 8388608
  574.8 56.9 %slice-start.3 = ((s8[5505024]{0:T(1024)(128)(4,1)}), s8[1310720]{0:T(1024)(128)(4,1)S(1)}, s32[]{:S(2)}) async-start(s8[5505024]{0:T(1024)(128)(4,1)} %bitcast.278), calls=%async_computation.6 | async-start | bytes 2621440
  586.1 120.9 %collective-permute-start.17 = (bf16[2,1,1,1,128,896]{5,4,0,3,2,1:T(8,128)(2,1)S(1)}, bf16[2,1,1,1,128,896]{5,4,0,3,2,1:T(8,128)(2,1)}, u32[]{:S(2)}, u32[]{:S(2)}) collective-permute-start(bf16[2,1,1,1,128,896]{5,4,0,3,2,1:T(8,128)(2,1)S(1)} %fusion.63), channel_id=1, source_target_pairs={{0,8},{4,12},{8,0},{12,4},{16,24},{20,28},{24,16},{28,20},{1,9},{5... | collective-permute-start | bytes 1376264 | tf_op jit(solution)/shard_map/ppermute | solution.py:721
  587.6 127.8 %collective-permute-start.18 = (bf16[2,1,1,1,128,896]{5,4,0,3,2,1:T(8,128)(2,1)S(1)}, bf16[2,1,1,1,128,896]{5,4,0,3,2,1:T(8,128)(2,1)}, u32[]{:S(2)}, u32[]{:S(2)}) collective-permute-start(bf16[2,1,1,1,128,896]{5,4,0,3,2,1:T(8,128)(2,1)S(1)} %fusion.64), channel_id=1, source_target_pairs={{0,8},{4,12},{8,0},{12,4},{16,24},{20,28},{24,16},{28,20},{1,9},{5... | collective-permute-start | bytes 1376264 | tf_op jit(solution)/shard_map/ppermute | solution.py:721
  610.8 21.0 %copy-start.89 = (f32[1792]{0:T(1024)S(1)}, f32[1792]{0:T(1024)}, u32[]{:S(2)}) copy-start(f32[1792]{0:T(1024)} %get-tuple-element.70) | copy-start | bytes 21508
  610.8 140.8 %collective-permute-start.15 = (bf16[2,2,1,1,112,2048]{5,4,0,3,2,1:T(8,128)(2,1)}, bf16[2,2,1,1,112,2048]{5,4,0,3,2,1:T(8,128)(2,1)}, u32[]{:S(2)}, u32[]{:S(2)}) collective-permute-start(bf16[2,2,1,1,112,2048]{5,4,0,3,2,1:T(8,128)(2,1)} %add_convert_fusion.2), channel_id=1, source_target_pairs={{0,1},{1,0},{2,3},{3,2},{4,5},{5,4},{6,7},{7,6},{8,9},{9,8},{10,11... | collective-permute-start | bytes 5505032 | tf_op jit(solution)/shard_map/ppermute | solution.py:721
  629.4 127.3 %collective-permute-start.16 = (bf16[2,2,1,1,112,2048]{5,4,0,3,2,1:T(8,128)(2,1)}, bf16[2,2,1,1,112,2048]{5,4,0,3,2,1:T(8,128)(2,1)}, u32[]{:S(2)}, u32[]{:S(2)}) collective-permute-start(bf16[2,2,1,1,112,2048]{5,4,0,3,2,1:T(8,128)(2,1)} %add_convert_fusion.1), channel_id=1, source_target_pairs={{0,4},{4,0},{8,12},{12,8},{16,20},{20,16},{24,28},{28,24},{1,5},{5... | collective-permute-start | bytes 5505032 | tf_op jit(solution)/shard_map/ppermute | solution.py:721
  631.8 8.9 slice-start.10
  658.8 50.7 %slice-start.6 = ((s8[5505024]{0:T(1024)(128)(4,1)}), s8[4194304]{0:T(1024)(128)(4,1)S(1)}, s32[]{:S(2)}) async-start(s8[5505024]{0:T(1024)(128)(4,1)} %bitcast.284), calls=%async_computation.9 | async-start | bytes 8388608
  662.9 46.7 %slice-start.7 = ((s8[5505024]{0:T(1024)(128)(4,1)}), s8[1310720]{0:T(1024)(128)(4,1)S(1)}, s32[]{:S(2)}) async-start(s8[5505024]{0:T(1024)(128)(4,1)} %bitcast.284), calls=%async_computation.10 | async-start | bytes 2621440
  705.7 9.6 copy-start.2
  705.7 9.6 copy-start.8
  705.7 9.6 copy-start.10
  709.0 32.8 %collective-permute-start.24 = (bf16[1,1,1,1,128,896]{5,4,0,3,2,1:T(8,128)(2,1)S(1)}, bf16[1,1,1,1,128,896]{5,4,0,3,2,1:T(8,128)(2,1)S(1)}, u32[]{:S(2)}, u32[]{:S(2)}) collective-permute-start(bf16[1,1,1,1,128,896]{5,4,0,3,2,1:T(8,128)(2,1)S(1)} %fusion.66), channel_id=1, source_target_pairs={{0,16},{4,20},{8,24},{12,28},{16,0},{20,4},{24,8},{28,12},{1,17},{... | collective-permute-start | bytes 688136 | tf_op jit(solution)/shard_map/ppermute | solution.py:721
  715.3 9.1 copy-start.3
  717.4 26.3 %collective-permute-start.25 = (bf16[1,1,1,1,128,896]{5,4,0,3,2,1:T(8,128)(2,1)S(1)}, bf16[1,1,1,1,128,896]{5,4,0,3,2,1:T(8,128)(2,1)S(1)}, u32[]{:S(2)}, u32[]{:S(2)}) collective-permute-start(bf16[1,1,1,1,128,896]{5,4,0,3,2,1:T(8,128)(2,1)S(1)} %fusion.67), channel_id=1, source_target_pairs={{0,16},{4,20},{8,24},{12,28},{16,0},{20,4},{24,8},{28,12},{1,17},{... | collective-permute-start | bytes 688136 | tf_op jit(solution)/shard_map/ppermute | solution.py:721
  723.1 23.8 %collective-permute-start.22 = (bf16[4,112,1792]{2,1,0:T(8,128)(2,1)}, bf16[4,112,1792]{2,1,0:T(8,128)(2,1)}, u32[]{:S(2)}, u32[]{:S(2)}) collective-permute-start(bf16[4,112,1792]{2,1,0:T(8,128)(2,1)} %dynamic-slice_bitcast_fusion), channel_id=1, source_target_pairs={{0,2},{2,0},{1,3},{3,1},{4,6},{6,4},{5,7},{7,5},{8,10},{10,8},{9,1... | collective-permute-start | bytes 4816904 | tf_op jit(solution)/shard_map/ppermute | solution.py:677
  730.3 8.5 slice-start.8
  741.8 53.6 %collective-permute-start.14 = (f32[384,1792]{1,0:T(8,128)}, f32[384,1792]{1,0:T(8,128)}, u32[]{:S(2)}, u32[]{:S(2)}) collective-permute-start(f32[384,1792]{1,0:T(8,128)} %dynamic-slice_add_fusion.1), channel_id=1, source_target_pairs={{0,2},{2,0},{1,3},{3,1},{4,6},{6,4},{5,7},{7,5},{8,10},{10,8},{9,1... | collective-permute-start | bytes 8257544 | tf_op jit(solution)/shard_map/ppermute | solution.py:677
  751.5 43.9 %slice-start.4 = ((s8[5505024]{0:T(1024)(128)(4,1)}), s8[4194304]{0:T(1024)(128)(4,1)S(1)}, s32[]{:S(2)}) async-start(s8[5505024]{0:T(1024)(128)(4,1)} %bitcast.280), calls=%async_computation.7 | async-start | bytes 8388608
  756.0 51.9 %collective-permute-start.20 = (bf16[2,1,1,1,112,2048]{5,4,0,3,2,1:T(8,128)(2,1)}, bf16[2,1,1,1,112,2048]{5,4,0,3,2,1:T(8,128)(2,1)}, u32[]{:S(2)}, u32[]{:S(2)}) collective-permute-start(bf16[2,1,1,1,112,2048]{5,4,0,3,2,1:T(8,128)(2,1)} %fusion.57), channel_id=1, source_target_pairs={{0,8},{4,12},{8,0},{12,4},{16,24},{20,28},{24,16},{28,20},{1,9},{5... | collective-permute-start | bytes 2752520 | tf_op jit(solution)/shard_map/ppermute | solution.py:721
  761.0 50.6 %collective-permute-start.21 = (bf16[2,1,1,1,112,2048]{5,4,0,3,2,1:T(8,128)(2,1)}, bf16[2,1,1,1,112,2048]{5,4,0,3,2,1:T(8,128)(2,1)}, u32[]{:S(2)}, u32[]{:S(2)}) collective-permute-start(bf16[2,1,1,1,112,2048]{5,4,0,3,2,1:T(8,128)(2,1)} %fusion.58), channel_id=1, source_target_pairs={{0,8},{4,12},{8,0},{12,4},{16,24},{20,28},{24,16},{28,20},{1,9},{5... | collective-permute-start | bytes 2752520 | tf_op jit(solution)/shard_map/ppermute | solution.py:721
  763.7 31.7 %slice-start.5 = ((s8[5505024]{0:T(1024)(128)(4,1)}), s8[1310720]{0:T(1024)(128)(4,1)S(1)}, s32[]{:S(2)}) async-start(s8[5505024]{0:T(1024)(128)(4,1)} %bitcast.280), calls=%async_computation.8 | async-start | bytes 2621440
  777.7 16.0 %copy-start.36 = (f32[768,1792]{1,0:T(8,128)}, f32[768,1792]{1,0:T(8,128)S(1)}, u32[]{:S(2)}) copy-start(f32[768,1792]{1,0:T(8,128)S(1)} %fusion) | copy-start | bytes 16515076
  795.4 198.0 %collective-permute-start.19 = (f32[384,1792]{1,0:T(8,128)}, f32[384,1792]{1,0:T(8,128)S(1)}, u32[]{:S(2)}, u32[]{:S(2)}) collective-permute-start(f32[384,1792]{1,0:T(8,128)} %constant_dynamic-slice_fusion), channel_id=1, source_target_pairs={{0,2},{2,0},{1,3},{3,1},{4,6},{6,4},{5,7},{7,5},{8,10},{10,8},{9,1... | collective-permute-start | bytes 8257544 | tf_op jit(solution)/shard_map/ppermute | solution.py:677
  962.3 9.2 copy-start.86
  962.4 9.2 copy-start.87
  972.6 9.2 collective-permute-start.23
  973.9 10.5 collective-permute-start.26
  993.4 26.2 %copy-start.111 = (f32[384]{0:T(512)S(1)}, f32[384]{0:T(512)}, u32[]{:S(2)}) copy-start(f32[384]{0:T(512)} %multiply_reduce_fusion.12) | copy-start | bytes 4612
  (107 other events, 379.9 us)
Sparse Core Ops, SparseCore 0:
  14.3 151.0 all-gather.7
  241.4 115.5 all-gather.5
  360.4 119.3 all-gather.9
